TPU v7x, 32 devices: a whole 2x2x4 slice. The times are simulated.
32 devices in a mesh: groups: 2 (over x), section: 16 (over z, y, core).
Axes of the slice: x: 2, y: 2, z: 4, core: 2. Of those that a mesh axis runs over, the one named last changes fastest.
Arguments:
- arriving: bfloat16 [4096, 4096], P(('groups', 'section')), parts along dimension 0, may hold values from -6 to 6
- memory: bfloat16 [2048, 4096], P(('groups', 'section')), parts along dimension 0, may hold values from -6 to 6
- w_query: bfloat16 [4096, 4096], P(None, 'section'), may hold values from -8 to 8, as said below
- w_key: bfloat16 [4096, 4096], P(None, 'section'), may hold values from -0.09375 to 0.09375
- w_value: bfloat16 [4096, 4096], P(None, 'section'), may hold values from -0.09375 to 0.09375
- w_out: bfloat16 [4096, 4096], P('section'), may hold values from -0.125 to 0.125
- tok_len: int32 [64], P('groups'), parts along dimension 0, may hold values from 16 to 64, as said below
- mem_len: int32 [32], P('groups'), parts along dimension 0, may hold values from 16 to 64, as said below
Outputs:
- mixed: bfloat16 [4096, 4096], P(('groups', 'section')), parts along dimension 0
There are 2 independent parts, one for each index of `groups`. A program takes and returns all parts, laid end to end along the dimension named above; an argument that names none is the same for every part. Nothing has to cross between parts.
Inputs may be any that keep to these rules, and one draw needn't show every extreme that they name: Rows of section s's microbatch b at positions tok_len[s * 16 + b] or later are padding. Frames of utterance u at positions mem_len[u] or later are padding. `w_query`: query projection weights, every entry within the stated range.
All inputs are finite; a program needn't handle non-finite values.
Results may differ from a plain program's by a relative error of at most 0.0028.
The roundings to bfloat16 on the way count: a program that leaves them out, or rounds other values in their place, can miss the bound.
Values may be sent and summed in bfloat16 or wider, within the bound.
No kernel may reach another device: no remote copies, remote signals or barrier semaphores. Data moves between devices by JAX's collectives and lax.ppermute only.
A program may use at most 128 MiB of HBM per device.

v0:
```python
import math

import jax
import jax.numpy as jnp
from jax import lax
from jax.sharding import PartitionSpec as P

HD = 128
FR = 64
GROUP = 8
MB = 16
MEMF = 64


norm_eps = 1e-06


def swapped(value, axis, bit):
    mask = 2**bit
    pairs = [(source, source ^ mask) for source in range(lax.axis_size(axis))]
    return lax.ppermute(value, axis, pairs)


def from_behind(x, axis, by):
    peers = lax.axis_size(axis)
    return lax.ppermute(x, axis, [(i, (i + by) % peers) for i in range(peers)])


def gather_group(row_block, dev_index):
    for bit_no in range(GROUP.bit_length() - 1):
        partner = swapped(row_block, "section", bit_no)
        is_lower = dev_index >> bit_no & 1 == 0
        row_block = jnp.where(
            is_lower,
            jnp.concatenate([row_block, partner], 0),
            jnp.concatenate([partner, row_block], 0),
        )
    return row_block


def shards(arriving, memory, w_query, w_key, w_value, w_out, tok_len, mem_len):
    dev_index = lax.axis_index("section")
    section_no = dev_index // GROUP
    tp_slot = dev_index % GROUP
    own_rows = arriving.shape[0]
    head_cols = w_query.shape[1]
    heads_here = head_cols // HD
    bit_count = GROUP.bit_length() - 1
    att_scale = 1.0 / math.sqrt(HD)
    w_pair = jnp.concatenate([w_key, w_value], 1)
    kv_pairs = jnp.dot(
        lax.all_gather(memory, "section", axis=0, tiled=True),
        w_pair,
        preferred_element_type=jnp.float32,
    ).astype(jnp.bfloat16)
    incoming = from_behind(arriving, "section", GROUP)
    all_rows = gather_group(incoming, dev_index)
    widened = all_rows.astype(jnp.float32)
    normed = (
        widened * lax.rsqrt(jnp.mean(widened * widened, -1, keepdims=True) + norm_eps)
    ).astype(jnp.bfloat16)
    queries = jnp.dot(normed, w_query, preferred_element_type=jnp.float32).astype(jnp.bfloat16)
    queries = queries.reshape(MB, FR, heads_here, HD)
    utt_order = (section_no + jnp.arange(MB, dtype=jnp.int32)) % MB
    kv_pairs = jnp.take(kv_pairs.reshape(MB, MEMF, 2 * head_cols), utt_order, axis=0)
    key_rows = kv_pairs[:, :, :head_cols].reshape(MB, MEMF, heads_here, HD)
    val_rows = kv_pairs[:, :, head_cols:].reshape(MB, MEMF, heads_here, HD)
    scores = (
        jnp.einsum("bqhd,bkhd->bhqk", queries, key_rows, preferred_element_type=jnp.float32)
        * att_scale
    )
    lengths = jnp.take(mem_len, utt_order)
    valid = jnp.arange(MEMF, dtype=jnp.int32)[None, :] < lengths[:, None]
    scores = jnp.where(valid[:, None, None, :], scores, -jnp.inf)
    row_max = jnp.max(scores, -1, keepdims=True)
    expo = jnp.exp(scores - row_max)
    att_probs = (expo / jnp.sum(expo, -1, keepdims=True)).astype(jnp.bfloat16)
    attended = jnp.einsum(
        "bhqk,bkhd->bqhd", att_probs, val_rows, preferred_element_type=jnp.float32
    ).astype(jnp.bfloat16)
    partial_value = jnp.dot(
        attended.reshape(MB * FR, head_cols), w_out, preferred_element_type=jnp.float32
    )
    for bit_no in reversed(range(bit_count)):
        half_rows = partial_value.shape[0] // 2
        is_upper = dev_index >> bit_no & 1 == 1
        lower_half = partial_value[:half_rows]
        upper_half = partial_value[half_rows:]
        send_half = jnp.where(is_upper, lower_half, upper_half)
        keep_half = jnp.where(is_upper, upper_half, lower_half)
        partial_value = keep_half + swapped(send_half, "section", bit_no)
    position = tp_slot * own_rows + jnp.arange(own_rows, dtype=jnp.int32)
    micro_idx = position // FR
    tok_limit = jnp.take(tok_len, section_no * MB + micro_idx)
    is_live = position % FR < tok_limit
    result = incoming.astype(jnp.float32) + jnp.where(is_live[:, None], partial_value, 0.0)
    return result.astype(jnp.bfloat16)


def solution(mesh):
    return jax.shard_map(
        shards,
        mesh=mesh,
        in_specs=(
            P(("groups", "section"), None),
            P(("groups", "section"), None),
            P(None, "section"),
            P(None, "section"),
            P(None, "section"),
            P("section", None),
            P("groups"),
            P("groups"),
        ),
        out_specs=P(("groups", "section"), None),
        check_vma=False,
    )
```

profile of v0, /device:TPU:0, one launch (start us, length us, event | category | flops | bytes accessed | tf_op | source)
XLA Modules:
  0.0 615.9 jit_solution(9641673262163692552)
XLA Ops:
  7.3 4.1 collective-permute-start
  11.4 76.1 %collective-permute-done = bf16[128,4096]{1,0:T(8,128)(2,1)S(1)} collective-permute-done((bf16[128,4096]{1,0:T(8,128)(2,1)}, bf16[128,4096]{1,0:T(8,128)(2,1)S(1)}, u32[]{:S(2)}, u32[]{:S(2)}) %collective-permute-start) | collective-permute-done | bytes 1048608 | tf_op jit(solution)/shard_map/ppermute | solution.py:26
  87.4 2.8 collective-permute-done.1
  90.2 3.7 maximum_select_fusion.2
  93.9 2.0 collective-permute-start.2
  95.9 46.2 %collective-permute-done.2 = bf16[256,4096]{1,0:T(8,128)(2,1)} collective-permute-done((bf16[256,4096]{1,0:T(8,128)(2,1)}, bf16[256,4096]{1,0:T(8,128)(2,1)}, u32[]{:S(2)}, u32[]{:S(2)}) %collective-permute-start.2) | collective-permute-done | bytes 2097184 | tf_op jit(solution)/shard_map/ppermute | solution.py:21
  142.2 6.0 maximum_select_fusion.1
  148.2 4.7 collective-permute-start.3
  153.7 89.5 %collective-permute-done.3 = bf16[512,4096]{1,0:T(8,128)(2,1)} collective-permute-done((bf16[512,4096]{1,0:T(8,128)(2,1)}, bf16[512,4096]{1,0:T(8,128)(2,1)}, u32[]{:S(2)}, u32[]{:S(2)}) %collective-permute-start.3) | collective-permute-done | bytes 4194336 | tf_op jit(solution)/shard_map/ppermute | solution.py:21
  243.2 7.6 %fusion.1 = f32[1024]{0:T(1024)S(1)} fusion(bf16[512,4096]{1,0:T(8,128)(2,1)} %maximum_select_fusion.1, bf16[512,4096]{1,0:T(8,128)(2,1)} %collective-permute-done.3, pred[]{:T(512)S(6)} %eq.27), kind=kLoop, calls=%fused_computation.6 | loop fusion | flops 50330624 | bytes 8392705 | tf_op jit(solution)/shard_map/reduce_sum | solution.py:60
  250.9 8.6 %fusion.19 = bf16[1024,256]{1,0:T(8,128)(2,1)} fusion(bf16[4096,256]{1,0:T(8,128)(2,1)S(1)} %copy-done.7, f32[1024]{0:T(1024)S(1)} %add_rsqrt_fusion, bf16[512,4096]{1,0:T(8,128)(2,1)} %maximum_select_fusion.1, bf16[512,4096]{1,0:T(8,128)(2,1)} %collective-permute-done.3, pred[]{:T(512)S(6)} %eq.27), kind=kOutput, calls=%fused_computation.29 | convolution fusion | flops 2198077440 | bytes 11014145 | tf_op jit(solution)/shard_map/dot_general | solution.py:62
  259.5 2.0 reshape.195
  261.5 10.2 %fusion.15 = bf16[1024,512]{0,1:T(8,128)(2,1)} fusion(bf16[1024,4096]{1,0:T(8,128)(2,1)} %all-gather.2.cloned.1.call-done, bf16[4096,256]{1,0:T(8,128)(2,1)} %param.12, bf16[4096,256]{1,0:T(8,128)(2,1)} %param.11), kind=kOutput, calls=%fused_computation.26 | convolution fusion | flops 4303880192 | bytes 13631488 | tf_op jit(solution)/shard_map/dot_general | solution.py:51
  271.6 2.3 copy.11
  273.9 2.8 gather_fusion.1
  276.7 1.4 broadcast_select_fusion
  281.3 2.9 fusion.22
  284.2 1.6 copy.16
  285.8 8.1 %fusion.23 = f32[1024,4096]{1,0:T(8,128)} fusion(bf16[256,4096]{1,0:T(8,128)(2,1)S(1)} %copy-done, bf16[128,8,2,128]{3,2,1,0:T(2,128)(2,1)S(1)} %bitcast.30), kind=kOutput, calls=%fused_computation.34 | convolution fusion | flops 2147483648 | bytes 19398656 | tf_op jit(solution)/shard_map/dot_general | solution.py:81
  293.9 11.1 %slice_select_fusion = f32[512,4096]{1,0:T(8,128)} fusion(f32[1024,4096]{1,0:T(8,128)} %fusion.23, pred[]{:T(512)S(6)} %eq.26), kind=kLoop, calls=%fused_computation.12 | loop fusion | flops 2097152 | bytes 25165824 | tf_op jit(solution)/shard_map/jit(_where)/select_n | solution.py:89
  305.1 1.7 collective-permute-start.4
  306.8 179.6 %collective-permute-done.4 = f32[512,4096]{1,0:T(8,128)} collective-permute-done((f32[512,4096]{1,0:T(8,128)}, f32[512,4096]{1,0:T(8,128)}, u32[]{:S(2)}, u32[]{:S(2)}) %collective-permute-start.4) | collective-permute-done | bytes 8388640 | tf_op jit(solution)/shard_map/ppermute | solution.py:21
  486.4 9.3 %select_add_fusion = f32[512,4096]{1,0:T(8,128)S(1)} fusion(f32[512,4096]{1,0:T(8,128)} %collective-permute-done.4, f32[1024,4096]{1,0:T(8,128)} %fusion.23, pred[]{:T(512)S(6)} %eq.26), kind=kLoop, calls=%fused_computation.10 | loop fusion | flops 4194304 | bytes 33554432 | tf_op jit(solution)/shard_map/add | solution.py:91
  495.7 2.8 slice_select_fusion.1
  498.5 1.7 copy-done.4
  500.2 1.6 collective-permute-start.5
  501.8 88.9 %collective-permute-done.5 = f32[256,4096]{1,0:T(8,128)} collective-permute-done((f32[256,4096]{1,0:T(8,128)}, f32[256,4096]{1,0:T(8,128)}, u32[]{:S(2)}, u32[]{:S(2)}) %collective-permute-start.5) | collective-permute-done | bytes 4194336 | tf_op jit(solution)/shard_map/ppermute | solution.py:21
  590.8 5.7 select_add_fusion.1
  596.5 1.9 copy-done.5
  598.4 1.6 slice_select_fusion.2
  601.3 3.2 collective-permute-done.6
  604.5 4.6 add_convert_fusion
  (35 shorter events, 5.9 us)
Async XLA Ops:
  6.5 279.3 %copy-start = (bf16[256,4096]{1,0:T(8,128)(2,1)S(1)}, bf16[256,4096]{1,0:T(8,128)(2,1)}, u32[]{:S(2)}) copy-start(bf16[256,4096]{1,0:T(8,128)(2,1)} %param.13) | copy-start | bytes 6291460
  6.5 254.9 %all-gather.2.cloned.1.call-start = ((), (), s32[]{:S(2)}) async-start(), calls=%async_computation | async-start | bytes 8912896 | tf_op jit(solution)/shard_map/all_gather | solution.py:52
  7.3 80.2 %collective-permute-start = (bf16[128,4096]{1,0:T(8,128)(2,1)}, bf16[128,4096]{1,0:T(8,128)(2,1)S(1)}, u32[]{:S(2)}, u32[]{:S(2)}) collective-permute-start(bf16[128,4096]{1,0:T(8,128)(2,1)} %param.8), channel_id=1, source_target_pairs={{0,8},{1,9},{2,10},{3,11},{4,12},{5,13},{6,14},{7,15},{8,0},{9,1},... | collective-permute-start | bytes 3145736 | tf_op jit(solution)/shard_map/ppermute | solution.py:26
  87.4 2.8 collective-permute-start.1
  93.9 48.3 %collective-permute-start.2 = (bf16[256,4096]{1,0:T(8,128)(2,1)}, bf16[256,4096]{1,0:T(8,128)(2,1)}, u32[]{:S(2)}, u32[]{:S(2)}) collective-permute-start(bf16[256,4096]{1,0:T(8,128)(2,1)} %maximum_select_fusion.2), channel_id=1, source_target_pairs={{0,2},{1,3},{2,0},{3,1},{4,6},{5,7},{6,4},{7,5},{8,10},{9,11},{10,... | collective-permute-start | bytes 6291464 | tf_op jit(solution)/shard_map/ppermute | solution.py:21
  95.9 57.0 %copy-start.2 = (s32[16]{0:T(128)S(1)}, s32[16]{0:T(128)}, u32[]{:S(2)}) copy-start(s32[16]{0:T(128)} %param.15) | copy-start | bytes 196
  148.2 95.1 %collective-permute-start.3 = (bf16[512,4096]{1,0:T(8,128)(2,1)}, bf16[512,4096]{1,0:T(8,128)(2,1)}, u32[]{:S(2)}, u32[]{:S(2)}) collective-permute-start(bf16[512,4096]{1,0:T(8,128)(2,1)} %maximum_select_fusion.1), channel_id=1, source_target_pairs={{0,4},{1,5},{2,6},{3,7},{4,0},{5,1},{6,2},{7,3},{8,12},{9,13},{10,... | collective-permute-start | bytes 12582920 | tf_op jit(solution)/shard_map/ppermute | solution.py:21
  153.7 97.1 %copy-start.7 = (bf16[4096,256]{1,0:T(8,128)(2,1)S(1)}, bf16[4096,256]{1,0:T(8,128)(2,1)}, u32[]{:S(2)}) copy-start(bf16[4096,256]{1,0:T(8,128)(2,1)} %param.10) | copy-start | bytes 6291460
  276.7 2.5 copy-start.6
  280.0 1.0 copy-start.8
  305.1 181.3 %collective-permute-start.4 = (f32[512,4096]{1,0:T(8,128)}, f32[512,4096]{1,0:T(8,128)}, u32[]{:S(2)}, u32[]{:S(2)}) collective-permute-start(f32[512,4096]{1,0:T(8,128)} %slice_select_fusion), channel_id=1, source_target_pairs={{0,4},{1,5},{2,6},{3,7},{4,0},{5,1},{6,2},{7,3},{8,12},{9,13},{10,... | collective-permute-start | bytes 25165832 | tf_op jit(solution)/shard_map/ppermute | solution.py:21
  495.7 4.5 copy-start.4
  500.2 90.5 %collective-permute-start.5 = (f32[256,4096]{1,0:T(8,128)}, f32[256,4096]{1,0:T(8,128)}, u32[]{:S(2)}, u32[]{:S(2)}) collective-permute-start(f32[256,4096]{1,0:T(8,128)} %slice_select_fusion.1), channel_id=1, source_target_pairs={{0,2},{1,3},{2,0},{3,1},{4,6},{5,7},{6,4},{7,5},{8,10},{9,11},{10,... | collective-permute-start | bytes 12582920 | tf_op jit(solution)/shard_map/ppermute | solution.py:21
  596.4 1.9 copy-start.5
  598.4 1.6 copy-start.3
  600.0 4.5 collective-permute-start.6
  601.2 7.8 %copy-start.1 = (bf16[256,4096]{1,0:T(8,128)(2,1)S(1)}, bf16[256,4096]{1,0:T(8,128)(2,1)}, u32[]{:S(2)}) copy-start(bf16[256,4096]{1,0:T(8,128)(2,1)} %param.13) | copy-start | bytes 6291460
Sparse Core Ops, SparseCore 0:
  9.5 100.5 all-gather.1
where the time goes:
time: 616 us
  waiting for transfers between devices  487 us (79%)
  other arithmetic  54.2 us (9%)
  matrix products  30.6 us (5%)
  local copies, waits for them, and re-layouts  16.3 us (3%)
  starting transfers between devices  14.2 us (2%)
  between operations  13.5 us (2%)
    ppermute x6, waiting for transfers between devices, swapped(): return lax.ppermute(value, axis, pairs)  410 us
    ppermute x1, waiting for transfers between devices, from_behind(): return lax.ppermute(x, axis, [(i, (i + by) % peers) for i in range(peers)])  76.1 us
    select_n x3, other arithmetic, shards(): send_half = jnp.where(is_upper, lower_half, upper_half)  15.5 us
    add x2, other arithmetic, shards(): partial_value = keep_half + swapped(send_half, 'section', bit_no)  14.9 us
  transfers between devices with their start and end apart: 8, of which 7 were waited for; matrix products, arithmetic and copies ran while one was open for 5% of the time, Pallas kernels for 0%

commit v1 on v0

v1 whole, which is shorter than its diff:
```python
import functools
import math

import jax
import jax.numpy as jnp
from jax import lax
from jax.experimental import pallas as pl
from jax.experimental.pallas import tpu as pltpu
from jax.sharding import PartitionSpec as P

HD = 128
FR = 64
GROUP = 8
MB = 16
MEMF = 64
NORM_EPS = 1e-06
BF16 = jnp.bfloat16
F32 = jnp.float32
VMEM_BYTES = 48 * 2**20

CORE, NEAR, FAR = 1, 2, 4
CHIPS = (0, NEAR, FAR, NEAR | FAR)


def flip(value, bits):
    size = lax.axis_size("section")
    return lax.ppermute(value, "section", [(i, i ^ bits) for i in range(size)])


def hop(value):
    size = lax.axis_size("section")
    return lax.ppermute(value, "section", [(i, (i + GROUP) % size) for i in range(size)])


def across(value):
    return lax.ppermute(value, "groups", [(0, 1), (1, 0)])


def whole(count):
    return [pl.BlockSpec(memory_space=pltpu.VMEM)] * count


def dot(a, b):
    return jnp.dot(a, b, preferred_element_type=F32)


def keys_values_kernel(*refs):
    *mem_refs, key_own, key_oth, val_own, val_oth, out, rows = refs
    for k, ref in enumerate(mem_refs):
        rows[k * MEMF:(k + 1) * MEMF, :] = ref[...]
    width = key_own.shape[1]
    for k, weight in enumerate((key_own, key_oth, val_own, val_oth)):
        out[:, k * width:(k + 1) * width] = dot(rows[...], weight[...]).astype(BF16)


def keys_values(pieces, weights):
    depth, width = weights[0].shape
    rows = len(pieces) * MEMF
    return pl.pallas_call(
        keys_values_kernel,
        out_shape=jax.ShapeDtypeStruct((rows, 4 * width), BF16),
        in_specs=whole(len(pieces) + 4),
        out_specs=pl.BlockSpec(memory_space=pltpu.VMEM),
        scratch_shapes=[pltpu.VMEM((rows, depth), BF16)],
        compiler_params=pltpu.CompilerParams(vmem_limit_bytes=VMEM_BYTES),
        cost_estimate=pl.CostEstimate(
            flops=8 * rows * depth * width,
            bytes_accessed=2 * (rows * depth + 4 * depth * width + 4 * rows * width),
            transcendentals=0,
        ),
    )(*pieces, *weights)


def attend_kernel(table, x0, x1, x2, x3, query_own, query_oth, kv_own, kv_oth, out, normed):
    width = query_own.shape[1]
    heads = 2 * width // HD
    for k, ref in enumerate((x0, x1, x2, x3)):
        wide = ref[...].astype(F32)
        scale = lax.rsqrt(jnp.mean(wide * wide, -1, keepdims=True) + NORM_EPS)
        normed[k * FR:(k + 1) * FR, :] = (wide * scale).astype(BF16)
    queries = jnp.concatenate(
        [dot(normed[...], query_own[...]), dot(normed[...], query_oth[...])], 1
    ).astype(BF16)
    is_own = table[0] == 1
    column = lax.broadcasted_iota(jnp.int32, (FR, MEMF), 1)
    scores, values = [], []
    for k in range(4):
        place = table[1 + k]
        length = table[5 + k]
        start = pl.multiple_of(place * MEMF, MEMF)
        mine = kv_own[pl.ds(start, MEMF), :]
        other = kv_oth[pl.ds(start, MEMF), :]
        other = jnp.concatenate(
            [other[:, n * width:(n + 1) * width] for n in (1, 0, 3, 2)], 1
        )
        kv = jnp.where(is_own, mine, other)
        values.append(kv[:, 2 * width:])
        for h in range(heads):
            found = lax.dot_general(
                queries[k * FR:(k + 1) * FR, h * HD:(h + 1) * HD],
                kv[:, h * HD:(h + 1) * HD],
                (((1,), (1,)), ((), ())),
                preferred_element_type=F32,
            )
            found = found * (1.0 / math.sqrt(HD))
            scores.append(jnp.where(column < length, found, -jnp.inf))
    score = jnp.concatenate(scores, 0)
    expo = jnp.exp(score - jnp.max(score, -1, keepdims=True))
    probs = (expo / jnp.sum(expo, -1, keepdims=True)).astype(BF16)
    for k in range(4):
        for h in range(heads):
            at = (k * heads + h) * FR
            out[k, :, h * HD:(h + 1) * HD] = dot(
                probs[at:at + FR], values[k][:, h * HD:(h + 1) * HD]
            ).astype(BF16)


def attend(table, pieces, weights, kv_own, kv_oth):
    depth, width = weights[0].shape
    return pl.pallas_call(
        attend_kernel,
        out_shape=jax.ShapeDtypeStruct((4, FR, 2 * width), BF16),
        in_specs=[pl.BlockSpec(memory_space=pltpu.SMEM)] + whole(8),
        out_specs=pl.BlockSpec(memory_space=pltpu.VMEM),
        scratch_shapes=[pltpu.VMEM((4 * FR, depth), BF16)],
        compiler_params=pltpu.CompilerParams(vmem_limit_bytes=VMEM_BYTES),
        cost_estimate=pl.CostEstimate(
            flops=16 * FR * depth * width,
            bytes_accessed=2 * (4 * FR * depth + 2 * depth * width) + 4 * kv_own.size,
            transcendentals=4 * FR * MEMF * 4,
        ),
    )(table, *pieces, *weights, kv_own, kv_oth)


def project_kernel(table, *refs):
    att = refs[:8]
    own, oth, direct, crossed = refs[8], refs[9], refs[10:16], refs[16:22]
    x_ref, out = refs[22:]
    step = pl.program_id(0)
    half_steps = pl.num_programs(0) // 2
    width = own.shape[0]

    def finish(others):
        total = None
        for k in range(4):
            pair = (own, oth) if k == 0 else (others[k - 1], others[k + 2])
            for n, weight in enumerate(pair):
                rows = jnp.concatenate(
                    [att[j * 4 + k][:, n * width:(n + 1) * width] for j in range(2)], 0
                )
                term = dot(rows, weight[...])
                total = term if total is None else total + term
        row = lax.broadcasted_iota(jnp.int32, total.shape, 0)
        limit = jnp.where(row < FR, table[1], table[2] + FR)
        branch = jnp.where(row < limit, total, 0.0)
        out[...] = (x_ref[...].astype(F32) + branch).astype(BF16)

    pl.when(step < half_steps)(lambda: finish(direct))
    pl.when(step >= half_steps)(lambda: finish(crossed))


def project(table, att, own, oth, direct, crossed, x):
    width, depth = own.shape
    rows = x.shape[0]
    tile = 512
    half = depth // 2 // tile

    def placed(i, table):
        group = table[0]
        return 0, jnp.where(i < half, group * half + i, (1 - group) * half + i - half)

    att_specs = [pl.BlockSpec((FR, 2 * width), lambda i, table: (0, 0))] * 8
    full = pl.BlockSpec((width, tile), placed)
    first = pl.BlockSpec((width, tile), lambda i, table: (0, jnp.minimum(i, half - 1)))
    second = pl.BlockSpec((width, tile), lambda i, table: (0, jnp.maximum(i - half, 0)))
    row_block = pl.BlockSpec((rows, tile), placed)
    return pl.pallas_call(
        project_kernel,
        out_shape=jax.ShapeDtypeStruct(x.shape, BF16),
        grid_spec=pltpu.PrefetchScalarGridSpec(
            num_scalar_prefetch=1,
            grid=(2 * half,),
            in_specs=att_specs + [full, full] + [first] * 6 + [second] * 6 + [row_block],
            out_specs=row_block,
        ),
        compiler_params=pltpu.CompilerParams(
            vmem_limit_bytes=VMEM_BYTES, dimension_semantics=("arbitrary",)
        ),
        cost_estimate=pl.CostEstimate(
            flops=16 * rows * width * depth,
            bytes_accessed=2 * (8 * width * depth + 2 * rows * depth),
            transcendentals=0,
        ),
    )(table, *att, own, oth, *direct, *crossed, x)


def shards(arriving, memory, w_query, w_key, w_value, w_out, tok_len, mem_len):
    me = lax.axis_index("section")
    size = lax.axis_size("section")
    section = me // GROUP
    slot = me % GROUP
    core = me & 1
    group = lax.axis_index("groups")
    depth = arriving.shape[1]

    ring = size == MB and memory.shape[0] == MEMF
    if ring:
        pieces = [memory]
        mem_far = flip(memory, FAR)
        mem_near = flip(memory, NEAR)
        mem_hop = hop(memory)
    x_first, x_last = arriving[:FR], arriving[FR:]

    query_pair = [w_query, flip(w_query, CORE)]
    kv_weights = [w_key, flip(w_key, CORE), w_value, flip(w_value, CORE)]
    out_core = flip(w_out, CORE)

    hop_x = [hop(x_first), hop(x_last)]
    if ring:
        mem_first = [memory, mem_near, mem_far, flip(mem_far, NEAR)]
        hop_far = flip(mem_hop, FAR)
        mem_second = [mem_hop, flip(mem_hop, NEAR), hop_far, flip(hop_far, NEAR)]
        place = lambda utt: (utt ^ me) >> 1
    else:
        gathered = lax.all_gather(memory, "section", axis=0, tiled=True)
        gathered = gathered.reshape(MB // 2, 2, MEMF, depth)
        gathered = lax.dynamic_index_in_dim(gathered, core, 1, keepdims=False)
        mem_first = [gathered[k] for k in range(4)]
        mem_second = [gathered[k] for k in range(4, 8)]
        place = lambda utt: utt >> 1
    kv_halves = [keys_values(part, kv_weights) for part in (mem_first, mem_second)]
    kv_own = jnp.concatenate(kv_halves, 0)
    kv_oth = jnp.concatenate([flip(part, CORE) for part in kv_halves], 0)

    half_cols = depth // 2
    half = lax.dynamic_slice_in_dim(w_out, group * half_cols, half_cols, 1)
    out_near = flip(half, NEAR)
    out_far = flip(half, FAR)
    out_diag = flip(out_near, FAR)
    direct = [out_near, out_far, out_diag]
    crossed = [across(part) for part in direct]
    direct = direct + [flip(part, CORE) for part in direct]
    crossed = crossed + [flip(part, CORE) for part in crossed]

    att = []
    for j in range(2):
        own = hop_x[j]
        far = flip(own, FAR)
        rows = [own, flip(own, NEAR), far, flip(far, NEAR)]
        micro = [2 * (slot ^ chip) + j for chip in CHIPS]
        utts = [(section + b) % MB for b in micro]
        is_own = ((section + j) & 1) == core
        table = jnp.stack(
            [is_own.astype(jnp.int32)]
            + [place(utt) for utt in utts]
            + [mem_len[utt] for utt in utts]
        )
        got = attend(table, rows, query_pair, kv_own, kv_oth)
        att += [got[0]] + [flip(got[k], CHIPS[k]) for k in range(1, 4)]

    limits = [tok_len[section * MB + 2 * slot + j] for j in range(2)]
    out_table = jnp.stack([group.astype(jnp.int32)] + limits)
    return project(
        out_table, att, w_out, out_core, direct, crossed, jnp.concatenate(hop_x, 0)
    )


def solution(mesh):
    return jax.shard_map(
        shards,
        mesh=mesh,
        in_specs=(
            P(("groups", "section"), None),
            P(("groups", "section"), None),
            P(None, "section"),
            P(None, "section"),
            P(None, "section"),
            P("section", None),
            P("groups"),
            P("groups"),
        ),
        out_specs=P(("groups", "section"), None),
        check_vma=False,
    )
```

time: 616 us -> 258 us (0.42)
  waiting for transfers between devices: 487 us -> 129 us
  starting transfers between devices: 14.2 us -> 75.6 us
  other arithmetic: 54.2 us -> 3.85 us
  Pallas kernels: 0 us -> 30.7 us
  matrix products: 30.6 us -> 0 us
  between operations: 13.5 us -> 0.33 us
    ppermute x7 -> x39, waiting for transfers between devices: 486 us -> 129 us  [the longest x33 63.5 us: flip(): return lax.ppermute(value, 'section', [(i, i ^ bits) for i in range(size)])]
    ppermute x7 -> x39, starting transfers between devices: 14.2 us -> 75.6 us  [the longest x33 63.8 us: flip(): return lax.ppermute(value, 'section', [(i, i ^ bits) for i in range(size)])]
    pallas_call x0 -> x5, Pallas kernels: none -> 30.7 us  [the longest x1 11 us: project(): pl.pallas_call(project_kernel, out_shape=jax.ShapeDtypeStruct(x.shape, BF...]
    dot_general x5 -> x0, matrix products: 30.6 us -> none  [the longest x1 10.2 us: shards(): jnp.dot(lax.all_gather(memory, 'section', axis=0, tiled=True), w_pair, pr...]
    select_n x9 -> x0, other arithmetic: 26.7 us -> none  [the longest x3 15.5 us: shards(): send_half = jnp.where(is_upper, lower_half, upper_half)]
    add x2 -> x0, other arithmetic: 14.9 us -> none  [shards(): partial_value = keep_half + swapped(send_half, 'section', bit_no)]
    reduce_sum x1 -> x0, other arithmetic: 7.59 us -> none  [shards(): jnp.mean(widened * widened, -1, keepdims=True) + norm_eps]
  transfers between devices with their start and end apart: 8 -> 39, of which waited for: 7 -> 16; matrix products, arithmetic and copies ran while one was open for 5% -> 5% of each run, Pallas kernels for 0% -> 8%
where the time goes in v1:
time: 258 us; the launch traced here: 257 us
  waiting for transfers between devices  129 us (50%)
  starting transfers between devices  75.6 us (29%)
  Pallas kernels  30.7 us (12%)
  local copies, waits for them, and re-layouts  17.2 us (7%)
  other arithmetic  3.85 us (1%)
    ppermute x33, starting transfers between devices, flip(): return lax.ppermute(value, 'section', [(i, i ^ bits) for i in range(size)])  63.8 us
    ppermute x33, waiting for transfers between devices, flip(): return lax.ppermute(value, 'section', [(i, i ^ bits) for i in range(size)])  63.5 us
    ppermute x3, waiting for transfers between devices, hop(): lax.ppermute(value, 'section', [(i, (i + GROUP) % size) for i in range(si...  36.3 us
    ppermute x3, waiting for transfers between devices, across(): return lax.ppermute(value, 'groups', [(0, 1), (1, 0)])  29.8 us
    pallas_call x1, Pallas kernels, project(): pl.pallas_call(project_kernel, out_shape=jax.ShapeDtypeStruct(x.shape, BF...  11 us
    pallas_call x2, Pallas kernels, keys_values(): pl.pallas_call(keys_values_kernel, out_shape=jax.ShapeDtypeStruct((rows,...  10.4 us
    pallas_call x2, Pallas kernels, attend(): pl.pallas_call(attend_kernel, out_shape=jax.ShapeDtypeStruct((4, FR, 2 *...  9.39 us
    unnamed x61, local copies, waits for them, and re-layouts  8.08 us
  transfers between devices with their start and end apart: 39, of which 16 were waited for; matrix products, arithmetic and copies ran while one was open for 5% of the time, Pallas kernels for 8%

profile of v1, /device:TPU:0, one launch (start us, length us, event | category | flops | bytes accessed | tf_op | source)
XLA Modules:
  0.0 257.2 jit_solution(1483168145760230716)
XLA Ops:
  0.0 4.0 %collective-permute-start.10 = (bf16[64,4096]{1,0:T(8,128)(2,1)}, bf16[64,4096]{1,0:T(8,128)(2,1)S(1)}, u32[]{:S(2)}, u32[]{:S(2)}) collective-permute-start(bf16[64,4096]{1,0:T(8,128)(2,1)} %refs_0_.1), channel_id=1, source_target_pairs={{0,8},{1,9},{2,10},{3,11},{4,12},{5,13},{6,14},{7,15},{8,0},{9,1},... | collective-permute-start | bytes 1572872 | tf_op jit(solution)/shard_map/ppermute | solution.py:32
  8.8 2.6 %collective-permute-start = (bf16[64,4096]{1,0:T(8,128)(2,1)S(1)}, bf16[64,4096]{1,0:T(8,128)(2,1)S(1)}, u32[]{:S(2)}, u32[]{:S(2)}) collective-permute-start(bf16[64,4096]{1,0:T(8,128)(2,1)S(1)} %get-tuple-element.6), channel_id=1, source_target_pairs={{0,8},{1,9},{2,10},{3,11},{4,12},{5,13},{6,14},{7,15},{8,0},{9,1},... | collective-permute-start | bytes 1572872 | tf_op jit(solution)/shard_map/ppermute | solution.py:32
  11.4 17.7 %collective-permute-done.10.refs_0_ = bf16[64,4096]{1,0:T(8,128)(2,1)S(1)} collective-permute-done((bf16[64,4096]{1,0:T(8,128)(2,1)}, bf16[64,4096]{1,0:T(8,128)(2,1)S(1)}, u32[]{:S(2)}, u32[]{:S(2)}) %collective-permute-start.10) | collective-permute-done | bytes 524320 | tf_op jit(solution)/shard_map/ppermute | solution.py:32
  29.2 22.4 %collective-permute-start.11 = (bf16[64,4096]{1,0:T(8,128)(2,1)S(1)}, bf16[64,4096]{1,0:T(8,128)(2,1)S(1)}, u32[]{:S(2)}, u32[]{:S(2)}) collective-permute-start(bf16[64,4096]{1,0:T(8,128)(2,1)S(1)} %collective-permute-done.10.refs_0_), channel_id=1, source_target_pairs={{0,2},{1,3},{2,0},{3,1},{4,6},{5,7},{6,4},{7,5},{8,10},{9,11},{10,... | collective-permute-start | bytes 1572872 | tf_op jit(solution)/shard_map/ppermute | solution.py:27
  54.0 8.0 %collective-permute-done.19.x0 = bf16[64,4096]{1,0:T(8,128)(2,1)S(1)} collective-permute-done((bf16[64,4096]{1,0:T(8,128)(2,1)S(1)}, bf16[64,4096]{1,0:T(8,128)(2,1)S(1)}, u32[]{:S(2)}, u32[]{:S(2)}) %collective-permute-start.19) | collective-permute-done | bytes 524320 | tf_op jit(solution)/shard_map/ppermute | solution.py:32
  62.0 10.5 %collective-permute-done.x0 = bf16[64,4096]{1,0:T(8,128)(2,1)S(1)} collective-permute-done((bf16[64,4096]{1,0:T(8,128)(2,1)S(1)}, bf16[64,4096]{1,0:T(8,128)(2,1)S(1)}, u32[]{:S(2)}, u32[]{:S(2)}) %collective-permute-start) | collective-permute-done | bytes 524320 | tf_op jit(solution)/shard_map/ppermute | solution.py:32
  76.3 10.5 %collective-permute-start.1 = (bf16[64,4096]{1,0:T(8,128)(2,1)S(1)}, bf16[64,4096]{1,0:T(8,128)(2,1)}, u32[]{:S(2)}, u32[]{:S(2)}) collective-permute-start(bf16[64,4096]{1,0:T(8,128)(2,1)S(1)} %collective-permute-done.x0), channel_id=1, source_target_pairs={{0,2},{1,3},{2,0},{3,1},{4,6},{5,7},{6,4},{7,5},{8,10},{9,11},{10,... | collective-permute-start | bytes 1572872 | tf_op jit(solution)/shard_map/ppermute | solution.py:27
  89.4 9.4 %collective-permute-start.27 = (bf16[256,2048]{1,0:T(8,128)(2,1)S(1)}, bf16[256,2048]{1,0:T(8,128)(2,1)}, u32[]{:S(2)}, u32[]{:S(2)}) collective-permute-start(bf16[256,2048]{1,0:T(8,128)(2,1)S(1)} %constant_dynamic-slice_fusion), channel_id=1, source_target_pairs={{0,2},{1,3},{2,0},{3,1},{4,6},{5,7},{6,4},{7,5},{8,10},{9,11},{10,... | collective-permute-start | bytes 3145736 | tf_op jit(solution)/shard_map/ppermute | solution.py:27
  99.5 23.2 %collective-permute-done.27.refs_10_ = bf16[256,2048]{1,0:T(8,128)(2,1)} collective-permute-done((bf16[256,2048]{1,0:T(8,128)(2,1)S(1)}, bf16[256,2048]{1,0:T(8,128)(2,1)}, u32[]{:S(2)}, u32[]{:S(2)}) %collective-permute-start.27) | collective-permute-done | bytes 1048608 | tf_op jit(solution)/shard_map/ppermute | solution.py:27
  122.7 1.7 collective-permute-start.13
  124.7 12.8 %collective-permute-done.13.refs_3_ = bf16[64,4096]{1,0:T(8,128)(2,1)S(1)} collective-permute-done((bf16[64,4096]{1,0:T(8,128)(2,1)S(1)}, bf16[64,4096]{1,0:T(8,128)(2,1)S(1)}, u32[]{:S(2)}, u32[]{:S(2)}) %collective-permute-start.13) | collective-permute-done | bytes 524320 | tf_op jit(solution)/shard_map/ppermute | solution.py:27
  137.5 1.8 collective-permute-start.3
  139.3 9.5 %collective-permute-done.22.x3 = bf16[64,4096]{1,0:T(8,128)(2,1)S(1)} collective-permute-done((bf16[64,4096]{1,0:T(8,128)(2,1)S(1)}, bf16[64,4096]{1,0:T(8,128)(2,1)S(1)}, u32[]{:S(2)}, u32[]{:S(2)}) %collective-permute-start.22) | collective-permute-done | bytes 524320 | tf_op jit(solution)/shard_map/ppermute | solution.py:27
  150.0 1.7 collective-permute-start.33
  151.8 5.2 %shard_map.83 = bf16[256,1024]{1,0:T(8,128)(2,1)S(1)} custom-call(bf16[64,4096]{1,0:T(8,128)(2,1)S(1)} %copy-done.16, bf16[64,4096]{1,0:T(8,128)(2,1)S(1)} %copy-done.22, bf16[64,4096]{1,0:T(8,128)(2,1)S(1)} %copy-done.18, bf16[64,4096]{1,0:T(8,128)(2,1)S(1)} %collective-permute-done.13.refs_3_, bf16[4096,256]{1,0:T(8,128)(2,1)S(1)} %copy-done, ...), custom_call_target="tpu_custom_call" | custom-call | flops 2147483648 | bytes 11010048 | tf_op jit(solution)/shard_map/pallas_call | solution.py:59
  157.0 1.9 collective-permute-done.3.x3
  159.7 5.2 %shard_map.82 = bf16[256,1024]{1,0:T(8,128)(2,1)S(1)} custom-call(bf16[64,4096]{1,0:T(8,128)(2,1)S(1)} %copy-done.10, bf16[64,4096]{1,0:T(8,128)(2,1)S(1)} %copy-done.14, bf16[64,4096]{1,0:T(8,128)(2,1)S(1)} %copy-done.12, bf16[64,4096]{1,0:T(8,128)(2,1)S(1)} %copy-done.20, bf16[4096,256]{1,0:T(8,128)(2,1)S(1)} %copy-done, ...), custom_call_target="tpu_custom_call" | custom-call | flops 2147483648 | bytes 11010048 | tf_op jit(solution)/shard_map/pallas_call | solution.py:59
  165.5 6.6 %collective-permute-done.29.refs_12_ = bf16[256,2048]{1,0:T(8,128)(2,1)} collective-permute-done((bf16[256,2048]{1,0:T(8,128)(2,1)}, bf16[256,2048]{1,0:T(8,128)(2,1)}, u32[]{:S(2)}, u32[]{:S(2)}) %collective-permute-start.29) | collective-permute-done | bytes 1048608 | tf_op jit(solution)/shard_map/ppermute | solution.py:27
  175.7 1.7 collective-permute-start.35
  178.1 2.5 stack.63.table
  182.4 4.6 %shard_map.85 = bf16[4,64,512]{2,1,0:T(8,128)(2,1)S(1)} custom-call(s32[9]{0:T(128)S(1)} %stack.63.table, bf16[64,4096]{1,0:T(8,128)(2,1)S(1)} %collective-permute-done.19.x0, bf16[64,4096]{1,0:T(8,128)(2,1)} %collective-permute-done.20.x1, bf16[64,4096]{1,0:T(8,128)(2,1)S(1)} %copy-done.5, bf16[64,4096]{1,0:T(8,128)(2,1)S(1)} %copy-done.9, ...), custom_call_target="tpu_custom_call" | custom-call | flops 1073741824 | bytes 8388608 | tf_op jit(solution)/shard_map/pallas_call | solution.py:120
  187.0 11.5 %collective-permute-done.34.refs_17_ = bf16[256,2048]{1,0:T(8,128)(2,1)} collective-permute-done((bf16[256,2048]{1,0:T(8,128)(2,1)}, bf16[256,2048]{1,0:T(8,128)(2,1)}, u32[]{:S(2)}, u32[]{:S(2)}) %collective-permute-start.34) | collective-permute-done | bytes 1048608 | tf_op jit(solution)/shard_map/ppermute | solution.py:36
  200.4 17.6 %collective-permute-done.35.refs_18_ = bf16[256,2048]{1,0:T(8,128)(2,1)} collective-permute-done((bf16[256,2048]{1,0:T(8,128)(2,1)}, bf16[256,2048]{1,0:T(8,128)(2,1)}, u32[]{:S(2)}, u32[]{:S(2)}) %collective-permute-start.35) | collective-permute-done | bytes 1048608 | tf_op jit(solution)/shard_map/ppermute | solution.py:36
  218.1 2.6 %stack.56.table = s32[9]{0:T(128)S(1)} concatenate(s32[1]{0:T(128)} %bitcast.1, s32[1]{0:T(128)} %bitcast.2, s32[1]{0:T(128)} %bitcast.3, s32[1]{0:T(128)} %bitcast.4, s32[1]{0:T(128)} %bitcast.5, s32[1]{0:T(128)} %get-tuple-element.21, s32[1]{0:T(128)} %get-tuple-element.20, s32[1]{0:T(128)} %get-tuple-element.19, s32[1]{0:T(128)} %get-tuple-element.18), dimensions={0} | concatenate | bytes 72 | tf_op jit(solution)/shard_map/stack | solution.py:253
  222.5 4.8 %shard_map.84 = bf16[4,64,512]{2,1,0:T(8,128)(2,1)S(1)} custom-call(s32[9]{0:T(128)S(1)} %stack.56.table, bf16[64,4096]{1,0:T(8,128)(2,1)S(1)} %collective-permute-done.x0, bf16[64,4096]{1,0:T(8,128)(2,1)} %collective-permute-done.1.x1, bf16[64,4096]{1,0:T(8,128)(2,1)} %collective-permute-done.2.x2, bf16[64,4096]{1,0:T(8,128)(2,1)S(1)} %copy-done.7, ...), custom_call_target="tpu_custom_call" | custom-call | flops 1073741824 | bytes 8388608 | tf_op jit(solution)/shard_map/pallas_call | solution.py:120
  227.3 2.1 collective-permute-start.25
  229.4 3.1 %collective-permute-done.25.refs_7_ = bf16[64,512]{1,0:T(8,128)(2,1)S(1)} collective-permute-done((bf16[64,512]{1,0:T(8,128)(2,1)S(1)}, bf16[64,512]{1,0:T(8,128)(2,1)S(1)}, u32[]{:S(2)}, u32[]{:S(2)}) %collective-permute-start.25) | collective-permute-done | bytes 65568 | tf_op jit(solution)/shard_map/ppermute | solution.py:27
  234.4 2.4 collective-permute-done.16.refs_1_
  239.4 1.6 collective-permute-done.17.refs_2_
  241.1 2.5 collective-permute-start.18
  244.6 1.6 collective-permute-done.18.refs_3_
  246.3 11.0 %shard_map.86 = bf16[128,4096]{1,0:T(8,128)(2,1)} custom-call(s32[3]{0:T(128)S(1)} %pad_add_fusion.table, bf16[64,512]{1,0:T(8,128)(2,1)S(1)} %get-tuple-element.14.refs_0_, bf16[64,512]{1,0:T(8,128)(2,1)S(1)} %collective-permute-done.16.refs_1_, bf16[64,512]{1,0:T(8,128)(2,1)S(1)} %collective-permute-done.17.refs_2_, ...), custom_call_target="tpu_custom_call" | custom-call | flops 2147483648 | bytes 18874368 | tf_op jit(solution)/shard_map/pallas_call | solution.py:177
  (124 shorter events, 32.6 us)
Async XLA Ops:
  0.0 29.1 %collective-permute-start.10 = (bf16[64,4096]{1,0:T(8,128)(2,1)}, bf16[64,4096]{1,0:T(8,128)(2,1)S(1)}, u32[]{:S(2)}, u32[]{:S(2)}) collective-permute-start(bf16[64,4096]{1,0:T(8,128)(2,1)} %refs_0_.1), channel_id=1, source_target_pairs={{0,8},{1,9},{2,10},{3,11},{4,12},{5,13},{6,14},{7,15},{8,0},{9,1},... | collective-permute-start | bytes 1572872 | tf_op jit(solution)/shard_map/ppermute | solution.py:32
  4.0 25.2 %collective-permute-start.6 = (bf16[64,4096]{1,0:T(8,128)(2,1)}, bf16[64,4096]{1,0:T(8,128)(2,1)S(1)}, u32[]{:S(2)}, u32[]{:S(2)}) collective-permute-start(bf16[64,4096]{1,0:T(8,128)(2,1)} %refs_0_.1), channel_id=1, source_target_pairs={{0,4},{1,5},{2,6},{3,7},{4,0},{5,1},{6,2},{7,3},{8,12},{9,13},{10,... | collective-permute-start | bytes 1572872 | tf_op jit(solution)/shard_map/ppermute | solution.py:27
  5.6 46.8 %collective-permute-start.5 = (bf16[64,4096]{1,0:T(8,128)(2,1)}, bf16[64,4096]{1,0:T(8,128)(2,1)S(1)}, u32[]{:S(2)}, u32[]{:S(2)}) collective-permute-start(bf16[64,4096]{1,0:T(8,128)(2,1)} %refs_0_.1), channel_id=1, source_target_pairs={{0,2},{1,3},{2,0},{3,1},{4,6},{5,7},{6,4},{7,5},{8,10},{9,11},{10,... | collective-permute-start | bytes 1572872 | tf_op jit(solution)/shard_map/ppermute | solution.py:27
  8.4 53.6 %collective-permute-start.19 = (bf16[64,4096]{1,0:T(8,128)(2,1)S(1)}, bf16[64,4096]{1,0:T(8,128)(2,1)S(1)}, u32[]{:S(2)}, u32[]{:S(2)}) collective-permute-start(bf16[64,4096]{1,0:T(8,128)(2,1)S(1)} %get-tuple-element.5), channel_id=1, source_target_pairs={{0,8},{1,9},{2,10},{3,11},{4,12},{5,13},{6,14},{7,15},{8,0},{9,1},... | collective-permute-start | bytes 1572872 | tf_op jit(solution)/shard_map/ppermute | solution.py:32
  8.8 63.7 %collective-permute-start = (bf16[64,4096]{1,0:T(8,128)(2,1)S(1)}, bf16[64,4096]{1,0:T(8,128)(2,1)S(1)}, u32[]{:S(2)}, u32[]{:S(2)}) collective-permute-start(bf16[64,4096]{1,0:T(8,128)(2,1)S(1)} %get-tuple-element.6), channel_id=1, source_target_pairs={{0,8},{1,9},{2,10},{3,11},{4,12},{5,13},{6,14},{7,15},{8,0},{9,1},... | collective-permute-start | bytes 1572872 | tf_op jit(solution)/shard_map/ppermute | solution.py:32
  29.1 44.9 %collective-permute-start.12 = (bf16[64,4096]{1,0:T(8,128)(2,1)S(1)}, bf16[64,4096]{1,0:T(8,128)(2,1)S(1)}, u32[]{:S(2)}, u32[]{:S(2)}) collective-permute-start(bf16[64,4096]{1,0:T(8,128)(2,1)S(1)} %collective-permute-done.10.refs_0_), channel_id=1, source_target_pairs={{0,4},{1,5},{2,6},{3,7},{4,0},{5,1},{6,2},{7,3},{8,12},{9,13},{10,... | collective-permute-start | bytes 1572872 | tf_op jit(solution)/shard_map/ppermute | solution.py:27
  29.2 45.4 %collective-permute-start.11 = (bf16[64,4096]{1,0:T(8,128)(2,1)S(1)}, bf16[64,4096]{1,0:T(8,128)(2,1)S(1)}, u32[]{:S(2)}, u32[]{:S(2)}) collective-permute-start(bf16[64,4096]{1,0:T(8,128)(2,1)S(1)} %collective-permute-done.10.refs_0_), channel_id=1, source_target_pairs={{0,2},{1,3},{2,0},{3,1},{4,6},{5,7},{6,4},{7,5},{8,10},{9,11},{10,... | collective-permute-start | bytes 1572872 | tf_op jit(solution)/shard_map/ppermute | solution.py:27
  53.2 22.3 %collective-permute-start.7 = (bf16[64,4096]{1,0:T(8,128)(2,1)S(1)}, bf16[64,4096]{1,0:T(8,128)(2,1)S(1)}, u32[]{:S(2)}, u32[]{:S(2)}) collective-permute-start(bf16[64,4096]{1,0:T(8,128)(2,1)S(1)} %collective-permute-done.6.refs_2_), channel_id=1, source_target_pairs={{0,2},{1,3},{2,0},{3,1},{4,6},{5,7},{6,4},{7,5},{8,10},{9,11},{10,... | collective-permute-start | bytes 1572872 | tf_op jit(solution)/shard_map/ppermute | solution.py:27
  62.0 24.8 %collective-permute-start.21 = (bf16[64,4096]{1,0:T(8,128)(2,1)S(1)}, bf16[64,4096]{1,0:T(8,128)(2,1)S(1)}, u32[]{:S(2)}, u32[]{:S(2)}) collective-permute-start(bf16[64,4096]{1,0:T(8,128)(2,1)S(1)} %collective-permute-done.19.x0), channel_id=1, source_target_pairs={{0,4},{1,5},{2,6},{3,7},{4,0},{5,1},{6,2},{7,3},{8,12},{9,13},{10,... | collective-permute-start | bytes 1572872 | tf_op jit(solution)/shard_map/ppermute | solution.py:27
  72.5 16.9 %collective-permute-start.20 = (bf16[64,4096]{1,0:T(8,128)(2,1)S(1)}, bf16[64,4096]{1,0:T(8,128)(2,1)}, u32[]{:S(2)}, u32[]{:S(2)}) collective-permute-start(bf16[64,4096]{1,0:T(8,128)(2,1)S(1)} %collective-permute-done.19.x0), channel_id=1, source_target_pairs={{0,2},{1,3},{2,0},{3,1},{4,6},{5,7},{6,4},{7,5},{8,10},{9,11},{10,... | collective-permute-start | bytes 1572872 | tf_op jit(solution)/shard_map/ppermute | solution.py:27
  74.1 24.7 %collective-permute-start.2 = (bf16[64,4096]{1,0:T(8,128)(2,1)S(1)}, bf16[64,4096]{1,0:T(8,128)(2,1)}, u32[]{:S(2)}, u32[]{:S(2)}) collective-permute-start(bf16[64,4096]{1,0:T(8,128)(2,1)S(1)} %collective-permute-done.x0), channel_id=1, source_target_pairs={{0,4},{1,5},{2,6},{3,7},{4,0},{5,1},{6,2},{7,3},{8,12},{9,13},{10,... | collective-permute-start | bytes 1572872 | tf_op jit(solution)/shard_map/ppermute | solution.py:27
  75.5 74.5 %collective-permute-start.8 = (bf16[4096,256]{1,0:T(8,128)(2,1)S(1)}, bf16[4096,256]{1,0:T(8,128)(2,1)}, u32[]{:S(2)}, u32[]{:S(2)}) collective-permute-start(bf16[4096,256]{1,0:T(8,128)(2,1)S(1)} %copy-done), channel_id=1, source_target_pairs={{0,1},{1,0},{2,3},{3,2},{4,5},{5,4},{6,7},{7,6},{8,9},{9,8},{10,11... | collective-permute-start | bytes 6291464 | tf_op jit(solution)/shard_map/ppermute | solution.py:27
  76.3 23.2 %collective-permute-start.1 = (bf16[64,4096]{1,0:T(8,128)(2,1)S(1)}, bf16[64,4096]{1,0:T(8,128)(2,1)}, u32[]{:S(2)}, u32[]{:S(2)}) collective-permute-start(bf16[64,4096]{1,0:T(8,128)(2,1)S(1)} %collective-permute-done.x0), channel_id=1, source_target_pairs={{0,2},{1,3},{2,0},{3,1},{4,6},{5,7},{6,4},{7,5},{8,10},{9,11},{10,... | collective-permute-start | bytes 1572872 | tf_op jit(solution)/shard_map/ppermute | solution.py:27
  87.6 64.1 %collective-permute-start.9 = (bf16[4096,256]{1,0:T(8,128)(2,1)}, bf16[4096,256]{1,0:T(8,128)(2,1)}, u32[]{:S(2)}, u32[]{:S(2)}) collective-permute-start(bf16[4096,256]{1,0:T(8,128)(2,1)} %refs_6_.3), channel_id=1, source_target_pairs={{0,1},{1,0},{2,3},{3,2},{4,5},{5,4},{6,7},{7,6},{8,9},{9,8},{10,11... | collective-permute-start | bytes 6291464 | tf_op jit(solution)/shard_map/ppermute | solution.py:27
  89.4 33.3 %collective-permute-start.27 = (bf16[256,2048]{1,0:T(8,128)(2,1)S(1)}, bf16[256,2048]{1,0:T(8,128)(2,1)}, u32[]{:S(2)}, u32[]{:S(2)}) collective-permute-start(bf16[256,2048]{1,0:T(8,128)(2,1)S(1)} %constant_dynamic-slice_fusion), channel_id=1, source_target_pairs={{0,2},{1,3},{2,0},{3,1},{4,6},{5,7},{6,4},{7,5},{8,10},{9,11},{10,... | collective-permute-start | bytes 3145736 | tf_op jit(solution)/shard_map/ppermute | solution.py:27
  98.8 25.7 %collective-permute-start.28 = (bf16[256,2048]{1,0:T(8,128)(2,1)S(1)}, bf16[256,2048]{1,0:T(8,128)(2,1)}, u32[]{:S(2)}, u32[]{:S(2)}) collective-permute-start(bf16[256,2048]{1,0:T(8,128)(2,1)S(1)} %constant_dynamic-slice_fusion), channel_id=1, source_target_pairs={{0,4},{1,5},{2,6},{3,7},{4,0},{5,1},{6,2},{7,3},{8,12},{9,13},{10,... | collective-permute-start | bytes 3145736 | tf_op jit(solution)/shard_map/ppermute | solution.py:27
  99.5 65.4 %collective-permute-start.4 = (bf16[4096,256]{1,0:T(8,128)(2,1)}, bf16[4096,256]{1,0:T(8,128)(2,1)S(1)}, u32[]{:S(2)}, u32[]{:S(2)}) collective-permute-start(bf16[4096,256]{1,0:T(8,128)(2,1)} %query_own.3), channel_id=1, source_target_pairs={{0,1},{1,0},{2,3},{3,2},{4,5},{5,4},{6,7},{7,6},{8,9},{9,8},{10,11... | collective-permute-start | bytes 6291464 | tf_op jit(solution)/shard_map/ppermute | solution.py:27
  122.7 14.8 %collective-permute-start.13 = (bf16[64,4096]{1,0:T(8,128)(2,1)S(1)}, bf16[64,4096]{1,0:T(8,128)(2,1)S(1)}, u32[]{:S(2)}, u32[]{:S(2)}) collective-permute-start(bf16[64,4096]{1,0:T(8,128)(2,1)S(1)} %copy-done.18), channel_id=1, source_target_pairs={{0,2},{1,3},{2,0},{3,1},{4,6},{5,7},{6,4},{7,5},{8,10},{9,11},{10,... | collective-permute-start | bytes 1572872 | tf_op jit(solution)/shard_map/ppermute | solution.py:27
  124.4 24.3 %collective-permute-start.22 = (bf16[64,4096]{1,0:T(8,128)(2,1)S(1)}, bf16[64,4096]{1,0:T(8,128)(2,1)S(1)}, u32[]{:S(2)}, u32[]{:S(2)}) collective-permute-start(bf16[64,4096]{1,0:T(8,128)(2,1)S(1)} %copy-done.4), channel_id=1, source_target_pairs={{0,2},{1,3},{2,0},{3,1},{4,6},{5,7},{6,4},{7,5},{8,10},{9,11},{10,... | collective-permute-start | bytes 1572872 | tf_op jit(solution)/shard_map/ppermute | solution.py:27
  137.5 21.4 %collective-permute-start.3 = (bf16[64,4096]{1,0:T(8,128)(2,1)}, bf16[64,4096]{1,0:T(8,128)(2,1)S(1)}, u32[]{:S(2)}, u32[]{:S(2)}) collective-permute-start(bf16[64,4096]{1,0:T(8,128)(2,1)} %collective-permute-done.2.x2), channel_id=1, source_target_pairs={{0,2},{1,3},{2,0},{3,1},{4,6},{5,7},{6,4},{7,5},{8,10},{9,11},{10,... | collective-permute-start | bytes 1572872 | tf_op jit(solution)/shard_map/ppermute | solution.py:27
  148.7 23.4 %collective-permute-start.29 = (bf16[256,2048]{1,0:T(8,128)(2,1)}, bf16[256,2048]{1,0:T(8,128)(2,1)}, u32[]{:S(2)}, u32[]{:S(2)}) collective-permute-start(bf16[256,2048]{1,0:T(8,128)(2,1)} %collective-permute-done.27.refs_10_), channel_id=1, source_target_pairs={{0,4},{1,5},{2,6},{3,7},{4,0},{5,1},{6,2},{7,3},{8,12},{9,13},{10,... | collective-permute-start | bytes 3145736 | tf_op jit(solution)/shard_map/ppermute | solution.py:27
  150.0 24.1 %collective-permute-start.33 = (bf16[256,2048]{1,0:T(8,128)(2,1)}, bf16[256,2048]{1,0:T(8,128)(2,1)}, u32[]{:S(2)}, u32[]{:S(2)}) collective-permute-start(bf16[256,2048]{1,0:T(8,128)(2,1)} %collective-permute-done.27.refs_10_), channel_id=1, source_target_pairs={{0,16},{16,0},{1,17},{17,1},{2,18},{18,2},{3,19},{19,3},{4,20},{20... | collective-permute-start | bytes 3145736 | tf_op jit(solution)/shard_map/ppermute | solution.py:36
  151.7 48.6 %collective-permute-start.26 = (bf16[256,4096]{1,0:T(8,128)(2,1)}, bf16[256,4096]{1,0:T(8,128)(2,1)}, u32[]{:S(2)}, u32[]{:S(2)}) collective-permute-start(bf16[256,4096]{1,0:T(8,128)(2,1)} %refs_8_.1), channel_id=1, source_target_pairs={{0,1},{1,0},{2,3},{3,2},{4,5},{5,4},{6,7},{7,6},{8,9},{9,8},{10,11... | collective-permute-start | bytes 6291464 | tf_op jit(solution)/shard_map/ppermute | solution.py:27
  172.1 26.4 %collective-permute-start.34 = (bf16[256,2048]{1,0:T(8,128)(2,1)}, bf16[256,2048]{1,0:T(8,128)(2,1)}, u32[]{:S(2)}, u32[]{:S(2)}) collective-permute-start(bf16[256,2048]{1,0:T(8,128)(2,1)} %collective-permute-done.28.refs_11_), channel_id=1, source_target_pairs={{0,16},{16,0},{1,17},{17,1},{2,18},{18,2},{3,19},{19,3},{4,20},{20... | collective-permute-start | bytes 3145736 | tf_op jit(solution)/shard_map/ppermute | solution.py:36
  174.0 25.8 %collective-permute-start.30 = (bf16[256,2048]{1,0:T(8,128)(2,1)}, bf16[256,2048]{1,0:T(8,128)(2,1)}, u32[]{:S(2)}, u32[]{:S(2)}) collective-permute-start(bf16[256,2048]{1,0:T(8,128)(2,1)} %collective-permute-done.27.refs_10_), channel_id=1, source_target_pairs={{0,1},{1,0},{2,3},{3,2},{4,5},{5,4},{6,7},{7,6},{8,9},{9,8},{10,11... | collective-permute-start | bytes 3145736 | tf_op jit(solution)/shard_map/ppermute | solution.py:27
  174.1 25.8 %collective-permute-start.31 = (bf16[256,2048]{1,0:T(8,128)(2,1)}, bf16[256,2048]{1,0:T(8,128)(2,1)}, u32[]{:S(2)}, u32[]{:S(2)}) collective-permute-start(bf16[256,2048]{1,0:T(8,128)(2,1)} %collective-permute-done.28.refs_11_), channel_id=1, source_target_pairs={{0,1},{1,0},{2,3},{3,2},{4,5},{5,4},{6,7},{7,6},{8,9},{9,8},{10,11... | collective-permute-start | bytes 3145736 | tf_op jit(solution)/shard_map/ppermute | solution.py:27
  175.7 42.4 %collective-permute-start.35 = (bf16[256,2048]{1,0:T(8,128)(2,1)}, bf16[256,2048]{1,0:T(8,128)(2,1)}, u32[]{:S(2)}, u32[]{:S(2)}) collective-permute-start(bf16[256,2048]{1,0:T(8,128)(2,1)} %collective-permute-done.29.refs_12_), channel_id=1, source_target_pairs={{0,16},{16,0},{1,17},{17,1},{2,18},{18,2},{3,19},{19,3},{4,20},{20... | collective-permute-start | bytes 3145736 | tf_op jit(solution)/shard_map/ppermute | solution.py:36
  198.5 22.1 %collective-permute-start.23 = (bf16[64,512]{1,0:T(8,128)(2,1)S(1)}, bf16[64,512]{1,0:T(8,128)(2,1)S(1)}, u32[]{:S(2)}, u32[]{:S(2)}) collective-permute-start(bf16[64,512]{1,0:T(8,128)(2,1)S(1)} %get-tuple-element.9), channel_id=1, source_target_pairs={{0,2},{1,3},{2,0},{3,1},{4,6},{5,7},{6,4},{7,5},{8,10},{9,11},{10,... | collective-permute-start | bytes 196616 | tf_op jit(solution)/shard_map/ppermute | solution.py:27
  199.8 46.4 %collective-permute-start.32 = (bf16[256,2048]{1,0:T(8,128)(2,1)}, bf16[256,2048]{1,0:T(8,128)(2,1)}, u32[]{:S(2)}, u32[]{:S(2)}) collective-permute-start(bf16[256,2048]{1,0:T(8,128)(2,1)} %collective-permute-done.29.refs_12_), channel_id=1, source_target_pairs={{0,1},{1,0},{2,3},{3,2},{4,5},{5,4},{6,7},{7,6},{8,9},{9,8},{10,11... | collective-permute-start | bytes 3145736 | tf_op jit(solution)/shard_map/ppermute | solution.py:27
  199.8 46.4 %collective-permute-start.36 = (bf16[256,2048]{1,0:T(8,128)(2,1)}, bf16[256,2048]{1,0:T(8,128)(2,1)}, u32[]{:S(2)}, u32[]{:S(2)}) collective-permute-start(bf16[256,2048]{1,0:T(8,128)(2,1)} %collective-permute-done.33.refs_16_), channel_id=1, source_target_pairs={{0,1},{1,0},{2,3},{3,2},{4,5},{5,4},{6,7},{7,6},{8,9},{9,8},{10,11... | collective-permute-start | bytes 3145736 | tf_op jit(solution)/shard_map/ppermute | solution.py:27
  200.4 45.9 %collective-permute-start.37 = (bf16[256,2048]{1,0:T(8,128)(2,1)}, bf16[256,2048]{1,0:T(8,128)(2,1)}, u32[]{:S(2)}, u32[]{:S(2)}) collective-permute-start(bf16[256,2048]{1,0:T(8,128)(2,1)} %collective-permute-done.34.refs_17_), channel_id=1, source_target_pairs={{0,1},{1,0},{2,3},{3,2},{4,5},{5,4},{6,7},{7,6},{8,9},{9,8},{10,11... | collective-permute-start | bytes 3145736 | tf_op jit(solution)/shard_map/ppermute | solution.py:27
  218.1 28.2 %collective-permute-start.38 = (bf16[256,2048]{1,0:T(8,128)(2,1)}, bf16[256,2048]{1,0:T(8,128)(2,1)}, u32[]{:S(2)}, u32[]{:S(2)}) collective-permute-start(bf16[256,2048]{1,0:T(8,128)(2,1)} %collective-permute-done.35.refs_18_), channel_id=1, source_target_pairs={{0,1},{1,0},{2,3},{3,2},{4,5},{5,4},{6,7},{7,6},{8,9},{9,8},{10,11... | collective-permute-start | bytes 3145736 | tf_op jit(solution)/shard_map/ppermute | solution.py:27
  (37 other events, 701.1 us)

commit v2 on v1

v2 whole, which is shorter than its diff:
```python
import functools
import math

import jax
import jax.numpy as jnp
from jax import lax
from jax.experimental import pallas as pl
from jax.experimental.pallas import tpu as pltpu
from jax.sharding import PartitionSpec as P

HD = 128
FR = 64
GROUP = 8
MB = 16
MEMF = 64
NORM_EPS = 1e-06
BF16 = jnp.bfloat16
F32 = jnp.float32
VMEM_BYTES = 48 * 2**20

CORE, NEAR, FAR = 1, 2, 4
CHIPS = (0, NEAR, FAR, NEAR | FAR)


def flip(value, bits):
    size = lax.axis_size("section")
    return lax.ppermute(value, "section", [(i, i ^ bits) for i in range(size)])


def hop(value):
    size = lax.axis_size("section")
    return lax.ppermute(value, "section", [(i, (i + GROUP) % size) for i in range(size)])


def after(value, *others):
    return lax.optimization_barrier((value, *others))[0]


def across(value):
    return lax.ppermute(value, "groups", [(0, 1), (1, 0)])


def whole(count):
    return [pl.BlockSpec(memory_space=pltpu.VMEM)] * count


def dot(a, b):
    return jnp.dot(a, b, preferred_element_type=F32)


def keys_values_kernel(*refs):
    *mem_refs, key_own, key_oth, val_own, val_oth, out, rows = refs
    for k, ref in enumerate(mem_refs):
        rows[k * MEMF:(k + 1) * MEMF, :] = ref[:MEMF]
    width = key_own.shape[1]
    for k, weight in enumerate((key_own, key_oth, val_own, val_oth)):
        out[:, k * width:(k + 1) * width] = dot(rows[...], weight[...]).astype(BF16)


def keys_values(pieces, weights):
    depth, width = weights[0].shape
    rows = len(pieces) * MEMF
    return pl.pallas_call(
        keys_values_kernel,
        out_shape=jax.ShapeDtypeStruct((rows, 4 * width), BF16),
        in_specs=whole(len(pieces) + 4),
        out_specs=pl.BlockSpec(memory_space=pltpu.VMEM),
        scratch_shapes=[pltpu.VMEM((rows, depth), BF16)],
        compiler_params=pltpu.CompilerParams(vmem_limit_bytes=VMEM_BYTES),
        cost_estimate=pl.CostEstimate(
            flops=8 * rows * depth * width,
            bytes_accessed=2 * (rows * depth + 4 * depth * width + 4 * rows * width),
            transcendentals=0,
        ),
    )(*pieces, *weights)


def attend_kernel(j, ring, *refs):
    mem_len, x0, x1, x2, x3, query_own, query_oth = refs[:7]
    own_a, own_b, oth_a, oth_b = refs[7:11]
    outs, normed = refs[11:15], refs[15]
    width = query_own.shape[1]
    heads = 2 * width // HD
    me = lax.axis_index("section")
    section, slot, core = me // GROUP, me % GROUP, me % 2
    for k, ref in enumerate((x0, x1, x2, x3)):
        wide = ref[ref.shape[0] - FR:].astype(F32)
        scale = lax.rsqrt(jnp.mean(wide * wide, -1, keepdims=True) + NORM_EPS)
        normed[k * FR:(k + 1) * FR, :] = (wide * scale).astype(BF16)
    queries = jnp.concatenate(
        [dot(normed[...], query_own[...]), dot(normed[...], query_oth[...])], 1
    ).astype(BF16)
    is_own = (section + j) % 2 == core
    column = lax.broadcasted_iota(jnp.int32, (FR, MEMF), 1)
    scores, values = [], []
    for k, chip in enumerate(CHIPS):
        utt = (section + 2 * (slot ^ chip) + j) % MB
        place = (utt ^ me) >> 1 if ring else utt >> 1
        start = pl.multiple_of((place & 3) * MEMF, MEMF)
        here = pl.ds(start, MEMF)
        mine = jnp.where(place < 4, own_a[here, :], own_b[here, :])
        other = jnp.where(place < 4, oth_a[here, :], oth_b[here, :])
        other = jnp.concatenate(
            [other[:, n * width:(n + 1) * width] for n in (1, 0, 3, 2)], 1
        )
        kv = jnp.where(is_own, mine, other)
        length = mem_len[utt]
        values.append(kv[:, 2 * width:])
        for h in range(heads):
            found = lax.dot_general(
                queries[k * FR:(k + 1) * FR, h * HD:(h + 1) * HD],
                kv[:, h * HD:(h + 1) * HD],
                (((1,), (1,)), ((), ())),
                preferred_element_type=F32,
            )
            found = found * (1.0 / math.sqrt(HD))
            scores.append(jnp.where(column < length, found, -jnp.inf))
    score = jnp.concatenate(scores, 0)
    expo = jnp.exp(score - jnp.max(score, -1, keepdims=True))
    probs = (expo / jnp.sum(expo, -1, keepdims=True)).astype(BF16)
    for k in range(4):
        for h in range(heads):
            at = (k * heads + h) * FR
            outs[k][:, h * HD:(h + 1) * HD] = dot(
                probs[at:at + FR], values[k][:, h * HD:(h + 1) * HD]
            ).astype(BF16)


def attend(j, ring, mem_len, pieces, weights, kv):
    depth, width = weights[0].shape
    return pl.pallas_call(
        functools.partial(attend_kernel, j, ring),
        out_shape=[jax.ShapeDtypeStruct((FR, 2 * width), BF16)] * 4,
        in_specs=[pl.BlockSpec(memory_space=pltpu.SMEM)] + whole(10),
        out_specs=whole(4),
        scratch_shapes=[pltpu.VMEM((4 * FR, depth), BF16)],
        compiler_params=pltpu.CompilerParams(vmem_limit_bytes=VMEM_BYTES),
        cost_estimate=pl.CostEstimate(
            flops=16 * FR * depth * width,
            bytes_accessed=2 * (4 * FR * depth + 2 * depth * width) + 8 * kv[0].size,
            transcendentals=4 * FR * MEMF * 4,
        ),
    )(mem_len, *pieces, *weights, *kv)


def project_kernel(group, tok_len, *refs):
    att = refs[:8]
    own, oth, direct, crossed = refs[8], refs[9], refs[10:16], refs[16:22]
    x_first, x_last, out = refs[22:]
    me = lax.axis_index("section")
    step = pl.program_id(0)
    half_steps = pl.num_programs(0) // 2
    width = own.shape[0]
    first_row = (me // GROUP) * MB + 2 * (me % GROUP)

    def finish(others):
        total = None
        for k in range(4):
            pair = (own, oth) if k == 0 else (others[k - 1], others[k + 2])
            for n, weight in enumerate(pair):
                rows = jnp.concatenate(
                    [att[j * 4 + k][:, n * width:(n + 1) * width] for j in range(2)], 0
                )
                term = dot(rows, weight[...])
                total = term if total is None else total + term
        row = lax.broadcasted_iota(jnp.int32, (FR, total.shape[1]), 0)
        for j, x_ref in enumerate((x_first, x_last)):
            branch = jnp.where(row < tok_len[first_row + j], total[j * FR:(j + 1) * FR], 0.0)
            out[j * FR:(j + 1) * FR, :] = (x_ref[...].astype(F32) + branch).astype(BF16)

    pl.when(step < half_steps)(lambda: finish(direct))
    pl.when(step >= half_steps)(lambda: finish(crossed))


def project(group, tok_len, att, own, oth, direct, crossed, x_first, x_last):
    width, depth = own.shape
    rows = 2 * FR
    tile = 512
    half = depth // 2 // tile

    def column(i, group):
        return jnp.where(i < half, group[0] * half + i, (1 - group[0]) * half + i - half)

    att_specs = [pl.BlockSpec((FR, 2 * width), lambda i, group: (0, 0))] * 8
    full = pl.BlockSpec((width, tile), lambda i, group: (0, column(i, group)))
    early = pl.BlockSpec((width, tile), lambda i, group: (0, jnp.minimum(i, half - 1)))
    late = pl.BlockSpec((width, tile), lambda i, group: (0, jnp.maximum(i - half, 0)))
    x_specs = [
        pl.BlockSpec((FR, tile), lambda i, group, at=at: (at, column(i, group)))
        for at in (x_first.shape[0] // FR - 1, x_last.shape[0] // FR - 1)
    ]
    return pl.pallas_call(
        project_kernel,
        out_shape=jax.ShapeDtypeStruct((rows, depth), BF16),
        grid_spec=pltpu.PrefetchScalarGridSpec(
            num_scalar_prefetch=1,
            grid=(2 * half,),
            in_specs=[pl.BlockSpec(memory_space=pltpu.SMEM)]
            + att_specs + [full, full] + [early] * 6 + [late] * 6 + x_specs,
            out_specs=pl.BlockSpec((rows, tile), lambda i, group: (0, column(i, group))),
        ),
        compiler_params=pltpu.CompilerParams(
            vmem_limit_bytes=VMEM_BYTES, dimension_semantics=("arbitrary",)
        ),
        cost_estimate=pl.CostEstimate(
            flops=16 * rows * width * depth,
            bytes_accessed=2 * (8 * width * depth + 2 * rows * depth),
            transcendentals=0,
        ),
    )(group, tok_len, *att, own, oth, *direct, *crossed, x_first, x_last)


def shards(arriving, memory, w_query, w_key, w_value, w_out, tok_len, mem_len):
    me = lax.axis_index("section")
    size = lax.axis_size("section")
    group = lax.axis_index("groups")
    depth = arriving.shape[1]
    half_cols = depth // 2
    ring = size == MB and memory.shape[0] == MEMF
    x_first, x_last = arriving[:FR], arriving[FR:]
    half = lax.dynamic_slice_in_dim(w_out, group * half_cols, half_cols, 1)
    key_oth = flip(w_key, CORE)
    value_oth = flip(after(w_value, key_oth), CORE)
    query_oth = flip(after(w_query, value_oth), CORE)
    out_core = flip(after(w_out, query_oth), CORE)
    kv_weights = [w_key, key_oth, w_value, value_oth]
    query_pair = [w_query, query_oth]

    out_near = flip(half, NEAR)
    if ring:
        mem_far = flip(memory, FAR)
        mem_near = flip(memory, NEAR)
        mem_diag = flip(mem_far, NEAR)
        mem_first = [memory, mem_near, mem_far, mem_diag]
        first_hop = hop(jnp.concatenate([memory, x_first], 0))
    else:
        first_hop = hop(x_first)
        gathered = lax.all_gather(memory, "section", axis=0, tiled=True)
        gathered = gathered.reshape(MB // 2, 2, MEMF, depth)
        gathered = lax.dynamic_index_in_dim(gathered, me & 1, 1, keepdims=False)
        mem_first = [gathered[k] for k in range(4)]
        mem_near, mem_far, mem_diag = mem_first[1:]
    out_far = flip(after(half, mem_near, mem_far), FAR)
    cross_near = across(out_near)

    first_hop_ready = after(first_hop, mem_diag, out_core)
    last_hop = hop(after(x_last, first_hop_ready))
    first_far = flip(first_hop_ready, FAR)
    first_near = flip(first_hop_ready, NEAR)
    kv_first = keys_values(mem_first, kv_weights)
    first_diag = flip(after(first_far, kv_first), NEAR)
    out_diag = flip(after(out_near, first_far), FAR)
    first = [first_hop, first_near, first_far, first_diag]
    cross_far = across(after(out_far, cross_near))
    last_far = flip(after(last_hop, first_near), FAR)
    last_near = flip(after(last_hop, first_near), NEAR)
    last_diag = flip(after(last_far, first_diag), NEAR)
    last = [last_hop, last_near, last_far, last_diag]
    cross_diag = across(after(out_diag, cross_far))

    mem_second = first if ring else [gathered[k] for k in range(4, 8)]
    kv_second = keys_values(mem_second, kv_weights)
    kv = [kv_first, kv_second, flip(kv_first, CORE), flip(kv_second, CORE)]

    direct = [out_near, out_far, out_diag]
    crossed = [cross_near, cross_far, cross_diag]
    direct = direct + [flip(part, CORE) for part in direct]
    crossed = crossed + [flip(part, CORE) for part in crossed]

    att = []
    for j, rows in enumerate((first, last)):
        got = attend(j, ring, mem_len, rows, query_pair, kv)
        att += [got[0]] + [flip(got[k], CHIPS[k]) for k in range(1, 4)]

    limits = tok_len
    return project(
        group.astype(jnp.int32).reshape(1), limits, att, w_out, out_core, direct, crossed, first[0], last[0]
    )


def solution(mesh):
    return jax.shard_map(
        shards,
        mesh=mesh,
        in_specs=(
            P(("groups", "section"), None),
            P(("groups", "section"), None),
            P(None, "section"),
            P(None, "section"),
            P(None, "section"),
            P("section", None),
            P("groups"),
            P("groups"),
        ),
        out_specs=P(("groups", "section"), None),
        check_vma=False,
    )
```

time: 258 us -> 207 us (0.80)
  starting transfers between devices: 75.6 us -> 39.4 us
  local copies, waits for them, and re-layouts: 17.2 us -> 2.41 us
  waiting for transfers between devices: 129 us -> 135 us
  other arithmetic: 3.85 us -> 0.09 us
    ppermute x33 -> x30, waiting for transfers between devices: 63.5 us -> 128 us  [flip(): return lax.ppermute(value, 'section', [(i, i ^ bits) for i in range(size)])]
    ppermute x33 -> x30, starting transfers between devices: 63.8 us -> 29.5 us  [flip(): return lax.ppermute(value, 'section', [(i, i ^ bits) for i in range(size)])]
    ppermute x3, waiting for transfers between devices: 29.8 us -> 0.01 us  [across(): return lax.ppermute(value, 'groups', [(0, 1), (1, 0)])]
    ppermute x3 -> x2, waiting for transfers between devices: 36.3 us -> 6.54 us  [hop(): lax.ppermute(value, 'section', [(i, (i + GROUP) % size) for i in range(si...]
    unnamed x61 -> x22, local copies, waits for them, and re-layouts: 8.08 us -> 0.96 us
    another operation x2 -> x0, local copies, waits for them, and re-layouts: 5.06 us -> none  [shards(): jnp.stack([is_own.astype(jnp.int32)] + [place(utt) for utt in utts] + [me...]
    ppermute x3 -> x2, starting transfers between devices: 7.03 us -> 5.39 us  [hop(): lax.ppermute(value, 'section', [(i, (i + GROUP) % size) for i in range(si...]
  transfers between devices with their start and end apart: 39 -> 35, of which waited for: 16 -> 14; matrix products, arithmetic and copies ran while one was open for 5% -> 1% of each run, Pallas kernels for 8% -> 10%
where the time goes in v2:
time: 207 us
  waiting for transfers between devices  135 us (65%)
  starting transfers between devices  39.4 us (19%)
  Pallas kernels  29.9 us (14%)
  local copies, waits for them, and re-layouts  2.41 us (1%)
    ppermute x30, waiting for transfers between devices, flip(): return lax.ppermute(value, 'section', [(i, i ^ bits) for i in range(size)])  128 us
    ppermute x30, starting transfers between devices, flip(): return lax.ppermute(value, 'section', [(i, i ^ bits) for i in range(size)])  29.5 us
    pallas_call x2, Pallas kernels, keys_values(): pl.pallas_call(keys_values_kernel, out_shape=jax.ShapeDtypeStruct((rows,...  11 us
    pallas_call x1, Pallas kernels, project(): pl.pallas_call(project_kernel, out_shape=jax.ShapeDtypeStruct((rows, dept...  9.68 us
    pallas_call x2, Pallas kernels, attend(): pl.pallas_call(functools.partial(attend_kernel, j, ring), out_shape=[jax....  9.25 us
    ppermute x2, waiting for transfers between devices, hop(): lax.ppermute(value, 'section', [(i, (i + GROUP) % size) for i in range(si...  6.54 us
    ppermute x2, starting transfers between devices, hop(): lax.ppermute(value, 'section', [(i, (i + GROUP) % size) for i in range(si...  5.39 us
    ppermute x3, starting transfers between devices, across(): return lax.ppermute(value, 'groups', [(0, 1), (1, 0)])  4.58 us
  transfers between devices with their start and end apart: 35, of which 14 were waited for; matrix products, arithmetic and copies ran while one was open for 1% of the time, Pallas kernels for 10%

profile of v2, /device:TPU:0, one launch (start us, length us, event | category | flops | bytes accessed | tf_op | source)
XLA Modules:
  0.0 206.8 jit_solution(4986866839987384161)
XLA Ops:
  0.5 4.1 %collective-permute-done.3.refs_5_ = bf16[4096,256]{1,0:T(8,128)(2,1)} collective-permute-done((bf16[4096,256]{1,0:T(8,128)(2,1)}, bf16[4096,256]{1,0:T(8,128)(2,1)}, u32[]{:S(2)}, u32[]{:S(2)}) %collective-permute-start.3) | collective-permute-done | bytes 2097184 | tf_op jit(solution)/shard_map/ppermute | solution.py:27
  5.0 4.1 %collective-permute-done.4.refs_7_ = bf16[4096,256]{1,0:T(8,128)(2,1)} collective-permute-done((bf16[4096,256]{1,0:T(8,128)(2,1)}, bf16[4096,256]{1,0:T(8,128)(2,1)}, u32[]{:S(2)}, u32[]{:S(2)}) %collective-permute-start.4) | collective-permute-done | bytes 2097184 | tf_op jit(solution)/shard_map/ppermute | solution.py:27
  10.9 2.7 %collective-permute-start.23 = (bf16[256,2048]{1,0:T(8,128)(2,1)S(1)}, bf16[256,2048]{1,0:T(8,128)(2,1)S(1)}, u32[]{:S(2)}, u32[]{:S(2)}) collective-permute-start(bf16[256,2048]{1,0:T(8,128)(2,1)S(1)} %constant_dynamic-slice_fusion), channel_id=1, source_target_pairs={{0,2},{1,3},{2,0},{3,1},{4,6},{5,7},{6,4},{7,5},{8,10},{9,11},{10,... | collective-permute-start | bytes 3145736 | tf_op jit(solution)/shard_map/ppermute | solution.py:27
  14.9 3.8 %collective-permute-start = (bf16[128,4096]{1,0:T(8,128)(2,1)S(1)}, bf16[128,4096]{1,0:T(8,128)(2,1)S(1)}, u32[]{:S(2)}, u32[]{:S(2)}) collective-permute-start(bf16[128,4096]{1,0:T(8,128)(2,1)S(1)} %pad_maximum_fusion), channel_id=1, source_target_pairs={{0,8},{1,9},{2,10},{3,11},{4,12},{5,13},{6,14},{7,15},{8,0},{9,1},... | collective-permute-start | bytes 3145736 | tf_op jit(solution)/shard_map/ppermute | solution.py:32
  18.8 1.6 collective-permute-start.1
  20.3 1.5 collective-permute-start.9
  21.9 30.9 %collective-permute-done.1.refs_2_ = bf16[64,4096]{1,0:T(8,128)(2,1)S(1)} collective-permute-done((bf16[64,4096]{1,0:T(8,128)(2,1)S(1)}, bf16[64,4096]{1,0:T(8,128)(2,1)S(1)}, u32[]{:S(2)}, u32[]{:S(2)}) %collective-permute-start.1) | collective-permute-done | bytes 524320 | tf_op jit(solution)/shard_map/ppermute | solution.py:27
  52.8 1.5 collective-permute-start.2
  54.3 2.5 %collective-permute-start.24 = (bf16[256,2048]{1,0:T(8,128)(2,1)S(1)}, bf16[256,2048]{1,0:T(8,128)(2,1)S(1)}, u32[]{:S(2)}, u32[]{:S(2)}) collective-permute-start(bf16[256,2048]{1,0:T(8,128)(2,1)S(1)} %constant_dynamic-slice_fusion), channel_id=1, source_target_pairs={{0,4},{1,5},{2,6},{3,7},{4,0},{5,1},{6,2},{7,3},{8,12},{9,13},{10,... | collective-permute-start | bytes 3145736 | tf_op jit(solution)/shard_map/ppermute | solution.py:27
  58.3 6.5 %collective-permute-done.refs_0_.refs_1_.refs_22_ = bf16[128,4096]{1,0:T(8,128)(2,1)S(1)} collective-permute-done((bf16[128,4096]{1,0:T(8,128)(2,1)S(1)}, bf16[128,4096]{1,0:T(8,128)(2,1)S(1)}, u32[]{:S(2)}, u32[]{:S(2)}) %collective-permute-start) | collective-permute-done | bytes 1048608 | tf_op jit(solution)/shard_map/ppermute | solution.py:32
  65.9 2.5 %collective-permute-start.8 = (bf16[128,4096]{1,0:T(8,128)(2,1)S(1)}, bf16[128,4096]{1,0:T(8,128)(2,1)S(1)}, u32[]{:S(2)}, u32[]{:S(2)}) collective-permute-start(bf16[128,4096]{1,0:T(8,128)(2,1)S(1)} %collective-permute-done.refs_0_.refs_1_.refs_22_), channel_id=1, source_target_pairs={{0,4},{1,5},{2,6},{3,7},{4,0},{5,1},{6,2},{7,3},{8,12},{9,13},{10,... | collective-permute-start | bytes 3145736 | tf_op jit(solution)/shard_map/ppermute | solution.py:27
  69.9 17.3 %collective-permute-done.24.refs_11_ = bf16[256,2048]{1,0:T(8,128)(2,1)S(1)} collective-permute-done((bf16[256,2048]{1,0:T(8,128)(2,1)S(1)}, bf16[256,2048]{1,0:T(8,128)(2,1)S(1)}, u32[]{:S(2)}, u32[]{:S(2)}) %collective-permute-start.24) | collective-permute-done | bytes 1048608 | tf_op jit(solution)/shard_map/ppermute | solution.py:27
  87.3 1.5 collective-permute-start.30
  88.8 1.6 collective-permute-start.16
  90.4 30.5 %collective-permute-done.8.refs_2_.refs_3_ = bf16[128,4096]{1,0:T(8,128)(2,1)S(1)} collective-permute-done((bf16[128,4096]{1,0:T(8,128)(2,1)S(1)}, bf16[128,4096]{1,0:T(8,128)(2,1)S(1)}, u32[]{:S(2)}, u32[]{:S(2)}) %collective-permute-start.8) | collective-permute-done | bytes 1048608 | tf_op jit(solution)/shard_map/ppermute | solution.py:27
  120.9 5.2 %shard_map.82.refs_7_ = bf16[256,1024]{1,0:T(8,128)(2,1)S(1)} custom-call(bf16[64,4096]{1,0:T(8,128)(2,1)S(1)} %copy-done.3, bf16[64,4096]{1,0:T(8,128)(2,1)S(1)} %collective-permute-done.9.refs_1_, bf16[64,4096]{1,0:T(8,128)(2,1)S(1)} %collective-permute-done.1.refs_2_, bf16[64,4096]{1,0:T(8,128)(2,1)S(1)} %collective-permute-done.2.refs_3_, ...), custom_call_target="tpu_custom_call" | custom-call | flops 2147483648 | bytes 11010048 | tf_op jit(solution)/shard_map/pallas_call | solution.py:63
  126.1 1.6 collective-permute-start.10
  127.7 2.1 %collective-permute-start.18 = (bf16[64,4096]{1,0:T(8,128)(2,1)S(1)}, bf16[64,4096]{1,0:T(8,128)(2,1)S(1)}, u32[]{:S(2)}, u32[]{:S(2)}) collective-permute-start(bf16[64,4096]{1,0:T(8,128)(2,1)S(1)} %collective-permute-done.16.refs_1_.refs_23_), channel_id=1, source_target_pairs={{0,4},{1,5},{2,6},{3,7},{4,0},{5,1},{6,2},{7,3},{8,12},{9,13},{10,... | collective-permute-start | bytes 1572872 | tf_op jit(solution)/shard_map/ppermute | solution.py:27
  129.8 17.0 %collective-permute-done.25.refs_12_ = bf16[256,2048]{1,0:T(8,128)(2,1)S(1)} collective-permute-done((bf16[256,2048]{1,0:T(8,128)(2,1)S(1)}, bf16[256,2048]{1,0:T(8,128)(2,1)S(1)}, u32[]{:S(2)}, u32[]{:S(2)}) %collective-permute-start.25) | collective-permute-done | bytes 1048608 | tf_op jit(solution)/shard_map/ppermute | solution.py:27
  146.9 1.5 collective-permute-start.31
  148.4 2.8 %collective-permute-done.10.refs_3_.refs_4_ = bf16[128,4096]{1,0:T(8,128)(2,1)S(1)} collective-permute-done((bf16[128,4096]{1,0:T(8,128)(2,1)S(1)}, bf16[128,4096]{1,0:T(8,128)(2,1)S(1)}, u32[]{:S(2)}, u32[]{:S(2)}) %collective-permute-start.10) | collective-permute-done | bytes 1048608 | tf_op jit(solution)/shard_map/ppermute | solution.py:27
  151.2 1.6 collective-permute-start.17
  152.8 5.8 %shard_map.83.refs_8_ = bf16[256,1024]{1,0:T(8,128)(2,1)S(1)} custom-call(bf16[128,4096]{1,0:T(8,128)(2,1)S(1)} %collective-permute-done.refs_0_.refs_1_.refs_22_, bf16[128,4096]{1,0:T(8,128)(2,1)S(1)} %collective-permute-done.7.refs_1_.refs_2_, bf16[128,4096]{1,0:T(8,128)(2,1)S(1)} %collective-permute-done.8.refs_2_.refs_3_, ...), custom_call_target="tpu_custom_call" | custom-call | flops 2147483648 | bytes 11010048 | tf_op jit(solution)/shard_map/pallas_call | solution.py:63
  159.4 6.7 %collective-permute-done.17.refs_2_ = bf16[64,4096]{1,0:T(8,128)(2,1)S(1)} collective-permute-done((bf16[64,4096]{1,0:T(8,128)(2,1)S(1)}, bf16[64,4096]{1,0:T(8,128)(2,1)S(1)}, u32[]{:S(2)}, u32[]{:S(2)}) %collective-permute-start.17) | collective-permute-done | bytes 524320 | tf_op jit(solution)/shard_map/ppermute | solution.py:27
  166.6 8.9 %collective-permute-done.19.refs_4_ = bf16[64,4096]{1,0:T(8,128)(2,1)S(1)} collective-permute-done((bf16[64,4096]{1,0:T(8,128)(2,1)S(1)}, bf16[64,4096]{1,0:T(8,128)(2,1)S(1)}, u32[]{:S(2)}, u32[]{:S(2)}) %collective-permute-start.19) | collective-permute-done | bytes 524320 | tf_op jit(solution)/shard_map/ppermute | solution.py:27
  176.0 4.5 %shard_map.85 = (bf16[64,512]{1,0:T(8,128)(2,1)S(1)}, bf16[64,512]{1,0:T(8,128)(2,1)S(1)}, bf16[64,512]{1,0:T(8,128)(2,1)S(1)}, bf16[64,512]{1,0:T(8,128)(2,1)S(1)}) custom-call(s32[16]{0:T(128)S(1)} %copy-done.4, bf16[64,4096]{1,0:T(8,128)(2,1)S(1)} %collective-permute-done.16.refs_1_.refs_23_, bf16[64,4096]{1,0:T(8,128)(2,1)S(1)} %collective-permute-done.17.refs_2_, ...), custom_call_target="tpu_custom_call" | custom-call | flops 1073741824 | bytes 8388608 | tf_op jit(solution)/shard_map/pallas_call | solution.py:131
  180.5 1.7 collective-permute-start.20
  184.1 4.8 %shard_map.84 = (bf16[64,512]{1,0:T(8,128)(2,1)S(1)}, bf16[64,512]{1,0:T(8,128)(2,1)S(1)}, bf16[64,512]{1,0:T(8,128)(2,1)S(1)}, bf16[64,512]{1,0:T(8,128)(2,1)S(1)}) custom-call(s32[16]{0:T(128)S(1)} %copy-done.4, bf16[128,4096]{1,0:T(8,128)(2,1)S(1)} %collective-permute-done.refs_0_.refs_1_.refs_22_, ...), custom_call_target="tpu_custom_call" | custom-call | flops 1073741824 | bytes 8388608 | tf_op jit(solution)/shard_map/pallas_call | solution.py:131
  188.9 1.6 collective-permute-start.13
  193.2 1.6 collective-permute-done.14.refs_2_
  194.8 2.3 %collective-permute-done.15.refs_3_ = bf16[64,512]{1,0:T(8,128)(2,1)S(1)} collective-permute-done((bf16[64,512]{1,0:T(8,128)(2,1)S(1)}, bf16[64,512]{1,0:T(8,128)(2,1)S(1)}, u32[]{:S(2)}, u32[]{:S(2)}) %collective-permute-start.15) | collective-permute-done | bytes 65568 | tf_op jit(solution)/shard_map/ppermute | solution.py:27
  197.1 9.7 %shard_map.86 = bf16[128,4096]{1,0:T(8,128)(2,1)} custom-call(s32[1]{0:T(128)} %bitcast.group, s32[32]{0:T(128)S(1)} %copy-done.5, bf16[64,512]{1,0:T(8,128)(2,1)S(1)} %get-tuple-element.30.refs_0_, bf16[64,512]{1,0:T(8,128)(2,1)S(1)} %collective-permute-done.13.refs_1_, bf16[64,512]{1,0:T(8,128)(2,1)S(1)} %collective-permute-done.14.refs_2_, ...), custom_call_target="tpu_custom_call" | custom-call | flops 2147483648 | bytes 18874368 | tf_op jit(solution)/shard_map/pallas_call | solution.py:192
  (68 shorter events, 14.5 us)
Async XLA Ops:
  0.0 4.6 %collective-permute-start.3 = (bf16[4096,256]{1,0:T(8,128)(2,1)}, bf16[4096,256]{1,0:T(8,128)(2,1)}, u32[]{:S(2)}, u32[]{:S(2)}) collective-permute-start(bf16[4096,256]{1,0:T(8,128)(2,1)} %refs_4_.3), channel_id=1, source_target_pairs={{0,1},{1,0},{2,3},{3,2},{4,5},{5,4},{6,7},{7,6},{8,9},{9,8},{10,11... | collective-permute-start | bytes 6291464 | tf_op jit(solution)/shard_map/ppermute | solution.py:27
  9.1 4.5 %collective-permute-start.5 = (bf16[4096,256]{1,0:T(8,128)(2,1)}, bf16[4096,256]{1,0:T(8,128)(2,1)S(1)}, u32[]{:S(2)}, u32[]{:S(2)}) collective-permute-start(bf16[4096,256]{1,0:T(8,128)(2,1)} %refs_5_.3), channel_id=1, source_target_pairs={{0,1},{1,0},{2,3},{3,2},{4,5},{5,4},{6,7},{7,6},{8,9},{9,8},{10,11... | collective-permute-start | bytes 6291464 | tf_op jit(solution)/shard_map/ppermute | solution.py:27
  10.9 45.9 %collective-permute-start.23 = (bf16[256,2048]{1,0:T(8,128)(2,1)S(1)}, bf16[256,2048]{1,0:T(8,128)(2,1)S(1)}, u32[]{:S(2)}, u32[]{:S(2)}) collective-permute-start(bf16[256,2048]{1,0:T(8,128)(2,1)S(1)} %constant_dynamic-slice_fusion), channel_id=1, source_target_pairs={{0,2},{1,3},{2,0},{3,1},{4,6},{5,7},{6,4},{7,5},{8,10},{9,11},{10,... | collective-permute-start | bytes 3145736 | tf_op jit(solution)/shard_map/ppermute | solution.py:27
  13.6 52.3 %collective-permute-start.6 = (bf16[256,4096]{1,0:T(8,128)(2,1)}, bf16[256,4096]{1,0:T(8,128)(2,1)S(1)}, u32[]{:S(2)}, u32[]{:S(2)}) collective-permute-start(bf16[256,4096]{1,0:T(8,128)(2,1)} %refs_8_.1), channel_id=1, source_target_pairs={{0,1},{1,0},{2,3},{3,2},{4,5},{5,4},{6,7},{7,6},{8,9},{9,8},{10,11... | collective-permute-start | bytes 6291464 | tf_op jit(solution)/shard_map/ppermute | solution.py:27
  14.9 49.8 %collective-permute-start = (bf16[128,4096]{1,0:T(8,128)(2,1)S(1)}, bf16[128,4096]{1,0:T(8,128)(2,1)S(1)}, u32[]{:S(2)}, u32[]{:S(2)}) collective-permute-start(bf16[128,4096]{1,0:T(8,128)(2,1)S(1)} %pad_maximum_fusion), channel_id=1, source_target_pairs={{0,8},{1,9},{2,10},{3,11},{4,12},{5,13},{6,14},{7,15},{8,0},{9,1},... | collective-permute-start | bytes 3145736 | tf_op jit(solution)/shard_map/ppermute | solution.py:32
  18.8 34.0 %collective-permute-start.1 = (bf16[64,4096]{1,0:T(8,128)(2,1)S(1)}, bf16[64,4096]{1,0:T(8,128)(2,1)S(1)}, u32[]{:S(2)}, u32[]{:S(2)}) collective-permute-start(bf16[64,4096]{1,0:T(8,128)(2,1)S(1)} %copy-done.3), channel_id=1, source_target_pairs={{0,4},{1,5},{2,6},{3,7},{4,0},{5,1},{6,2},{7,3},{8,12},{9,13},{10,... | collective-permute-start | bytes 1572872 | tf_op jit(solution)/shard_map/ppermute | solution.py:27
  20.3 33.9 %collective-permute-start.9 = (bf16[64,4096]{1,0:T(8,128)(2,1)S(1)}, bf16[64,4096]{1,0:T(8,128)(2,1)S(1)}, u32[]{:S(2)}, u32[]{:S(2)}) collective-permute-start(bf16[64,4096]{1,0:T(8,128)(2,1)S(1)} %copy-done.3), channel_id=1, source_target_pairs={{0,2},{1,3},{2,0},{3,1},{4,6},{5,7},{6,4},{7,5},{8,10},{9,11},{10,... | collective-permute-start | bytes 1572872 | tf_op jit(solution)/shard_map/ppermute | solution.py:27
  52.8 13.1 %collective-permute-start.2 = (bf16[64,4096]{1,0:T(8,128)(2,1)S(1)}, bf16[64,4096]{1,0:T(8,128)(2,1)S(1)}, u32[]{:S(2)}, u32[]{:S(2)}) collective-permute-start(bf16[64,4096]{1,0:T(8,128)(2,1)S(1)} %collective-permute-done.1.refs_2_), channel_id=1, source_target_pairs={{0,2},{1,3},{2,0},{3,1},{4,6},{5,7},{6,4},{7,5},{8,10},{9,11},{10,... | collective-permute-start | bytes 1572872 | tf_op jit(solution)/shard_map/ppermute | solution.py:27
  54.3 33.0 %collective-permute-start.24 = (bf16[256,2048]{1,0:T(8,128)(2,1)S(1)}, bf16[256,2048]{1,0:T(8,128)(2,1)S(1)}, u32[]{:S(2)}, u32[]{:S(2)}) collective-permute-start(bf16[256,2048]{1,0:T(8,128)(2,1)S(1)} %constant_dynamic-slice_fusion), channel_id=1, source_target_pairs={{0,4},{1,5},{2,6},{3,7},{4,0},{5,1},{6,2},{7,3},{8,12},{9,13},{10,... | collective-permute-start | bytes 3145736 | tf_op jit(solution)/shard_map/ppermute | solution.py:27
  56.8 30.5 %collective-permute-start.29 = (bf16[256,2048]{1,0:T(8,128)(2,1)S(1)}, bf16[256,2048]{1,0:T(8,128)(2,1)S(1)}, u32[]{:S(2)}, u32[]{:S(2)}) collective-permute-start(bf16[256,2048]{1,0:T(8,128)(2,1)S(1)} %collective-permute-done.23.refs_10_), channel_id=1, source_target_pairs={{0,16},{16,0},{1,17},{17,1},{2,18},{18,2},{3,19},{19,3},{4,20},{20... | collective-permute-start | bytes 3145736 | tf_op jit(solution)/shard_map/ppermute | solution.py:40
  65.9 55.0 %collective-permute-start.8 = (bf16[128,4096]{1,0:T(8,128)(2,1)S(1)}, bf16[128,4096]{1,0:T(8,128)(2,1)S(1)}, u32[]{:S(2)}, u32[]{:S(2)}) collective-permute-start(bf16[128,4096]{1,0:T(8,128)(2,1)S(1)} %collective-permute-done.refs_0_.refs_1_.refs_22_), channel_id=1, source_target_pairs={{0,4},{1,5},{2,6},{3,7},{4,0},{5,1},{6,2},{7,3},{8,12},{9,13},{10,... | collective-permute-start | bytes 3145736 | tf_op jit(solution)/shard_map/ppermute | solution.py:27
  68.4 59.4 %collective-permute-start.7 = (bf16[128,4096]{1,0:T(8,128)(2,1)S(1)}, bf16[128,4096]{1,0:T(8,128)(2,1)S(1)}, u32[]{:S(2)}, u32[]{:S(2)}) collective-permute-start(bf16[128,4096]{1,0:T(8,128)(2,1)S(1)} %collective-permute-done.refs_0_.refs_1_.refs_22_), channel_id=1, source_target_pairs={{0,2},{1,3},{2,0},{3,1},{4,6},{5,7},{6,4},{7,5},{8,10},{9,11},{10,... | collective-permute-start | bytes 3145736 | tf_op jit(solution)/shard_map/ppermute | solution.py:27
  87.3 42.6 %collective-permute-start.30 = (bf16[256,2048]{1,0:T(8,128)(2,1)S(1)}, bf16[256,2048]{1,0:T(8,128)(2,1)}, u32[]{:S(2)}, u32[]{:S(2)}) collective-permute-start(bf16[256,2048]{1,0:T(8,128)(2,1)S(1)} %collective-permute-done.24.refs_11_), channel_id=1, source_target_pairs={{0,16},{16,0},{1,17},{17,1},{2,18},{18,2},{3,19},{19,3},{4,20},{20... | collective-permute-start | bytes 3145736 | tf_op jit(solution)/shard_map/ppermute | solution.py:40
  88.8 38.9 %collective-permute-start.16 = (bf16[64,4096]{1,0:T(8,128)(2,1)S(1)}, bf16[64,4096]{1,0:T(8,128)(2,1)S(1)}, u32[]{:S(2)}, u32[]{:S(2)}) collective-permute-start(bf16[64,4096]{1,0:T(8,128)(2,1)S(1)} %get-tuple-element.34), channel_id=1, source_target_pairs={{0,8},{1,9},{2,10},{3,11},{4,12},{5,13},{6,14},{7,15},{8,0},{9,1},... | collective-permute-start | bytes 1572872 | tf_op jit(solution)/shard_map/ppermute | solution.py:32
  120.9 26.0 %collective-permute-start.25 = (bf16[256,2048]{1,0:T(8,128)(2,1)S(1)}, bf16[256,2048]{1,0:T(8,128)(2,1)S(1)}, u32[]{:S(2)}, u32[]{:S(2)}) collective-permute-start(bf16[256,2048]{1,0:T(8,128)(2,1)S(1)} %collective-permute-done.23.refs_10_), channel_id=1, source_target_pairs={{0,4},{1,5},{2,6},{3,7},{4,0},{5,1},{6,2},{7,3},{8,12},{9,13},{10,... | collective-permute-start | bytes 3145736 | tf_op jit(solution)/shard_map/ppermute | solution.py:27
  126.1 25.1 %collective-permute-start.10 = (bf16[128,4096]{1,0:T(8,128)(2,1)S(1)}, bf16[128,4096]{1,0:T(8,128)(2,1)S(1)}, u32[]{:S(2)}, u32[]{:S(2)}) collective-permute-start(bf16[128,4096]{1,0:T(8,128)(2,1)S(1)} %collective-permute-done.8.refs_2_.refs_3_), channel_id=1, source_target_pairs={{0,2},{1,3},{2,0},{3,1},{4,6},{5,7},{6,4},{7,5},{8,10},{9,11},{10,... | collective-permute-start | bytes 3145736 | tf_op jit(solution)/shard_map/ppermute | solution.py:27
  127.7 31.0 %collective-permute-start.26 = (bf16[256,2048]{1,0:T(8,128)(2,1)S(1)}, bf16[256,2048]{1,0:T(8,128)(2,1)S(1)}, u32[]{:S(2)}, u32[]{:S(2)}) collective-permute-start(bf16[256,2048]{1,0:T(8,128)(2,1)S(1)} %collective-permute-done.23.refs_10_), channel_id=1, source_target_pairs={{0,1},{1,0},{2,3},{3,2},{4,5},{5,4},{6,7},{7,6},{8,9},{9,8},{10,11... | collective-permute-start | bytes 3145736 | tf_op jit(solution)/shard_map/ppermute | solution.py:27
  127.7 30.9 %collective-permute-start.18 = (bf16[64,4096]{1,0:T(8,128)(2,1)S(1)}, bf16[64,4096]{1,0:T(8,128)(2,1)S(1)}, u32[]{:S(2)}, u32[]{:S(2)}) collective-permute-start(bf16[64,4096]{1,0:T(8,128)(2,1)S(1)} %collective-permute-done.16.refs_1_.refs_23_), channel_id=1, source_target_pairs={{0,4},{1,5},{2,6},{3,7},{4,0},{5,1},{6,2},{7,3},{8,12},{9,13},{10,... | collective-permute-start | bytes 1572872 | tf_op jit(solution)/shard_map/ppermute | solution.py:27
  146.9 28.6 %collective-permute-start.31 = (bf16[256,2048]{1,0:T(8,128)(2,1)S(1)}, bf16[256,2048]{1,0:T(8,128)(2,1)S(1)}, u32[]{:S(2)}, u32[]{:S(2)}) collective-permute-start(bf16[256,2048]{1,0:T(8,128)(2,1)S(1)} %collective-permute-done.25.refs_12_), channel_id=1, source_target_pairs={{0,16},{16,0},{1,17},{17,1},{2,18},{18,2},{3,19},{19,3},{4,20},{20... | collective-permute-start | bytes 3145736 | tf_op jit(solution)/shard_map/ppermute | solution.py:40
  148.4 10.8 %collective-permute-start.11 = (bf16[256,1024]{1,0:T(8,128)(2,1)S(1)}, bf16[256,1024]{1,0:T(8,128)(2,1)S(1)}, u32[]{:S(2)}, u32[]{:S(2)}) collective-permute-start(bf16[256,1024]{1,0:T(8,128)(2,1)S(1)} %shard_map.82.refs_7_), channel_id=1, source_target_pairs={{0,1},{1,0},{2,3},{3,2},{4,5},{5,4},{6,7},{7,6},{8,9},{9,8},{10,11... | collective-permute-start | bytes 1572872 | tf_op jit(solution)/shard_map/ppermute | solution.py:27
  151.2 14.9 %collective-permute-start.17 = (bf16[64,4096]{1,0:T(8,128)(2,1)S(1)}, bf16[64,4096]{1,0:T(8,128)(2,1)S(1)}, u32[]{:S(2)}, u32[]{:S(2)}) collective-permute-start(bf16[64,4096]{1,0:T(8,128)(2,1)S(1)} %collective-permute-done.16.refs_1_.refs_23_), channel_id=1, source_target_pairs={{0,2},{1,3},{2,0},{3,1},{4,6},{5,7},{6,4},{7,5},{8,10},{9,11},{10,... | collective-permute-start | bytes 1572872 | tf_op jit(solution)/shard_map/ppermute | solution.py:27
  158.7 7.5 %collective-permute-start.12 = (bf16[256,1024]{1,0:T(8,128)(2,1)S(1)}, bf16[256,1024]{1,0:T(8,128)(2,1)S(1)}, u32[]{:S(2)}, u32[]{:S(2)}) collective-permute-start(bf16[256,1024]{1,0:T(8,128)(2,1)S(1)} %shard_map.83.refs_8_), channel_id=1, source_target_pairs={{0,1},{1,0},{2,3},{3,2},{4,5},{5,4},{6,7},{7,6},{8,9},{9,8},{10,11... | collective-permute-start | bytes 1572872 | tf_op jit(solution)/shard_map/ppermute | solution.py:27
  158.8 16.7 %collective-permute-start.19 = (bf16[64,4096]{1,0:T(8,128)(2,1)S(1)}, bf16[64,4096]{1,0:T(8,128)(2,1)S(1)}, u32[]{:S(2)}, u32[]{:S(2)}) collective-permute-start(bf16[64,4096]{1,0:T(8,128)(2,1)S(1)} %collective-permute-done.18.refs_3_), channel_id=1, source_target_pairs={{0,2},{1,3},{2,0},{3,1},{4,6},{5,7},{6,4},{7,5},{8,10},{9,11},{10,... | collective-permute-start | bytes 1572872 | tf_op jit(solution)/shard_map/ppermute | solution.py:27
  159.3 21.2 %collective-permute-start.27 = (bf16[256,2048]{1,0:T(8,128)(2,1)S(1)}, bf16[256,2048]{1,0:T(8,128)(2,1)}, u32[]{:S(2)}, u32[]{:S(2)}) collective-permute-start(bf16[256,2048]{1,0:T(8,128)(2,1)S(1)} %collective-permute-done.24.refs_11_), channel_id=1, source_target_pairs={{0,1},{1,0},{2,3},{3,2},{4,5},{5,4},{6,7},{7,6},{8,9},{9,8},{10,11... | collective-permute-start | bytes 3145736 | tf_op jit(solution)/shard_map/ppermute | solution.py:27
  166.1 16.1 %collective-permute-start.32 = (bf16[256,2048]{1,0:T(8,128)(2,1)S(1)}, bf16[256,2048]{1,0:T(8,128)(2,1)}, u32[]{:S(2)}, u32[]{:S(2)}) collective-permute-start(bf16[256,2048]{1,0:T(8,128)(2,1)S(1)} %collective-permute-done.29.refs_16_), channel_id=1, source_target_pairs={{0,1},{1,0},{2,3},{3,2},{4,5},{5,4},{6,7},{7,6},{8,9},{9,8},{10,11... | collective-permute-start | bytes 3145736 | tf_op jit(solution)/shard_map/ppermute | solution.py:27
  166.1 17.5 %collective-permute-start.33 = (bf16[256,2048]{1,0:T(8,128)(2,1)}, bf16[256,2048]{1,0:T(8,128)(2,1)}, u32[]{:S(2)}, u32[]{:S(2)}) collective-permute-start(bf16[256,2048]{1,0:T(8,128)(2,1)} %collective-permute-done.30.refs_17_), channel_id=1, source_target_pairs={{0,1},{1,0},{2,3},{3,2},{4,5},{5,4},{6,7},{7,6},{8,9},{9,8},{10,11... | collective-permute-start | bytes 3145736 | tf_op jit(solution)/shard_map/ppermute | solution.py:27
  175.5 21.6 %collective-permute-start.28 = (bf16[256,2048]{1,0:T(8,128)(2,1)S(1)}, bf16[256,2048]{1,0:T(8,128)(2,1)}, u32[]{:S(2)}, u32[]{:S(2)}) collective-permute-start(bf16[256,2048]{1,0:T(8,128)(2,1)S(1)} %collective-permute-done.25.refs_12_), channel_id=1, source_target_pairs={{0,1},{1,0},{2,3},{3,2},{4,5},{5,4},{6,7},{7,6},{8,9},{9,8},{10,11... | collective-permute-start | bytes 3145736 | tf_op jit(solution)/shard_map/ppermute | solution.py:27
  175.5 21.6 %collective-permute-start.34 = (bf16[256,2048]{1,0:T(8,128)(2,1)S(1)}, bf16[256,2048]{1,0:T(8,128)(2,1)}, u32[]{:S(2)}, u32[]{:S(2)}) collective-permute-start(bf16[256,2048]{1,0:T(8,128)(2,1)S(1)} %collective-permute-done.31.refs_18_), channel_id=1, source_target_pairs={{0,1},{1,0},{2,3},{3,2},{4,5},{5,4},{6,7},{7,6},{8,9},{9,8},{10,11... | collective-permute-start | bytes 3145736 | tf_op jit(solution)/shard_map/ppermute | solution.py:27
  180.5 8.4 %collective-permute-start.20 = (bf16[64,512]{1,0:T(8,128)(2,1)S(1)}, bf16[64,512]{1,0:T(8,128)(2,1)S(1)}, u32[]{:S(2)}, u32[]{:S(2)}) collective-permute-start(bf16[64,512]{1,0:T(8,128)(2,1)S(1)} %get-tuple-element.38), channel_id=1, source_target_pairs={{0,2},{1,3},{2,0},{3,1},{4,6},{5,7},{6,4},{7,5},{8,10},{9,11},{10,... | collective-permute-start | bytes 196616 | tf_op jit(solution)/shard_map/ppermute | solution.py:27
  182.2 8.4 %collective-permute-start.21 = (bf16[64,512]{1,0:T(8,128)(2,1)S(1)}, bf16[64,512]{1,0:T(8,128)(2,1)S(1)}, u32[]{:S(2)}, u32[]{:S(2)}) collective-permute-start(bf16[64,512]{1,0:T(8,128)(2,1)S(1)} %get-tuple-element.39), channel_id=1, source_target_pairs={{0,4},{1,5},{2,6},{3,7},{4,0},{5,1},{6,2},{7,3},{8,12},{9,13},{10,... | collective-permute-start | bytes 196616 | tf_op jit(solution)/shard_map/ppermute | solution.py:27
  183.6 8.4 %collective-permute-start.22 = (bf16[64,512]{1,0:T(8,128)(2,1)S(1)}, bf16[64,512]{1,0:T(8,128)(2,1)S(1)}, u32[]{:S(2)}, u32[]{:S(2)}) collective-permute-start(bf16[64,512]{1,0:T(8,128)(2,1)S(1)} %get-tuple-element.40), channel_id=1, source_target_pairs={{0,6},{1,7},{2,4},{3,5},{4,2},{5,3},{6,0},{7,1},{8,14},{9,15},{10,... | collective-permute-start | bytes 196616 | tf_op jit(solution)/shard_map/ppermute | solution.py:27
  191.9 5.2 %collective-permute-start.15 = (bf16[64,512]{1,0:T(8,128)(2,1)S(1)}, bf16[64,512]{1,0:T(8,128)(2,1)S(1)}, u32[]{:S(2)}, u32[]{:S(2)}) collective-permute-start(bf16[64,512]{1,0:T(8,128)(2,1)S(1)} %get-tuple-element.33), channel_id=1, source_target_pairs={{0,6},{1,7},{2,4},{3,5},{4,2},{5,3},{6,0},{7,1},{8,14},{9,15},{10,... | collective-permute-start | bytes 196616 | tf_op jit(solution)/shard_map/ppermute | solution.py:27
  (14 other events, 476.9 us)

commit v3 on v2

v3 whole, which is shorter than its diff:
```python
import functools
import math

import jax
import jax.numpy as jnp
from jax import lax
from jax.experimental import pallas as pl
from jax.experimental.pallas import tpu as pltpu
from jax.sharding import PartitionSpec as P

HD = 128
FR = 64
GROUP = 8
MB = 16
MEMF = 64
NORM_EPS = 1e-06
BF16 = jnp.bfloat16
F32 = jnp.float32
VMEM_BYTES = 32 * 2**20
WIDE_VMEM_BYTES = 48 * 2**20

CORE, NEAR, FAR = 1, 2, 4
CHIPS = (0, NEAR, FAR, NEAR | FAR)


def flip(value, bits):
    size = lax.axis_size("section")
    return lax.ppermute(value, "section", [(i, i ^ bits) for i in range(size)])


def hop(value):
    size = lax.axis_size("section")
    return lax.ppermute(value, "section", [(i, (i + GROUP) % size) for i in range(size)])


def after(value, *others):
    return lax.optimization_barrier((value, *others))[0]


def together(*values):
    return lax.optimization_barrier(values)


def across(value):
    return lax.ppermute(value, "groups", [(0, 1), (1, 0)])


def whole(count):
    return [pl.BlockSpec(memory_space=pltpu.VMEM)] * count


def dot(a, b):
    return jnp.dot(a, b, preferred_element_type=F32)


def keys_values_kernel(*refs):
    *mem_refs, key_own, key_oth, val_own, val_oth, out, rows = refs
    for k, ref in enumerate(mem_refs):
        rows[k * MEMF:(k + 1) * MEMF, :] = ref[:MEMF]
    width = key_own.shape[1]
    for k, weight in enumerate((key_own, key_oth, val_own, val_oth)):
        out[:, k * width:(k + 1) * width] = dot(rows[...], weight[...]).astype(BF16)


def keys_values(pieces, weights):
    depth, width = weights[0].shape
    rows = len(pieces) * MEMF
    return pl.pallas_call(
        keys_values_kernel,
        out_shape=jax.ShapeDtypeStruct((rows, 4 * width), BF16),
        in_specs=whole(len(pieces) + 4),
        out_specs=pl.BlockSpec(memory_space=pltpu.VMEM),
        scratch_shapes=[pltpu.VMEM((rows, depth), BF16)],
        compiler_params=pltpu.CompilerParams(vmem_limit_bytes=VMEM_BYTES),
        cost_estimate=pl.CostEstimate(flops=0, bytes_accessed=0, transcendentals=0),
    )(*pieces, *weights)


def attend_kernel(j, ring, *refs):
    mem_len, x0, x1, x2, x3, query_own, query_oth = refs[:7]
    own_a, own_b, oth_a, oth_b = refs[7:11]
    outs, normed = refs[11:13], refs[13]
    width = query_own.shape[1]
    heads = 2 * width // HD
    me = lax.axis_index("section")
    section, slot, core = me // GROUP, me % GROUP, me % 2
    for k, ref in enumerate((x0, x1, x2, x3)):
        wide = ref[ref.shape[0] - FR:].astype(F32)
        scale = lax.rsqrt(jnp.mean(wide * wide, -1, keepdims=True) + NORM_EPS)
        normed[k * FR:(k + 1) * FR, :] = (wide * scale).astype(BF16)
    queries = jnp.concatenate(
        [dot(normed[...], query_own[...]), dot(normed[...], query_oth[...])], 1
    ).astype(BF16)
    is_own = (section + j) % 2 == core
    column = lax.broadcasted_iota(jnp.int32, (FR, MEMF), 1)
    scores, values = [], []
    for k, chip in enumerate(CHIPS):
        utt = (section + 2 * (slot ^ chip) + j) % MB
        place = (utt ^ me) >> 1 if ring else utt >> 1
        start = pl.multiple_of((place & 3) * MEMF, MEMF)
        here = pl.ds(start, MEMF)
        mine = jnp.where(place < 4, own_a[here, :], own_b[here, :])
        other = jnp.where(place < 4, oth_a[here, :], oth_b[here, :])
        other = jnp.concatenate(
            [other[:, n * width:(n + 1) * width] for n in (1, 0, 3, 2)], 1
        )
        kv = jnp.where(is_own, mine, other)
        length = mem_len[utt]
        values.append(kv[:, 2 * width:])
        for h in range(heads):
            found = lax.dot_general(
                queries[k * FR:(k + 1) * FR, h * HD:(h + 1) * HD],
                kv[:, h * HD:(h + 1) * HD],
                (((1,), (1,)), ((), ())),
                preferred_element_type=F32,
            )
            found = found * (1.0 / math.sqrt(HD))
            scores.append(jnp.where(column < length, found, -jnp.inf))
    score = jnp.concatenate(scores, 0)
    expo = jnp.exp(score - jnp.max(score, -1, keepdims=True))
    probs = (expo / jnp.sum(expo, -1, keepdims=True)).astype(BF16)
    for k in range(4):
        for h in range(heads):
            at = (k * heads + h) * FR
            outs[k // 2][k % 2 * FR:(k % 2 + 1) * FR, h * HD:(h + 1) * HD] = dot(
                probs[at:at + FR], values[k][:, h * HD:(h + 1) * HD]
            ).astype(BF16)


def attend(j, ring, mem_len, pieces, weights, kv):
    depth, width = weights[0].shape
    return pl.pallas_call(
        functools.partial(attend_kernel, j, ring),
        out_shape=[jax.ShapeDtypeStruct((2 * FR, 2 * width), BF16)] * 2,
        in_specs=[pl.BlockSpec(memory_space=pltpu.SMEM)] + whole(10),
        out_specs=whole(2),
        scratch_shapes=[pltpu.VMEM((4 * FR, depth), BF16)],
        compiler_params=pltpu.CompilerParams(vmem_limit_bytes=VMEM_BYTES),
        cost_estimate=pl.CostEstimate(flops=0, bytes_accessed=0, transcendentals=0),
    )(mem_len, *pieces, *weights, *kv)


def project_kernel(near, place, tok_len, *refs):
    att = refs[:8]
    own, oth, direct, crossed = refs[8], refs[9], refs[10:16], refs[16:22]
    x_refs, out = refs[22:24], refs[24]
    me = lax.axis_index("section")
    step = pl.program_id(0)
    half_steps = pl.num_programs(0) // 2
    width = own.shape[0]
    slot = (me % GROUP) ^ (NEAR if near else 0)
    first_row = (me // GROUP) * MB + 2 * slot

    def finish(others):
        total = None
        for k in range(4):
            at = FR if near != (k % 2 == 1) else 0
            pair = (own, oth) if k == 0 else (others[k - 1], others[k + 2])
            for n, weight in enumerate(pair):
                rows = jnp.concatenate(
                    [att[j * 4 + k][at:at + FR, n * width:(n + 1) * width] for j in range(2)], 0
                )
                term = dot(rows, weight[...])
                total = term if total is None else total + term
        row = lax.broadcasted_iota(jnp.int32, (FR, total.shape[1]), 0)
        for j, x_ref in enumerate(x_refs):
            branch = jnp.where(row < tok_len[first_row + j], total[j * FR:(j + 1) * FR], 0.0)
            out[j * FR:(j + 1) * FR, :] = (x_ref[...].astype(F32) + branch).astype(BF16)

    pl.when(step < half_steps)(lambda: finish(direct))
    pl.when(step >= half_steps)(lambda: finish(crossed))


def project(near, place, tok_len, att, own, oth, direct, crossed, x_first, x_last):
    width, depth = own.shape
    rows = 2 * FR
    tile = 512
    half = direct[0].shape[1] // tile

    def column(i, place):
        return jnp.where(i < half, place[0] * half + i, (1 - place[0]) * half + i - half)

    def everywhere(i, place):
        return 0, place[1] * 2 * half + column(i, place)

    att_specs = [pl.BlockSpec((2 * FR, 2 * width), lambda i, place: (0, 0))] * 8
    full = pl.BlockSpec((width, tile), everywhere)
    x_specs = [
        pl.BlockSpec((FR, tile), lambda i, place, at=ref.shape[0] // FR - 1: (at, everywhere(i, place)[1]))
        for ref in (x_first, x_last)
    ]
    early = pl.BlockSpec((width, tile), lambda i, place: (0, jnp.minimum(i, half - 1)))
    late = pl.BlockSpec((width, tile), lambda i, place: (0, jnp.maximum(i - half, 0)))
    return pl.pallas_call(
        functools.partial(project_kernel, near),
        out_shape=jax.ShapeDtypeStruct((rows, 2 * half * tile), BF16),
        grid_spec=pltpu.PrefetchScalarGridSpec(
            num_scalar_prefetch=1,
            grid=(2 * half,),
            in_specs=[pl.BlockSpec(memory_space=pltpu.SMEM)]
            + att_specs + [full, full] + [early] * 6 + [late] * 6
            + x_specs,
            out_specs=pl.BlockSpec((rows, tile), lambda i, place: (0, column(i, place))),
        ),
        compiler_params=pltpu.CompilerParams(
            vmem_limit_bytes=WIDE_VMEM_BYTES, dimension_semantics=("arbitrary",)
        ),
        cost_estimate=pl.CostEstimate(flops=0, bytes_accessed=0, transcendentals=0),
    )(place, tok_len, *att, own, oth, *direct, *crossed, x_first, x_last)


def shards(arriving, memory, w_query, w_key, w_value, w_out, tok_len, mem_len):
    me = lax.axis_index("section")
    size = lax.axis_size("section")
    group = lax.axis_index("groups")
    side = (me // NEAR) % 2
    depth = arriving.shape[1]
    ring = size == MB and memory.shape[0] == MEMF

    part_cols = depth // 4
    to_near = lax.dynamic_slice_in_dim(w_out, (2 * (1 - side) + group) * part_cols, part_cols, 1)
    to_far = lax.dynamic_slice_in_dim(w_out, (2 * side + group) * part_cols, part_cols, 1)
    if not ring:
        gathered = lax.all_gather(memory, "section", axis=0, tiled=True)
        gathered = gathered.reshape(MB // 2, 2, MEMF, depth)
        gathered = lax.dynamic_index_in_dim(gathered, me & 1, 1, keepdims=False)
        gathered = [gathered[k] for k in range(MB // 2)]

    out_near = flip(to_near, NEAR)
    key_oth = flip(w_key, CORE)
    if ring:
        mem_hop, mem_near, mem_far = hop(memory), flip(memory, NEAR), flip(memory, FAR)
    else:
        mem_hop = mem_near = mem_far = out_near
    mem_hop, mem_near, mem_far, out_near, key_oth, arriving, w_value = together(
        mem_hop, mem_near, mem_far, out_near, key_oth, arriving, w_value
    )
    first_hop = hop(arriving[:FR])
    value_oth = flip(w_value, CORE)
    if ring:
        hop_far, hop_near, mem_diag = flip(mem_hop, FAR), flip(mem_hop, NEAR), flip(mem_far, NEAR)
    else:
        hop_far = hop_near = mem_diag = mem_far
    first_hop, hop_far, hop_near, mem_diag, value_oth, arriving, out_near = together(
        first_hop, hop_far, hop_near, mem_diag, value_oth, arriving, out_near
    )
    kv_weights = [w_key, key_oth, w_value, value_oth]
    last_hop = hop(arriving[FR:])
    first_far, first_near = flip(first_hop, FAR), flip(first_hop, NEAR)
    hop_diag = flip(hop_far, NEAR) if ring else hop_far
    cross_near = across(out_near)
    mem_first = [memory, mem_near, mem_far, mem_diag] if ring else gathered[:4]
    kv_first = keys_values(mem_first, kv_weights)
    last_hop, first_far, first_near, hop_diag, cross_near, kv_first, to_far, w_query = together(
        last_hop, first_far, first_near, hop_diag, cross_near, kv_first, to_far, w_query
    )
    last_far, last_near, first_diag = flip(last_hop, FAR), flip(last_hop, NEAR), flip(first_far, NEAR)
    out_far = flip(to_far, FAR)
    query_oth = flip(w_query, CORE)
    mem_second = [mem_hop, hop_near, hop_far, hop_diag] if ring else gathered[4:]
    kv_second = keys_values(mem_second, kv_weights)
    last_far, last_near, first_diag, out_far, query_oth, kv_second, kv_first, out_near, w_out = together(
        last_far, last_near, first_diag, out_far, query_oth, kv_second, kv_first, out_near, w_out
    )
    query_pair = [w_query, query_oth]
    last_diag = flip(last_far, NEAR)
    out_diag = flip(out_near, FAR)
    cross_far = across(out_far)
    kv = [kv_first, kv_second, flip(kv_first, CORE), flip(kv_second, CORE)]
    first = [first_hop, first_near, first_far, first_diag]
    here, there = attend(0, ring, mem_len, first, query_pair, kv)
    att = [here, flip(here, NEAR), flip(there, FAR), flip(there, NEAR | FAR)]
    near_core, far_core, cross_core = [
        flip(after(part, kv[2], kv[3]), CORE) for part in (out_near, out_far, cross_near)
    ]
    last_diag, out_diag, cross_far, w_out, near_core, far_core, cross_core, *att[1:] = together(
        last_diag, out_diag, cross_far, w_out, near_core, far_core, cross_core, *att[1:]
    )
    cross_diag = across(out_diag)
    out_core = flip(w_out, CORE)
    last = [last_hop, last_near, last_far, last_diag]
    here, there = attend(1, ring, mem_len, last, query_pair, kv)
    att += [here, flip(here, NEAR), flip(there, FAR), flip(there, NEAR | FAR)]
    rest = [out_diag, cross_far, cross_diag]
    diag_core, cross_far_core, cross_diag_core = [
        flip(part, CORE) for part in together(*rest, *att[5:])[:3]
    ]
    direct = [out_near, out_far, out_diag]
    crossed = [cross_near, cross_far, cross_diag]
    direct_core = [near_core, far_core, diag_core]
    crossed_core = [cross_core, cross_far_core, cross_diag_core]

    place = jnp.stack([group, side]).astype(jnp.int32)
    direct = direct + direct_core
    crossed = crossed + crossed_core
    theirs = project(True, place, tok_len, att, w_out, out_core, direct, crossed, first[1], last[1])
    theirs = flip(theirs, NEAR)
    mine = project(False, place, tok_len, att, w_out, out_core, direct, crossed, first[0], last[0])
    return jnp.where(
        side == 0, jnp.concatenate([mine, theirs], 1), jnp.concatenate([theirs, mine], 1)
    )


def solution(mesh):
    return jax.shard_map(
        shards,
        mesh=mesh,
        in_specs=(
            P(("groups", "section"), None),
            P(("groups", "section"), None),
            P(None, "section"),
            P(None, "section"),
            P(None, "section"),
            P("section", None),
            P("groups"),
            P("groups"),
        ),
        out_specs=P(("groups", "section"), None),
        check_vma=False,
    )
```

time: 207 us -> 184 us (0.89)
  waiting for transfers between devices: 135 us -> 103 us
  local copies, waits for them, and re-layouts: 2.41 us -> 16.3 us
  Pallas kernels: 29.9 us -> 23.8 us
  other arithmetic: 0.09 us -> 2.49 us
  starting transfers between devices: 39.4 us -> 37 us
    ppermute x30 -> x34, waiting for transfers between devices: 128 us -> 57.7 us  [flip(): return lax.ppermute(value, 'section', [(i, i ^ bits) for i in range(size)])]
    ppermute x2 -> x3, waiting for transfers between devices: 6.54 us -> 44.9 us  [hop(): lax.ppermute(value, 'section', [(i, (i + GROUP) % size) for i in range(si...]
    unnamed x22 -> x72, local copies, waits for them, and re-layouts: 0.96 us -> 12.7 us
    pallas_call x2, Pallas kernels: 9.25 us -> 5.52 us  [attend(): pl.pallas_call(functools.partial(attend_kernel, j, ring), out_shape=[jax....]
    pallas_call x2, Pallas kernels: 11 us -> 8.06 us  [keys_values(): pl.pallas_call(keys_values_kernel, out_shape=jax.ShapeDtypeStruct((rows,...]
    select_n x0 -> x1, other arithmetic: none -> 2.41 us  [shards(): jnp.where(side == 0, jnp.concatenate([mine, theirs], 1), jnp.concatenate(...]
    slice x1 -> x2, local copies, waits for them, and re-layouts: 0.07 us -> 2.26 us  [the longest x1 1.18 us: shards(): first_hop = hop(arriving[:FR])]
    ppermute x30 -> x34, starting transfers between devices: 29.5 us -> 28.5 us  [flip(): return lax.ppermute(value, 'section', [(i, i ^ bits) for i in range(size)])]
  transfers between devices with their start and end apart: 35 -> 40, of which waited for: 14 -> 24; matrix products, arithmetic and copies ran while one was open for 1% -> 1% of each run, Pallas kernels for 10% -> 10%
where the time goes in v3:
time: 184 us; the launch traced here: 183 us
  waiting for transfers between devices  103 us (56%)
  starting transfers between devices  37 us (20%)
  Pallas kernels  23.8 us (13%)
  local copies, waits for them, and re-layouts  16.3 us (9%)
  other arithmetic  2.49 us (1%)
    ppermute x34, waiting for transfers between devices, flip(): return lax.ppermute(value, 'section', [(i, i ^ bits) for i in range(size)])  57.7 us
    ppermute x3, waiting for transfers between devices, hop(): lax.ppermute(value, 'section', [(i, (i + GROUP) % size) for i in range(si...  44.9 us
    ppermute x34, starting transfers between devices, flip(): return lax.ppermute(value, 'section', [(i, i ^ bits) for i in range(size)])  28.5 us
    unnamed x72, local copies, waits for them, and re-layouts  12.7 us
    pallas_call x2, Pallas kernels, project(): pl.pallas_call(functools.partial(project_kernel, near), out_shape=jax.Sha...  10.2 us
    pallas_call x2, Pallas kernels, keys_values(): pl.pallas_call(keys_values_kernel, out_shape=jax.ShapeDtypeStruct((rows,...  8.06 us
    pallas_call x2, Pallas kernels, attend(): pl.pallas_call(functools.partial(attend_kernel, j, ring), out_shape=[jax....  5.52 us
    ppermute x3, starting transfers between devices, hop(): lax.ppermute(value, 'section', [(i, (i + GROUP) % size) for i in range(si...  4.93 us
  transfers between devices with their start and end apart: 40, of which 24 were waited for; matrix products, arithmetic and copies ran while one was open for 1% of the time, Pallas kernels for 10%

profile of v3, /device:TPU:0, one launch (start us, length us, event | category | flops | bytes accessed | tf_op | source)
XLA Modules:
  0.0 183.2 jit_solution(11330845397485501687)
XLA Ops:
  0.5 2.6 %collective-permute-start.1 = (bf16[64,4096]{1,0:T(8,128)(2,1)}, bf16[64,4096]{1,0:T(8,128)(2,1)S(1)}, u32[]{:S(2)}, u32[]{:S(2)}) collective-permute-start(bf16[64,4096]{1,0:T(8,128)(2,1)} %refs_0_.3), channel_id=1, source_target_pairs={{0,2},{1,3},{2,0},{3,1},{4,6},{5,7},{6,4},{7,5},{8,10},{9,11},{10,... | collective-permute-start | bytes 1572872 | tf_op jit(solution)/shard_map/ppermute | solution.py:28
  3.0 2.6 %collective-permute-start = (bf16[64,4096]{1,0:T(8,128)(2,1)}, bf16[64,4096]{1,0:T(8,128)(2,1)S(1)}, u32[]{:S(2)}, u32[]{:S(2)}) collective-permute-start(bf16[64,4096]{1,0:T(8,128)(2,1)} %refs_0_.3), channel_id=1, source_target_pairs={{0,8},{1,9},{2,10},{3,11},{4,12},{5,13},{6,14},{7,15},{8,0},{9,1},... | collective-permute-start | bytes 1572872 | tf_op jit(solution)/shard_map/ppermute | solution.py:33
  5.6 1.6 collective-permute-start.2
  7.2 1.4 constant_dynamic-slice_fusion
  9.2 6.8 %collective-permute-done.1.refs_1_ = bf16[64,4096]{1,0:T(8,128)(2,1)S(1)} collective-permute-done((bf16[64,4096]{1,0:T(8,128)(2,1)}, bf16[64,4096]{1,0:T(8,128)(2,1)S(1)}, u32[]{:S(2)}, u32[]{:S(2)}) %collective-permute-start.1) | collective-permute-done | bytes 524320 | tf_op jit(solution)/shard_map/ppermute | solution.py:28
  16.8 12.7 %collective-permute-done.refs_0_ = bf16[64,4096]{1,0:T(8,128)(2,1)S(1)} collective-permute-done((bf16[64,4096]{1,0:T(8,128)(2,1)}, bf16[64,4096]{1,0:T(8,128)(2,1)S(1)}, u32[]{:S(2)}, u32[]{:S(2)}) %collective-permute-start) | collective-permute-done | bytes 524320 | tf_op jit(solution)/shard_map/ppermute | solution.py:33
  31.1 1.4 collective-permute-start.5
  33.0 1.5 collective-permute-start.7
  34.5 2.5 %collective-permute-start.6 = (bf16[64,4096]{1,0:T(8,128)(2,1)S(1)}, bf16[64,4096]{1,0:T(8,128)(2,1)S(1)}, u32[]{:S(2)}, u32[]{:S(2)}) collective-permute-start(bf16[64,4096]{1,0:T(8,128)(2,1)S(1)} %collective-permute-done.refs_0_), channel_id=1, source_target_pairs={{0,4},{1,5},{2,6},{3,7},{4,0},{5,1},{6,2},{7,3},{8,12},{9,13},{10,... | collective-permute-start | bytes 1572872 | tf_op jit(solution)/shard_map/ppermute | solution.py:28
  37.0 20.6 %collective-permute-done.5.refs_1_.refs_22_ = bf16[64,4096]{1,0:T(8,128)(2,1)S(1)} collective-permute-done((bf16[64,4096]{1,0:T(8,128)(2,1)S(1)}, bf16[64,4096]{1,0:T(8,128)(2,1)S(1)}, u32[]{:S(2)}, u32[]{:S(2)}) %collective-permute-start.5) | collective-permute-done | bytes 524320 | tf_op jit(solution)/shard_map/ppermute | solution.py:33
  61.2 1.5 collective-permute-start.14
  62.7 1.5 collective-permute-start.12
  64.2 2.5 %collective-permute-start.11 = (bf16[64,4096]{1,0:T(8,128)(2,1)S(1)}, bf16[64,4096]{1,0:T(8,128)(2,1)S(1)}, u32[]{:S(2)}, u32[]{:S(2)}) collective-permute-start(bf16[64,4096]{1,0:T(8,128)(2,1)S(1)} %collective-permute-done.5.refs_1_.refs_22_), channel_id=1, source_target_pairs={{0,4},{1,5},{2,6},{3,7},{4,0},{5,1},{6,2},{7,3},{8,12},{9,13},{10,... | collective-permute-start | bytes 1572872 | tf_op jit(solution)/shard_map/ppermute | solution.py:28
  68.8 4.1 %shard_map.82.refs_7_ = bf16[256,1024]{1,0:T(8,128)(2,1)S(1)} custom-call(bf16[64,4096]{1,0:T(8,128)(2,1)S(1)} %copy-done.13, bf16[64,4096]{1,0:T(8,128)(2,1)S(1)} %copy-done.17, bf16[64,4096]{1,0:T(8,128)(2,1)} %collective-permute-done.2.refs_2_, bf16[64,4096]{1,0:T(8,128)(2,1)S(1)} %collective-permute-done.8.refs_3_, bf16[4096,256]{1,0:T(8,128)(2,1)S(1)} %copy-done, ...), custom_call_target="tpu_custom_call" | custom-call | tf_op jit(solution)/shard_map/pallas_call | solution.py:68
  73.0 11.6 %collective-permute-done.10.refs_1_.refs_23_ = bf16[64,4096]{1,0:T(8,128)(2,1)S(1)} collective-permute-done((bf16[64,4096]{1,0:T(8,128)(2,1)S(1)}, bf16[64,4096]{1,0:T(8,128)(2,1)S(1)}, u32[]{:S(2)}, u32[]{:S(2)}) %collective-permute-start.10) | collective-permute-done | bytes 524320 | tf_op jit(solution)/shard_map/ppermute | solution.py:33
  84.6 1.4 collective-permute-done.11.refs_3_
  87.3 1.6 collective-permute-start.16
  90.1 3.9 %shard_map.83.refs_8_ = bf16[256,1024]{1,0:T(8,128)(2,1)S(1)} custom-call(bf16[64,4096]{1,0:T(8,128)(2,1)S(1)} %copy-done.15, bf16[64,4096]{1,0:T(8,128)(2,1)S(1)} %collective-permute-done.7.refs_1_, bf16[64,4096]{1,0:T(8,128)(2,1)S(1)} %collective-permute-done.6.refs_2_, bf16[64,4096]{1,0:T(8,128)(2,1)S(1)} %collective-permute-done.13.refs_3_, ...), custom_call_target="tpu_custom_call" | custom-call | tf_op jit(solution)/shard_map/pallas_call | solution.py:68
  94.1 6.7 %collective-permute-done.18.refs_11_ = bf16[256,1024]{1,0:T(8,128)(2,1)S(1)} collective-permute-done((bf16[256,1024]{1,0:T(8,128)(2,1)S(1)}, bf16[256,1024]{1,0:T(8,128)(2,1)S(1)}, u32[]{:S(2)}, u32[]{:S(2)}) %collective-permute-start.18) | collective-permute-done | bytes 524320 | tf_op jit(solution)/shard_map/ppermute | solution.py:28
  101.6 10.4 %collective-permute-done.16.refs_2_.refs_23_ = bf16[64,4096]{1,0:T(8,128)(2,1)S(1)} collective-permute-done((bf16[64,4096]{1,0:T(8,128)(2,1)S(1)}, bf16[64,4096]{1,0:T(8,128)(2,1)S(1)}, u32[]{:S(2)}, u32[]{:S(2)}) %collective-permute-start.16) | collective-permute-done | bytes 524320 | tf_op jit(solution)/shard_map/ppermute | solution.py:28
  115.5 11.0 %collective-permute-done.22.refs_4_ = bf16[64,4096]{1,0:T(8,128)(2,1)S(1)} collective-permute-done((bf16[64,4096]{1,0:T(8,128)(2,1)S(1)}, bf16[64,4096]{1,0:T(8,128)(2,1)S(1)}, u32[]{:S(2)}, u32[]{:S(2)}) %collective-permute-start.22) | collective-permute-done | bytes 524320 | tf_op jit(solution)/shard_map/ppermute | solution.py:28
  126.5 2.8 %shard_map.84 = (bf16[128,512]{1,0:T(8,128)(2,1)S(1)}, bf16[128,512]{1,0:T(8,128)(2,1)S(1)}) custom-call(s32[16]{0:T(128)S(1)} %copy-done.28, bf16[64,4096]{1,0:T(8,128)(2,1)S(1)} %collective-permute-done.5.refs_1_.refs_22_, bf16[64,4096]{1,0:T(8,128)(2,1)S(1)} %collective-permute-done.12.refs_2_.refs_22_, ...), custom_call_target="tpu_custom_call" | custom-call | tf_op jit(solution)/shard_map/pallas_call | solution.py:132
  131.3 5.2 %collective-permute-done.30.refs_3_ = bf16[128,512]{1,0:T(8,128)(2,1)S(1)} collective-permute-done((bf16[128,512]{1,0:T(8,128)(2,1)S(1)}, bf16[128,512]{1,0:T(8,128)(2,1)S(1)}, u32[]{:S(2)}, u32[]{:S(2)}) %collective-permute-start.30) | collective-permute-done | bytes 131104 | tf_op jit(solution)/shard_map/ppermute | solution.py:28
  138.0 3.5 %collective-permute-done.28.refs_1_ = bf16[128,512]{1,0:T(8,128)(2,1)S(1)} collective-permute-done((bf16[128,512]{1,0:T(8,128)(2,1)S(1)}, bf16[128,512]{1,0:T(8,128)(2,1)S(1)}, u32[]{:S(2)}, u32[]{:S(2)}) %collective-permute-start.28) | collective-permute-done | bytes 131104 | tf_op jit(solution)/shard_map/ppermute | solution.py:28
  141.6 1.6 collective-permute-start.35
  143.2 2.8 %shard_map.85 = (bf16[128,512]{1,0:T(8,128)(2,1)S(1)}, bf16[128,512]{1,0:T(8,128)(2,1)S(1)}) custom-call(s32[16]{0:T(128)S(1)} %copy-done.28, bf16[64,4096]{1,0:T(8,128)(2,1)S(1)} %collective-permute-done.10.refs_1_.refs_23_, bf16[64,4096]{1,0:T(8,128)(2,1)S(1)} %collective-permute-done.16.refs_2_.refs_23_, ...), custom_call_target="tpu_custom_call" | custom-call | tf_op jit(solution)/shard_map/pallas_call | solution.py:132
  146.4 1.6 collective-permute-start.32
  148.0 1.5 collective-permute-start.31
  149.5 3.8 %collective-permute-done.33.refs_7_ = bf16[128,512]{1,0:T(8,128)(2,1)S(1)} collective-permute-done((bf16[128,512]{1,0:T(8,128)(2,1)S(1)}, bf16[128,512]{1,0:T(8,128)(2,1)S(1)}, u32[]{:S(2)}, u32[]{:S(2)}) %collective-permute-start.33) | collective-permute-done | bytes 131104 | tf_op jit(solution)/shard_map/ppermute | solution.py:28
  161.5 5.1 %shard_map.87 = bf16[128,2048]{1,0:T(8,128)(2,1)S(1)} custom-call(s32[2]{0:T(128)S(1)} %pad_add_fusion.place, s32[32]{0:T(128)S(1)} %copy-done.29, bf16[128,512]{1,0:T(8,128)(2,1)S(1)} %get-tuple-element.81.refs_0_, bf16[128,512]{1,0:T(8,128)(2,1)S(1)} %collective-permute-done.28.refs_1_, bf16[128,512]{1,0:T(8,128)(2,1)S(1)} %collective-permute-done.29.refs_2_, ...), custom_call_target="tpu_custom_call" | custom-call | tf_op jit(solution)/shard_map/pallas_call | solution.py:194
  174.9 5.1 %shard_map.86 = bf16[128,2048]{1,0:T(8,128)(2,1)S(1)} custom-call(s32[2]{0:T(128)S(1)} %pad_add_fusion.place, s32[32]{0:T(128)S(1)} %copy-done.29, bf16[128,512]{1,0:T(8,128)(2,1)S(1)} %get-tuple-element.81.refs_0_, bf16[128,512]{1,0:T(8,128)(2,1)S(1)} %copy-done.19, bf16[128,512]{1,0:T(8,128)(2,1)S(1)} %collective-permute-done.29.refs_2_, ...), custom_call_target="tpu_custom_call" | custom-call | tf_op jit(solution)/shard_map/pallas_call | solution.py:194
  180.8 2.4 %maximum_select_fusion = bf16[128,4096]{1,0:T(8,128)(2,1)} fusion(bf16[128,2048]{1,0:T(8,128)(2,1)} %collective-permute-done.39, bf16[128,2048]{1,0:T(8,128)(2,1)S(1)} %shard_map.86, pred[]{:T(512)S(6)} %eq.5), kind=kLoop, calls=%fused_computation | loop fusion | flops 4718592 | bytes 2097153 | tf_op jit(solution)/shard_map/jit(_where)/select_n | solution.py:299
  (131 shorter events, 37.6 us)
Async XLA Ops:
  0.0 29.8 %collective-permute-start.4 = (bf16[4096,256]{1,0:T(8,128)(2,1)}, bf16[4096,256]{1,0:T(8,128)(2,1)}, u32[]{:S(2)}, u32[]{:S(2)}) collective-permute-start(bf16[4096,256]{1,0:T(8,128)(2,1)} %refs_4_.3), channel_id=1, source_target_pairs={{0,1},{1,0},{2,3},{3,2},{4,5},{5,4},{6,7},{7,6},{8,9},{9,8},{10,11... | collective-permute-start | bytes 6291464 | tf_op jit(solution)/shard_map/ppermute | solution.py:28
  0.5 15.6 %collective-permute-start.1 = (bf16[64,4096]{1,0:T(8,128)(2,1)}, bf16[64,4096]{1,0:T(8,128)(2,1)S(1)}, u32[]{:S(2)}, u32[]{:S(2)}) collective-permute-start(bf16[64,4096]{1,0:T(8,128)(2,1)} %refs_0_.3), channel_id=1, source_target_pairs={{0,2},{1,3},{2,0},{3,1},{4,6},{5,7},{6,4},{7,5},{8,10},{9,11},{10,... | collective-permute-start | bytes 1572872 | tf_op jit(solution)/shard_map/ppermute | solution.py:28
  3.0 26.5 %collective-permute-start = (bf16[64,4096]{1,0:T(8,128)(2,1)}, bf16[64,4096]{1,0:T(8,128)(2,1)S(1)}, u32[]{:S(2)}, u32[]{:S(2)}) collective-permute-start(bf16[64,4096]{1,0:T(8,128)(2,1)} %refs_0_.3), channel_id=1, source_target_pairs={{0,8},{1,9},{2,10},{3,11},{4,12},{5,13},{6,14},{7,15},{8,0},{9,1},... | collective-permute-start | bytes 1572872 | tf_op jit(solution)/shard_map/ppermute | solution.py:33
  5.6 24.2 %collective-permute-start.2 = (bf16[64,4096]{1,0:T(8,128)(2,1)}, bf16[64,4096]{1,0:T(8,128)(2,1)}, u32[]{:S(2)}, u32[]{:S(2)}) collective-permute-start(bf16[64,4096]{1,0:T(8,128)(2,1)} %refs_0_.3), channel_id=1, source_target_pairs={{0,4},{1,5},{2,6},{3,7},{4,0},{5,1},{6,2},{7,3},{8,12},{9,13},{10,... | collective-permute-start | bytes 1572872 | tf_op jit(solution)/shard_map/ppermute | solution.py:28
  8.6 21.2 %collective-permute-start.3 = (bf16[256,1024]{1,0:T(8,128)(2,1)S(1)}, bf16[256,1024]{1,0:T(8,128)(2,1)S(1)}, u32[]{:S(2)}, u32[]{:S(2)}) collective-permute-start(bf16[256,1024]{1,0:T(8,128)(2,1)S(1)} %get-tuple-element.108), channel_id=1, source_target_pairs={{0,2},{1,3},{2,0},{3,1},{4,6},{5,7},{6,4},{7,5},{8,10},{9,11},{10,... | collective-permute-start | bytes 1572872 | tf_op jit(solution)/shard_map/ppermute | solution.py:28
  29.8 28.9 %collective-permute-start.9 = (bf16[4096,256]{1,0:T(8,128)(2,1)S(1)}, bf16[4096,256]{1,0:T(8,128)(2,1)S(1)}, u32[]{:S(2)}, u32[]{:S(2)}) collective-permute-start(bf16[4096,256]{1,0:T(8,128)(2,1)S(1)} %copy-done.1), channel_id=1, source_target_pairs={{0,1},{1,0},{2,3},{3,2},{4,5},{5,4},{6,7},{7,6},{8,9},{9,8},{10,11... | collective-permute-start | bytes 6291464 | tf_op jit(solution)/shard_map/ppermute | solution.py:28
  31.1 26.5 %collective-permute-start.5 = (bf16[64,4096]{1,0:T(8,128)(2,1)S(1)}, bf16[64,4096]{1,0:T(8,128)(2,1)S(1)}, u32[]{:S(2)}, u32[]{:S(2)}) collective-permute-start(bf16[64,4096]{1,0:T(8,128)(2,1)S(1)} %slice.6), channel_id=1, source_target_pairs={{0,8},{1,9},{2,10},{3,11},{4,12},{5,13},{6,14},{7,15},{8,0},{9,1},... | collective-permute-start | bytes 1572872 | tf_op jit(solution)/shard_map/ppermute | solution.py:33
  32.5 25.1 %collective-permute-start.8 = (bf16[64,4096]{1,0:T(8,128)(2,1)}, bf16[64,4096]{1,0:T(8,128)(2,1)S(1)}, u32[]{:S(2)}, u32[]{:S(2)}) collective-permute-start(bf16[64,4096]{1,0:T(8,128)(2,1)} %collective-permute-done.2.refs_2_), channel_id=1, source_target_pairs={{0,2},{1,3},{2,0},{3,1},{4,6},{5,7},{6,4},{7,5},{8,10},{9,11},{10,... | collective-permute-start | bytes 1572872 | tf_op jit(solution)/shard_map/ppermute | solution.py:28
  33.0 24.8 %collective-permute-start.7 = (bf16[64,4096]{1,0:T(8,128)(2,1)S(1)}, bf16[64,4096]{1,0:T(8,128)(2,1)S(1)}, u32[]{:S(2)}, u32[]{:S(2)}) collective-permute-start(bf16[64,4096]{1,0:T(8,128)(2,1)S(1)} %collective-permute-done.refs_0_), channel_id=1, source_target_pairs={{0,2},{1,3},{2,0},{3,1},{4,6},{5,7},{6,4},{7,5},{8,10},{9,11},{10,... | collective-permute-start | bytes 1572872 | tf_op jit(solution)/shard_map/ppermute | solution.py:28
  34.5 24.2 %collective-permute-start.6 = (bf16[64,4096]{1,0:T(8,128)(2,1)S(1)}, bf16[64,4096]{1,0:T(8,128)(2,1)S(1)}, u32[]{:S(2)}, u32[]{:S(2)}) collective-permute-start(bf16[64,4096]{1,0:T(8,128)(2,1)S(1)} %collective-permute-done.refs_0_), channel_id=1, source_target_pairs={{0,4},{1,5},{2,6},{3,7},{4,0},{5,1},{6,2},{7,3},{8,12},{9,13},{10,... | collective-permute-start | bytes 1572872 | tf_op jit(solution)/shard_map/ppermute | solution.py:28
  59.8 24.7 %collective-permute-start.10 = (bf16[64,4096]{1,0:T(8,128)(2,1)S(1)}, bf16[64,4096]{1,0:T(8,128)(2,1)S(1)}, u32[]{:S(2)}, u32[]{:S(2)}) collective-permute-start(bf16[64,4096]{1,0:T(8,128)(2,1)S(1)} %slice.7), channel_id=1, source_target_pairs={{0,8},{1,9},{2,10},{3,11},{4,12},{5,13},{6,14},{7,15},{8,0},{9,1},... | collective-permute-start | bytes 1572872 | tf_op jit(solution)/shard_map/ppermute | solution.py:33
  60.7 23.8 %collective-permute-start.13 = (bf16[64,4096]{1,0:T(8,128)(2,1)S(1)}, bf16[64,4096]{1,0:T(8,128)(2,1)S(1)}, u32[]{:S(2)}, u32[]{:S(2)}) collective-permute-start(bf16[64,4096]{1,0:T(8,128)(2,1)S(1)} %collective-permute-done.6.refs_2_), channel_id=1, source_target_pairs={{0,2},{1,3},{2,0},{3,1},{4,6},{5,7},{6,4},{7,5},{8,10},{9,11},{10,... | collective-permute-start | bytes 1572872 | tf_op jit(solution)/shard_map/ppermute | solution.py:28
  61.2 23.3 %collective-permute-start.14 = (bf16[256,1024]{1,0:T(8,128)(2,1)S(1)}, bf16[256,1024]{1,0:T(8,128)(2,1)S(1)}, u32[]{:S(2)}, u32[]{:S(2)}) collective-permute-start(bf16[256,1024]{1,0:T(8,128)(2,1)S(1)} %collective-permute-done.3.refs_10_), channel_id=1, source_target_pairs={{0,16},{16,0},{1,17},{17,1},{2,18},{18,2},{3,19},{19,3},{4,20},{20... | collective-permute-start | bytes 1572872 | tf_op jit(solution)/shard_map/ppermute | solution.py:45
  62.7 21.9 %collective-permute-start.12 = (bf16[64,4096]{1,0:T(8,128)(2,1)S(1)}, bf16[64,4096]{1,0:T(8,128)(2,1)S(1)}, u32[]{:S(2)}, u32[]{:S(2)}) collective-permute-start(bf16[64,4096]{1,0:T(8,128)(2,1)S(1)} %collective-permute-done.5.refs_1_.refs_22_), channel_id=1, source_target_pairs={{0,2},{1,3},{2,0},{3,1},{4,6},{5,7},{6,4},{7,5},{8,10},{9,11},{10,... | collective-permute-start | bytes 1572872 | tf_op jit(solution)/shard_map/ppermute | solution.py:28
  64.2 21.8 %collective-permute-start.11 = (bf16[64,4096]{1,0:T(8,128)(2,1)S(1)}, bf16[64,4096]{1,0:T(8,128)(2,1)S(1)}, u32[]{:S(2)}, u32[]{:S(2)}) collective-permute-start(bf16[64,4096]{1,0:T(8,128)(2,1)S(1)} %collective-permute-done.5.refs_1_.refs_22_), channel_id=1, source_target_pairs={{0,4},{1,5},{2,6},{3,7},{4,0},{5,1},{6,2},{7,3},{8,12},{9,13},{10,... | collective-permute-start | bytes 1572872 | tf_op jit(solution)/shard_map/ppermute | solution.py:28
  86.0 26.0 %collective-permute-start.19 = (bf16[4096,256]{1,0:T(8,128)(2,1)S(1)}, bf16[4096,256]{1,0:T(8,128)(2,1)S(1)}, u32[]{:S(2)}, u32[]{:S(2)}) collective-permute-start(bf16[4096,256]{1,0:T(8,128)(2,1)S(1)} %copy-done.2), channel_id=1, source_target_pairs={{0,1},{1,0},{2,3},{3,2},{4,5},{5,4},{6,7},{7,6},{8,9},{9,8},{10,11... | collective-permute-start | bytes 6291464 | tf_op jit(solution)/shard_map/ppermute | solution.py:28
  86.0 14.8 %collective-permute-start.18 = (bf16[256,1024]{1,0:T(8,128)(2,1)S(1)}, bf16[256,1024]{1,0:T(8,128)(2,1)S(1)}, u32[]{:S(2)}, u32[]{:S(2)}) collective-permute-start(bf16[256,1024]{1,0:T(8,128)(2,1)S(1)} %get-tuple-element.72), channel_id=1, source_target_pairs={{0,4},{1,5},{2,6},{3,7},{4,0},{5,1},{6,2},{7,3},{8,12},{9,13},{10,... | collective-permute-start | bytes 1572872 | tf_op jit(solution)/shard_map/ppermute | solution.py:28
  86.8 14.8 %collective-permute-start.17 = (bf16[64,4096]{1,0:T(8,128)(2,1)S(1)}, bf16[64,4096]{1,0:T(8,128)(2,1)S(1)}, u32[]{:S(2)}, u32[]{:S(2)}) collective-permute-start(bf16[64,4096]{1,0:T(8,128)(2,1)S(1)} %collective-permute-done.11.refs_3_), channel_id=1, source_target_pairs={{0,2},{1,3},{2,0},{3,1},{4,6},{5,7},{6,4},{7,5},{8,10},{9,11},{10,... | collective-permute-start | bytes 1572872 | tf_op jit(solution)/shard_map/ppermute | solution.py:28
  87.3 24.7 %collective-permute-start.16 = (bf16[64,4096]{1,0:T(8,128)(2,1)S(1)}, bf16[64,4096]{1,0:T(8,128)(2,1)S(1)}, u32[]{:S(2)}, u32[]{:S(2)}) collective-permute-start(bf16[64,4096]{1,0:T(8,128)(2,1)S(1)} %collective-permute-done.10.refs_1_.refs_23_), channel_id=1, source_target_pairs={{0,2},{1,3},{2,0},{3,1},{4,6},{5,7},{6,4},{7,5},{8,10},{9,11},{10,... | collective-permute-start | bytes 1572872 | tf_op jit(solution)/shard_map/ppermute | solution.py:28
  88.8 23.2 %collective-permute-start.15 = (bf16[64,4096]{1,0:T(8,128)(2,1)S(1)}, bf16[64,4096]{1,0:T(8,128)(2,1)S(1)}, u32[]{:S(2)}, u32[]{:S(2)}) collective-permute-start(bf16[64,4096]{1,0:T(8,128)(2,1)S(1)} %collective-permute-done.10.refs_1_.refs_23_), channel_id=1, source_target_pairs={{0,4},{1,5},{2,6},{3,7},{4,0},{5,1},{6,2},{7,3},{8,12},{9,13},{10,... | collective-permute-start | bytes 1572872 | tf_op jit(solution)/shard_map/ppermute | solution.py:28
  112.6 13.9 %collective-permute-start.22 = (bf16[64,4096]{1,0:T(8,128)(2,1)S(1)}, bf16[64,4096]{1,0:T(8,128)(2,1)S(1)}, u32[]{:S(2)}, u32[]{:S(2)}) collective-permute-start(bf16[64,4096]{1,0:T(8,128)(2,1)S(1)} %collective-permute-done.15.refs_3_), channel_id=1, source_target_pairs={{0,2},{1,3},{2,0},{3,1},{4,6},{5,7},{6,4},{7,5},{8,10},{9,11},{10,... | collective-permute-start | bytes 1572872 | tf_op jit(solution)/shard_map/ppermute | solution.py:28
  113.1 16.2 %collective-permute-start.23 = (bf16[256,1024]{1,0:T(8,128)(2,1)S(1)}, bf16[256,1024]{1,0:T(8,128)(2,1)S(1)}, u32[]{:S(2)}, u32[]{:S(2)}) collective-permute-start(bf16[256,1024]{1,0:T(8,128)(2,1)S(1)} %collective-permute-done.3.refs_10_), channel_id=1, source_target_pairs={{0,4},{1,5},{2,6},{3,7},{4,0},{5,1},{6,2},{7,3},{8,12},{9,13},{10,... | collective-permute-start | bytes 1572872 | tf_op jit(solution)/shard_map/ppermute | solution.py:28
  114.4 16.2 %collective-permute-start.24 = (bf16[256,1024]{1,0:T(8,128)(2,1)S(1)}, bf16[256,1024]{1,0:T(8,128)(2,1)S(1)}, u32[]{:S(2)}, u32[]{:S(2)}) collective-permute-start(bf16[256,1024]{1,0:T(8,128)(2,1)S(1)} %collective-permute-done.18.refs_11_), channel_id=1, source_target_pairs={{0,16},{16,0},{1,17},{17,1},{2,18},{18,2},{3,19},{19,3},{4,20},{20... | collective-permute-start | bytes 1572872 | tf_op jit(solution)/shard_map/ppermute | solution.py:45
  115.0 26.6 %collective-permute-start.25 = (bf16[256,1024]{1,0:T(8,128)(2,1)S(1)}, bf16[256,1024]{1,0:T(8,128)(2,1)S(1)}, u32[]{:S(2)}, u32[]{:S(2)}) collective-permute-start(bf16[256,1024]{1,0:T(8,128)(2,1)S(1)} %collective-permute-done.3.refs_10_), channel_id=1, source_target_pairs={{0,1},{1,0},{2,3},{3,2},{4,5},{5,4},{6,7},{7,6},{8,9},{9,8},{10,11... | collective-permute-start | bytes 1572872 | tf_op jit(solution)/shard_map/ppermute | solution.py:28
  115.0 26.5 %collective-permute-start.26 = (bf16[256,1024]{1,0:T(8,128)(2,1)S(1)}, bf16[256,1024]{1,0:T(8,128)(2,1)S(1)}, u32[]{:S(2)}, u32[]{:S(2)}) collective-permute-start(bf16[256,1024]{1,0:T(8,128)(2,1)S(1)} %collective-permute-done.18.refs_11_), channel_id=1, source_target_pairs={{0,1},{1,0},{2,3},{3,2},{4,5},{5,4},{6,7},{7,6},{8,9},{9,8},{10,11... | collective-permute-start | bytes 1572872 | tf_op jit(solution)/shard_map/ppermute | solution.py:28
  126.5 15.0 %collective-permute-start.27 = (bf16[256,1024]{1,0:T(8,128)(2,1)S(1)}, bf16[256,1024]{1,0:T(8,128)(2,1)S(1)}, u32[]{:S(2)}, u32[]{:S(2)}) collective-permute-start(bf16[256,1024]{1,0:T(8,128)(2,1)S(1)} %collective-permute-done.14.refs_16_), channel_id=1, source_target_pairs={{0,1},{1,0},{2,3},{3,2},{4,5},{5,4},{6,7},{7,6},{8,9},{9,8},{10,11... | collective-permute-start | bytes 1572872 | tf_op jit(solution)/shard_map/ppermute | solution.py:28
  130.6 7.4 %collective-permute-start.29 = (bf16[128,512]{1,0:T(8,128)(2,1)S(1)}, bf16[128,512]{1,0:T(8,128)(2,1)S(1)}, u32[]{:S(2)}, u32[]{:S(2)}) collective-permute-start(bf16[128,512]{1,0:T(8,128)(2,1)S(1)} %get-tuple-element.90), channel_id=1, source_target_pairs={{0,4},{1,5},{2,6},{3,7},{4,0},{5,1},{6,2},{7,3},{8,12},{9,13},{10,... | collective-permute-start | bytes 393224 | tf_op jit(solution)/shard_map/ppermute | solution.py:28
  141.6 17.8 %collective-permute-start.34 = (bf16[256,4096]{1,0:T(8,128)(2,1)S(1)}, bf16[256,4096]{1,0:T(8,128)(2,1)S(1)}, u32[]{:S(2)}, u32[]{:S(2)}) collective-permute-start(bf16[256,4096]{1,0:T(8,128)(2,1)S(1)} %copy-done.30), channel_id=1, source_target_pairs={{0,1},{1,0},{2,3},{3,2},{4,5},{5,4},{6,7},{7,6},{8,9},{9,8},{10,11... | collective-permute-start | bytes 6291464 | tf_op jit(solution)/shard_map/ppermute | solution.py:28
  141.6 14.3 %collective-permute-start.35 = (bf16[256,1024]{1,0:T(8,128)(2,1)S(1)}, bf16[256,1024]{1,0:T(8,128)(2,1)S(1)}, u32[]{:S(2)}, u32[]{:S(2)}) collective-permute-start(bf16[256,1024]{1,0:T(8,128)(2,1)S(1)} %collective-permute-done.23.refs_12_), channel_id=1, source_target_pairs={{0,16},{16,0},{1,17},{17,1},{2,18},{18,2},{3,19},{19,3},{4,20},{20... | collective-permute-start | bytes 1572872 | tf_op jit(solution)/shard_map/ppermute | solution.py:45
  146.4 8.0 %collective-permute-start.32 = (bf16[128,512]{1,0:T(8,128)(2,1)S(1)}, bf16[128,512]{1,0:T(8,128)(2,1)S(1)}, u32[]{:S(2)}, u32[]{:S(2)}) collective-permute-start(bf16[128,512]{1,0:T(8,128)(2,1)S(1)} %get-tuple-element.97), channel_id=1, source_target_pairs={{0,4},{1,5},{2,6},{3,7},{4,0},{5,1},{6,2},{7,3},{8,12},{9,13},{10,... | collective-permute-start | bytes 393224 | tf_op jit(solution)/shard_map/ppermute | solution.py:28
  148.0 7.3 %collective-permute-start.31 = (bf16[128,512]{1,0:T(8,128)(2,1)S(1)}, bf16[128,512]{1,0:T(8,128)(2,1)S(1)}, u32[]{:S(2)}, u32[]{:S(2)}) collective-permute-start(bf16[128,512]{1,0:T(8,128)(2,1)S(1)} %get-tuple-element.96.refs_4_), channel_id=1, source_target_pairs={{0,2},{1,3},{2,0},{3,1},{4,6},{5,7},{6,4},{7,5},{8,10},{9,11},{10,... | collective-permute-start | bytes 393224 | tf_op jit(solution)/shard_map/ppermute | solution.py:28
  166.6 14.1 %collective-permute-start.39 = (bf16[128,2048]{1,0:T(8,128)(2,1)S(1)}, bf16[128,2048]{1,0:T(8,128)(2,1)}, u32[]{:S(2)}, u32[]{:S(2)}) collective-permute-start(bf16[128,2048]{1,0:T(8,128)(2,1)S(1)} %shard_map.87), channel_id=1, source_target_pairs={{0,2},{1,3},{2,0},{3,1},{4,6},{5,7},{6,4},{7,5},{8,10},{9,11},{10,... | collective-permute-start | bytes 1572872 | tf_op jit(solution)/shard_map/ppermute | solution.py:28
  (44 other events, 872.3 us)

commit v4 on v3

v4 whole, which is shorter than its diff:
```python
import functools
import math

import jax
import jax.numpy as jnp
from jax import lax
from jax.experimental import pallas as pl
from jax.experimental.pallas import tpu as pltpu
from jax.sharding import PartitionSpec as P

HD = 128
FR = 64
GROUP = 8
MB = 16
MEMF = 64
NORM_EPS = 1e-06
BF16 = jnp.bfloat16
F32 = jnp.float32
VMEM_BYTES = 32 * 2**20
WIDE_VMEM_BYTES = 58 * 2**20

CORE, NEAR, FAR = 1, 2, 4
CHIPS = (0, NEAR, FAR, NEAR | FAR)


def flip(value, bits):
    size = lax.axis_size("section")
    return lax.ppermute(value, "section", [(i, i ^ bits) for i in range(size)])


def hop(value):
    size = lax.axis_size("section")
    return lax.ppermute(value, "section", [(i, (i + GROUP) % size) for i in range(size)])


def after(value, *others):
    return lax.optimization_barrier((value, *others))[0]


def together(*values):
    return lax.optimization_barrier(values)


def across(value):
    return lax.ppermute(value, "groups", [(0, 1), (1, 0)])


def whole(count):
    return [pl.BlockSpec(memory_space=pltpu.VMEM)] * count


def dot(a, b):
    return jnp.dot(a, b, preferred_element_type=F32)


def keys_values_kernel(*refs):
    *mem_refs, key_own, val_own, pair_oth = refs[:7]
    earlier, out, rows = refs[7:-2], refs[-2], refs[-1]
    done = earlier[0].shape[0] if earlier else 0
    if earlier:
        out[:done, :] = earlier[0][...]
    for k, ref in enumerate(mem_refs):
        rows[k * MEMF:(k + 1) * MEMF, :] = ref[:MEMF]
    width = key_own.shape[1]
    weights = (key_own[...], pair_oth[:, :width], val_own[...], pair_oth[:, width:])
    for k, weight in enumerate(weights):
        out[done:, k * width:(k + 1) * width] = dot(rows[...], weight).astype(BF16)


def keys_values(pieces, weights, *earlier):
    depth, width = weights[0].shape
    rows = len(pieces) * MEMF
    total = rows + sum(part.shape[0] for part in earlier)
    return pl.pallas_call(
        keys_values_kernel,
        out_shape=jax.ShapeDtypeStruct((total, 4 * width), BF16),
        in_specs=whole(len(pieces) + 3 + len(earlier)),
        out_specs=pl.BlockSpec(memory_space=pltpu.VMEM),
        scratch_shapes=[pltpu.VMEM((rows, depth), BF16)],
        compiler_params=pltpu.CompilerParams(vmem_limit_bytes=VMEM_BYTES),
        cost_estimate=pl.CostEstimate(flops=0, bytes_accessed=0, transcendentals=0),
    )(*pieces, *weights, *earlier)


def attend_kernel(j, ring, *refs):
    mem_len, x0, x1, x2, x3, query_own, query_oth = refs[:7]
    kv_own, kv_oth = refs[7:9]
    outs, normed = refs[9:11], refs[11]
    width = query_own.shape[1]
    heads = 2 * width // HD
    me = lax.axis_index("section")
    section, slot, core = me // GROUP, me % GROUP, me % 2
    for k, ref in enumerate((x0, x1, x2, x3)):
        wide = ref[ref.shape[0] - FR:].astype(F32)
        scale = lax.rsqrt(jnp.mean(wide * wide, -1, keepdims=True) + NORM_EPS)
        normed[k * FR:(k + 1) * FR, :] = (wide * scale).astype(BF16)
    queries = jnp.concatenate(
        [dot(normed[...], query_own[...]), dot(normed[...], query_oth[...])], 1
    ).astype(BF16)
    is_own = (section + j) % 2 == core
    column = lax.broadcasted_iota(jnp.int32, (FR, MEMF), 1)
    scores, values = [], []
    for k, chip in enumerate(CHIPS):
        utt = (section + 2 * (slot ^ chip) + j) % MB
        place = (utt ^ me) >> 1 if ring else utt >> 1
        here = pl.ds(pl.multiple_of(place * MEMF, MEMF), MEMF)
        mine, other = kv_own[here, :], kv_oth[here, :]
        other = jnp.concatenate(
            [other[:, n * width:(n + 1) * width] for n in (1, 0, 3, 2)], 1
        )
        kv = jnp.where(is_own, mine, other)
        length = mem_len[utt]
        values.append(kv[:, 2 * width:])
        for h in range(heads):
            found = lax.dot_general(
                queries[k * FR:(k + 1) * FR, h * HD:(h + 1) * HD],
                kv[:, h * HD:(h + 1) * HD],
                (((1,), (1,)), ((), ())),
                preferred_element_type=F32,
            )
            found = found * (1.0 / math.sqrt(HD))
            scores.append(jnp.where(column < length, found, -jnp.inf))
    score = jnp.concatenate(scores, 0)
    expo = jnp.exp(score - jnp.max(score, -1, keepdims=True))
    probs = (expo / jnp.sum(expo, -1, keepdims=True)).astype(BF16)
    for k in range(4):
        for h in range(heads):
            at = (k * heads + h) * FR
            outs[k // 2][k % 2 * FR:(k % 2 + 1) * FR, h * HD:(h + 1) * HD] = dot(
                probs[at:at + FR], values[k][:, h * HD:(h + 1) * HD]
            ).astype(BF16)


def attend(j, ring, mem_len, pieces, weights, kv):
    depth, width = weights[0].shape
    return pl.pallas_call(
        functools.partial(attend_kernel, j, ring),
        out_shape=[jax.ShapeDtypeStruct((2 * FR, 2 * width), BF16)] * 2,
        in_specs=[pl.BlockSpec(memory_space=pltpu.SMEM)] + whole(8),
        out_specs=whole(2),
        scratch_shapes=[pltpu.VMEM((4 * FR, depth), BF16)],
        compiler_params=pltpu.CompilerParams(vmem_limit_bytes=VMEM_BYTES),
        cost_estimate=pl.CostEstimate(flops=0, bytes_accessed=0, transcendentals=0),
    )(mem_len, *pieces, *weights, *kv)


def project_kernel(near, place, tok_len, *refs):
    att, weights, x_refs, out = refs[:8], refs[8:16], refs[16:18], refs[18]
    me = lax.axis_index("section")
    width = weights[0].shape[0]
    slot = (me % GROUP) ^ (NEAR if near else 0)
    first_row = (me // GROUP) * MB + 2 * slot
    total = None
    for k in range(4):
        at = FR if near != (k % 2 == 1) else 0
        for n in range(2):
            rows = jnp.concatenate(
                [att[j * 4 + k][at:at + FR, n * width:(n + 1) * width] for j in range(2)], 0
            )
            term = dot(rows, weights[4 * n + k][...])
            total = term if total is None else total + term
    row = lax.broadcasted_iota(jnp.int32, (FR, total.shape[1]), 0)
    for j, x_ref in enumerate(x_refs):
        branch = jnp.where(row < tok_len[first_row + j], total[j * FR:(j + 1) * FR], 0.0)
        out[j * FR:(j + 1) * FR, :] = (x_ref[...].astype(F32) + branch).astype(BF16)


def project(near, place, tok_len, att, own, oth, pieces, x_first, x_last):
    width, depth = own.shape
    rows = 2 * FR
    tile = 512
    steps = pieces[0][0].shape[1] // tile

    def everywhere(i, place):
        return 0, place[0] * steps + i

    def here(i, place):
        return 0, i

    att_specs = [pl.BlockSpec((2 * FR, 2 * width), lambda i, place: (0, 0))] * 8
    full = pl.BlockSpec((width, tile), everywhere)
    parts = [
        pl.BlockSpec((width, tile), lambda i, place, block=block: (block, i)) for _, block in pieces
    ]
    x_specs = [
        pl.BlockSpec((FR, tile), lambda i, place, at=ref.shape[0] // FR - 1: (at, everywhere(i, place)[1]))
        for ref in (x_first, x_last)
    ]
    arrays = [array for array, _ in pieces]
    weights = [own, *arrays[:3], oth, *arrays[3:]]
    return pl.pallas_call(
        functools.partial(project_kernel, near),
        out_shape=jax.ShapeDtypeStruct((rows, steps * tile), BF16),
        grid_spec=pltpu.PrefetchScalarGridSpec(
            num_scalar_prefetch=1,
            grid=(steps,),
            in_specs=[pl.BlockSpec(memory_space=pltpu.SMEM)]
            + att_specs + [full, *parts[:3], full, *parts[3:]] + x_specs,
            out_specs=pl.BlockSpec((rows, tile), here),
        ),
        compiler_params=pltpu.CompilerParams(
            vmem_limit_bytes=WIDE_VMEM_BYTES, dimension_semantics=("arbitrary",)
        ),
        cost_estimate=pl.CostEstimate(flops=0, bytes_accessed=0, transcendentals=0),
    )(place, tok_len, *att, *weights, x_first, x_last)


def assemble_kernel(order, *refs):
    out = refs[-1]
    cols = refs[0].shape[1]
    for k, ref in enumerate(refs[:-1]):
        out[:, pl.ds(pl.multiple_of(order[k] * cols, 128), cols)] = ref[...]


def assemble(order, parts):
    rows, cols = parts[0].shape
    return pl.pallas_call(
        assemble_kernel,
        out_shape=jax.ShapeDtypeStruct((rows, len(parts) * cols), BF16),
        in_specs=[pl.BlockSpec(memory_space=pltpu.SMEM)] + whole(len(parts)),
        out_specs=pl.BlockSpec(memory_space=pltpu.VMEM),
        compiler_params=pltpu.CompilerParams(vmem_limit_bytes=VMEM_BYTES),
    )(order, *parts)


def shards(arriving, memory, w_query, w_key, w_value, w_out, tok_len, mem_len):
    me = lax.axis_index("section")
    size = lax.axis_size("section")
    group = lax.axis_index("groups")
    side = (me // NEAR) % 2
    depth = arriving.shape[1]
    ring = size == MB and memory.shape[0] == MEMF

    part_cols = depth // 4
    to_near = lax.dynamic_slice_in_dim(w_out, (2 * (1 - side) + group) * part_cols, part_cols, 1)
    to_far = lax.dynamic_slice_in_dim(w_out, (2 * side + group) * part_cols, part_cols, 1)
    if not ring:
        gathered = lax.all_gather(memory, "section", axis=0, tiled=True)
        gathered = gathered.reshape(MB // 2, 2, MEMF, depth)
        gathered = lax.dynamic_index_in_dim(gathered, me & 1, 1, keepdims=False)
        gathered = [gathered[k] for k in range(MB // 2)]

    out_near = flip(to_near, NEAR)
    out_core = flip(w_out, CORE)
    kv_pair = jnp.concatenate([w_key, w_value], 1)
    if ring:
        mem_hop, mem_near, mem_far = hop(memory), flip(memory, NEAR), flip(memory, FAR)
    else:
        mem_hop = mem_near = mem_far = out_near
    mem_hop, mem_near, mem_far, out_near, out_core, arriving, kv_pair = together(
        mem_hop, mem_near, mem_far, out_near, out_core, arriving, kv_pair
    )
    first_hop = hop(arriving[:FR])
    kv_pair = flip(kv_pair, CORE)
    if ring:
        hop_far, hop_near, mem_diag = flip(mem_hop, FAR), flip(mem_hop, NEAR), flip(mem_far, NEAR)
    else:
        hop_far = hop_near = mem_diag = mem_far
    first_hop, hop_far, hop_near, mem_diag, kv_pair, arriving, out_near = together(
        first_hop, hop_far, hop_near, mem_diag, kv_pair, arriving, out_near
    )
    kv_weights = [w_key, w_value, kv_pair]
    last_hop = hop(arriving[FR:])
    first_far, first_near = flip(first_hop, FAR), flip(first_hop, NEAR)
    hop_diag = flip(hop_far, NEAR) if ring else hop_far
    cross_near = across(out_near)
    mem_first = [memory, mem_near, mem_far, mem_diag] if ring else gathered[:4]
    kv_first = keys_values(mem_first, kv_weights)
    last_hop, first_far, first_near, hop_diag, cross_near, kv_first, to_far, w_query = together(
        last_hop, first_far, first_near, hop_diag, cross_near, kv_first, to_far, w_query
    )
    last_far, last_near, first_diag = flip(last_hop, FAR), flip(last_hop, NEAR), flip(first_far, NEAR)
    out_far = flip(to_far, FAR)
    query_oth = flip(w_query, CORE)
    mem_second = [mem_hop, hop_near, hop_far, hop_diag] if ring else gathered[4:]
    kv_second = keys_values(mem_second, kv_weights, kv_first)
    last_far, last_near, first_diag, out_far, query_oth, kv_second, out_near = together(
        last_far, last_near, first_diag, out_far, query_oth, kv_second, out_near
    )
    query_pair = [w_query, query_oth]
    last_diag = flip(last_far, NEAR)
    out_diag = flip(out_near, FAR)
    cross_far = across(out_far)
    kv = [kv_second, flip(kv_second, CORE)]
    first = [first_hop, first_near, first_far, first_diag]
    here, there = attend(0, ring, mem_len, first, query_pair, kv)
    att = [here, flip(here, NEAR), flip(there, FAR), flip(there, NEAR | FAR)]
    last_diag, out_diag, cross_far, *att[1:] = together(
        last_diag, out_diag, cross_far, *att[1:]
    )
    cross_diag = across(out_diag)
    direct_core = flip(jnp.concatenate([out_near, out_far, out_diag], 0), CORE)
    last = [last_hop, last_near, last_far, last_diag]
    here, there = attend(1, ring, mem_len, last, query_pair, kv)
    att += [here, flip(here, NEAR), flip(there, FAR), flip(there, NEAR | FAR)]
    crossed_core = flip(after(jnp.concatenate([cross_near, cross_far], 0), *att[5:]), CORE)
    fetched = [(out_near, 0), (out_far, 0), (out_diag, 0)] + [(direct_core, k) for k in range(3)]
    handed = [(cross_near, 0), (cross_far, 0), (cross_diag, 0)]
    handed += [(crossed_core, 0), (crossed_core, 1), (flip(after(cross_diag, *att[5:]), CORE), 0)]

    quarters = jnp.stack(
        [2 * side + group, 2 * side + 1 - group, 2 - 2 * side + group, 3 - 2 * side - group]
    ).astype(jnp.int32)
    def part(near, n, pieces, *others):
        at = 1 if near else 0
        return project(
            near, after(quarters[n:n + 1], *others), tok_len, att, w_out, out_core, pieces, first[at], last[at]
        )

    theirs_b = flip(part(True, 1, handed), NEAR)
    theirs_a = flip(part(True, 0, fetched), NEAR)
    mine = [part(False, 0, fetched), part(False, 1, handed)]
    return assemble(quarters, mine + [theirs_a, theirs_b])


def solution(mesh):
    return jax.shard_map(
        shards,
        mesh=mesh,
        in_specs=(
            P(("groups", "section"), None),
            P(("groups", "section"), None),
            P(None, "section"),
            P(None, "section"),
            P(None, "section"),
            P("section", None),
            P("groups"),
            P("groups"),
        ),
        out_specs=P(("groups", "section"), None),
        check_vma=False,
    )
```

time: 184 us -> 174 us (0.946)
  local copies, waits for them, and re-layouts: 16.3 us -> 5.36 us
  waiting for transfers between devices: 103 us -> 97.5 us
  Pallas kernels: 23.8 us -> 28.5 us
  other arithmetic: 2.49 us -> 4.43 us
    unnamed x72 -> x62, local copies, waits for them, and re-layouts: 12.7 us -> 4.02 us
    ppermute x3, waiting for transfers between devices: 44.9 us -> 39.1 us  [hop(): lax.ppermute(value, 'section', [(i, (i + GROUP) % size) for i in range(si...]
    pallas_call x2 -> x4, Pallas kernels: 10.2 us -> 15.7 us  [project(): pl.pallas_call(functools.partial(project_kernel, near), out_shape=jax.Sha...]
    concatenate x0 -> x3, other arithmetic: none -> 4.36 us  [the longest x1 2.04 us: shards(): kv_pair = jnp.concatenate([w_key, w_value], 1)]
    select_n x1 -> x0, other arithmetic: 2.41 us -> none  [shards(): jnp.where(side == 0, jnp.concatenate([mine, theirs], 1), jnp.concatenate(...]
    ppermute x34 -> x30, starting transfers between devices: 28.5 us -> 27.4 us  [flip(): return lax.ppermute(value, 'section', [(i, i ^ bits) for i in range(size)])]
    pallas_call x2 -> x3, Pallas kernels: 8.06 us -> 7.27 us  [the longest x2 5.69 us: keys_values(): pl.pallas_call(keys_values_kernel, out_shape=jax.ShapeDtypeStruct((total,...]
    ppermute x34 -> x30, waiting for transfers between devices: 57.7 us -> 58.4 us  [flip(): return lax.ppermute(value, 'section', [(i, i ^ bits) for i in range(size)])]
  transfers between devices with their start and end apart: 40 -> 36, of which waited for: 24 -> 13; matrix products, arithmetic and copies ran while one was open for 1% -> 3% of each run, Pallas kernels for 10% -> 15%
where the time goes in v4:
time: 174 us
  waiting for transfers between devices  97.5 us (56%)
  starting transfers between devices  38 us (22%)
  Pallas kernels  28.5 us (16%)
  local copies, waits for them, and re-layouts  5.36 us (3%)
  other arithmetic  4.43 us (3%)
    ppermute x30, waiting for transfers between devices, flip(): return lax.ppermute(value, 'section', [(i, i ^ bits) for i in range(size)])  58.4 us
    ppermute x3, waiting for transfers between devices, hop(): lax.ppermute(value, 'section', [(i, (i + GROUP) % size) for i in range(si...  39.1 us
    ppermute x30, starting transfers between devices, flip(): return lax.ppermute(value, 'section', [(i, i ^ bits) for i in range(size)])  27.4 us
    pallas_call x4, Pallas kernels, project(): pl.pallas_call(functools.partial(project_kernel, near), out_shape=jax.Sha...  15.7 us
    ppermute x3, starting transfers between devices, hop(): lax.ppermute(value, 'section', [(i, (i + GROUP) % size) for i in range(si...  6.09 us
    pallas_call x2, Pallas kernels, keys_values(): pl.pallas_call(keys_values_kernel, out_shape=jax.ShapeDtypeStruct((total,...  5.69 us
    pallas_call x2, Pallas kernels, attend(): pl.pallas_call(functools.partial(attend_kernel, j, ring), out_shape=[jax....  5.52 us
    ppermute x3, starting transfers between devices, across(): return lax.ppermute(value, 'groups', [(0, 1), (1, 0)])  4.47 us
  transfers between devices with their start and end apart: 36, of which 13 were waited for; matrix products, arithmetic and copies ran while one was open for 3% of the time, Pallas kernels for 15%

profile of v4, /device:TPU:0, one launch (start us, length us, event | category | flops | bytes accessed | tf_op | source)
XLA Modules:
  0.0 174.2 jit_solution(2192228017150565646)
XLA Ops:
  0.5 3.6 %collective-permute-start = (bf16[64,4096]{1,0:T(8,128)(2,1)}, bf16[64,4096]{1,0:T(8,128)(2,1)S(1)}, u32[]{:S(2)}, u32[]{:S(2)}) collective-permute-start(bf16[64,4096]{1,0:T(8,128)(2,1)} %refs_0_.3), channel_id=1, source_target_pairs={{0,8},{1,9},{2,10},{3,11},{4,12},{5,13},{6,14},{7,15},{8,0},{9,1},... | collective-permute-start | bytes 1572872 | tf_op jit(solution)/shard_map/ppermute | solution.py:33
  4.1 1.5 collective-permute-start.1
  5.6 1.6 collective-permute-start.2
  9.1 2.0 %pad_maximum_fusion = bf16[4096,512]{1,0:T(8,128)(2,1)S(1)} fusion(bf16[4096,256]{1,0:T(8,128)(2,1)} %refs_5_.3, bf16[4096,256]{1,0:T(8,128)(2,1)S(1)} %copy-done), kind=kLoop, calls=%fused_computation | loop fusion | flops 8388608 | bytes 8388608 | tf_op jit(solution)/shard_map/concatenate | solution.py:245
  11.1 18.4 %collective-permute-done.3.refs_9_ = bf16[256,1024]{1,0:T(8,128)(2,1)S(1)} collective-permute-done((bf16[256,1024]{1,0:T(8,128)(2,1)S(1)}, bf16[256,1024]{1,0:T(8,128)(2,1)S(1)}, u32[]{:S(2)}, u32[]{:S(2)}) %collective-permute-start.3) | collective-permute-done | bytes 524320 | tf_op jit(solution)/shard_map/ppermute | solution.py:28
  30.9 2.5 %collective-permute-start.6 = (bf16[64,4096]{1,0:T(8,128)(2,1)S(1)}, bf16[64,4096]{1,0:T(8,128)(2,1)S(1)}, u32[]{:S(2)}, u32[]{:S(2)}) collective-permute-start(bf16[64,4096]{1,0:T(8,128)(2,1)S(1)} %collective-permute-done.refs_0_), channel_id=1, source_target_pairs={{0,4},{1,5},{2,6},{3,7},{4,0},{5,1},{6,2},{7,3},{8,12},{9,13},{10,... | collective-permute-start | bytes 1572872 | tf_op jit(solution)/shard_map/ppermute | solution.py:28
  33.3 1.5 collective-permute-start.7
  35.4 21.7 %collective-permute-done.5.refs_1_.refs_16_ = bf16[64,4096]{1,0:T(8,128)(2,1)S(1)} collective-permute-done((bf16[64,4096]{1,0:T(8,128)(2,1)S(1)}, bf16[64,4096]{1,0:T(8,128)(2,1)S(1)}, u32[]{:S(2)}, u32[]{:S(2)}) %collective-permute-start.5) | collective-permute-done | bytes 524320 | tf_op jit(solution)/shard_map/ppermute | solution.py:33
  60.1 2.1 %collective-permute-start.10 = (bf16[64,4096]{1,0:T(8,128)(2,1)S(1)}, bf16[64,4096]{1,0:T(8,128)(2,1)S(1)}, u32[]{:S(2)}, u32[]{:S(2)}) collective-permute-start(bf16[64,4096]{1,0:T(8,128)(2,1)S(1)} %slice.7), channel_id=1, source_target_pairs={{0,8},{1,9},{2,10},{3,11},{4,12},{5,13},{6,14},{7,15},{8,0},{9,1},... | collective-permute-start | bytes 1572872 | tf_op jit(solution)/shard_map/ppermute | solution.py:33
  62.7 1.5 collective-permute-start.14
  64.2 3.4 %shard_map.82.refs_7_ = bf16[256,1024]{1,0:T(8,128)(2,1)S(1)} custom-call(bf16[64,4096]{1,0:T(8,128)(2,1)S(1)} %copy-done.13, bf16[64,4096]{1,0:T(8,128)(2,1)S(1)} %copy-done.15, bf16[64,4096]{1,0:T(8,128)(2,1)} %collective-permute-done.2.refs_2_, bf16[64,4096]{1,0:T(8,128)(2,1)S(1)} %collective-permute-done.8.refs_3_, bf16[4096,256]{1,0:T(8,128)(2,1)S(1)} %copy-done, ...), custom_call_target="tpu_custom_call" | custom-call | tf_op jit(solution)/shard_map/pallas_call | solution.py:74
  67.6 17.4 %collective-permute-done.10.refs_1_.refs_17_ = bf16[64,4096]{1,0:T(8,128)(2,1)S(1)} collective-permute-done((bf16[64,4096]{1,0:T(8,128)(2,1)S(1)}, bf16[64,4096]{1,0:T(8,128)(2,1)S(1)}, u32[]{:S(2)}, u32[]{:S(2)}) %collective-permute-start.10) | collective-permute-done | bytes 524320 | tf_op jit(solution)/shard_map/ppermute | solution.py:33
  87.3 1.9 %collective-permute-start.18 = (bf16[256,1024]{1,0:T(8,128)(2,1)S(1)}, bf16[256,1024]{1,0:T(8,128)(2,1)S(1)}, u32[]{:S(2)}, u32[]{:S(2)}) collective-permute-start(bf16[256,1024]{1,0:T(8,128)(2,1)S(1)} %get-tuple-element.61), channel_id=1, source_target_pairs={{0,4},{1,5},{2,6},{3,7},{4,0},{5,1},{6,2},{7,3},{8,12},{9,13},{10,... | collective-permute-start | bytes 1572872 | tf_op jit(solution)/shard_map/ppermute | solution.py:28
  89.2 2.3 %shard_map.83.refs_7_ = bf16[512,1024]{1,0:T(8,128)(2,1)S(1)} custom-call(bf16[64,4096]{1,0:T(8,128)(2,1)S(1)} %copy-done.12, bf16[64,4096]{1,0:T(8,128)(2,1)S(1)} %collective-permute-done.7.refs_1_, bf16[64,4096]{1,0:T(8,128)(2,1)S(1)} %collective-permute-done.6.refs_2_, bf16[64,4096]{1,0:T(8,128)(2,1)S(1)} %collective-permute-done.13.refs_3_, ...), custom_call_target="tpu_custom_call" | custom-call | tf_op jit(solution)/shard_map/pallas_call | solution.py:74
  91.6 8.3 %collective-permute-done.15.refs_3_ = bf16[64,4096]{1,0:T(8,128)(2,1)S(1)} collective-permute-done((bf16[64,4096]{1,0:T(8,128)(2,1)S(1)}, bf16[64,4096]{1,0:T(8,128)(2,1)S(1)}, u32[]{:S(2)}, u32[]{:S(2)}) %collective-permute-start.15) | collective-permute-done | bytes 524320 | tf_op jit(solution)/shard_map/ppermute | solution.py:28
  100.0 10.7 %collective-permute-done.17.refs_4_ = bf16[64,4096]{1,0:T(8,128)(2,1)S(1)} collective-permute-done((bf16[64,4096]{1,0:T(8,128)(2,1)S(1)}, bf16[64,4096]{1,0:T(8,128)(2,1)S(1)}, u32[]{:S(2)}, u32[]{:S(2)}) %collective-permute-start.17) | collective-permute-done | bytes 524320 | tf_op jit(solution)/shard_map/ppermute | solution.py:28
  111.5 1.8 %collective-permute-start.22 = (bf16[256,1024]{1,0:T(8,128)(2,1)S(1)}, bf16[256,1024]{1,0:T(8,128)(2,1)S(1)}, u32[]{:S(2)}, u32[]{:S(2)}) collective-permute-start(bf16[256,1024]{1,0:T(8,128)(2,1)S(1)} %collective-permute-done.3.refs_9_), channel_id=1, source_target_pairs={{0,4},{1,5},{2,6},{3,7},{4,0},{5,1},{6,2},{7,3},{8,12},{9,13},{10,... | collective-permute-start | bytes 1572872 | tf_op jit(solution)/shard_map/ppermute | solution.py:28
  113.2 1.5 collective-permute-start.23
  114.8 2.8 %shard_map.84 = (bf16[128,512]{1,0:T(8,128)(2,1)S(1)}, bf16[128,512]{1,0:T(8,128)(2,1)S(1)}) custom-call(s32[16]{0:T(128)S(1)} %copy-done.16, bf16[64,4096]{1,0:T(8,128)(2,1)S(1)} %collective-permute-done.5.refs_1_.refs_16_, bf16[64,4096]{1,0:T(8,128)(2,1)S(1)} %collective-permute-done.12.refs_2_.refs_16_, ...), custom_call_target="tpu_custom_call" | custom-call | tf_op jit(solution)/shard_map/pallas_call | solution.py:136
  119.2 6.3 %collective-permute-done.21.refs_4_ = bf16[64,4096]{1,0:T(8,128)(2,1)S(1)} collective-permute-done((bf16[64,4096]{1,0:T(8,128)(2,1)S(1)}, bf16[64,4096]{1,0:T(8,128)(2,1)S(1)}, u32[]{:S(2)}, u32[]{:S(2)}) %collective-permute-start.21) | collective-permute-done | bytes 524320 | tf_op jit(solution)/shard_map/ppermute | solution.py:28
  125.6 1.8 %collective-permute-start.26 = (bf16[128,512]{1,0:T(8,128)(2,1)S(1)}, bf16[128,512]{1,0:T(8,128)(2,1)S(1)}, u32[]{:S(2)}, u32[]{:S(2)}) collective-permute-start(bf16[128,512]{1,0:T(8,128)(2,1)S(1)} %get-tuple-element.73), channel_id=1, source_target_pairs={{0,6},{1,7},{2,4},{3,5},{4,2},{5,3},{6,0},{7,1},{8,14},{9,15},{10,... | collective-permute-start | bytes 393224 | tf_op jit(solution)/shard_map/ppermute | solution.py:28
  129.1 2.9 %collective-permute-done.26.refs_3_ = bf16[128,512]{1,0:T(8,128)(2,1)S(1)} collective-permute-done((bf16[128,512]{1,0:T(8,128)(2,1)S(1)}, bf16[128,512]{1,0:T(8,128)(2,1)S(1)}, u32[]{:S(2)}, u32[]{:S(2)}) %collective-permute-start.26) | collective-permute-done | bytes 131104 | tf_op jit(solution)/shard_map/ppermute | solution.py:28
  133.2 1.5 collective-permute-start.31
  134.7 2.8 %shard_map.85 = (bf16[128,512]{1,0:T(8,128)(2,1)S(1)}, bf16[128,512]{1,0:T(8,128)(2,1)S(1)}) custom-call(s32[16]{0:T(128)S(1)} %copy-done.16, bf16[64,4096]{1,0:T(8,128)(2,1)S(1)} %collective-permute-done.10.refs_1_.refs_17_, bf16[64,4096]{1,0:T(8,128)(2,1)S(1)} %collective-permute-done.16.refs_2_.refs_17_, ...), custom_call_target="tpu_custom_call" | custom-call | tf_op jit(solution)/shard_map/pallas_call | solution.py:136
  137.5 1.8 %collective-permute-start.28 = (bf16[128,512]{1,0:T(8,128)(2,1)S(1)}, bf16[128,512]{1,0:T(8,128)(2,1)S(1)}, u32[]{:S(2)}, u32[]{:S(2)}) collective-permute-start(bf16[128,512]{1,0:T(8,128)(2,1)S(1)} %get-tuple-element.80), channel_id=1, source_target_pairs={{0,4},{1,5},{2,6},{3,7},{4,0},{5,1},{6,2},{7,3},{8,12},{9,13},{10,... | collective-permute-start | bytes 393224 | tf_op jit(solution)/shard_map/ppermute | solution.py:28
  142.1 5.5 %collective-permute-done.27.refs_5_ = bf16[128,512]{1,0:T(8,128)(2,1)S(1)} collective-permute-done((bf16[128,512]{1,0:T(8,128)(2,1)S(1)}, bf16[128,512]{1,0:T(8,128)(2,1)S(1)}, u32[]{:S(2)}, u32[]{:S(2)}) %collective-permute-start.27) | collective-permute-done | bytes 131104 | tf_op jit(solution)/shard_map/ppermute | solution.py:28
  148.3 3.2 %collective-permute-done.33.refs_15_ = bf16[256,1024]{1,0:T(8,128)(2,1)} collective-permute-done((bf16[256,1024]{1,0:T(8,128)(2,1)}, bf16[256,1024]{1,0:T(8,128)(2,1)}, u32[]{:S(2)}, u32[]{:S(2)}) %collective-permute-start.33) | collective-permute-done | bytes 524320 | tf_op jit(solution)/shard_map/ppermute | solution.py:28
  152.5 3.9 %shard_map.89 = bf16[128,1024]{1,0:T(8,128)(2,1)} custom-call(s32[1]{0:T(128)} %bitcast.1.place, s32[32]{0:T(128)} %tok_len.7, bf16[128,512]{1,0:T(8,128)(2,1)} %copy-done.7, bf16[128,512]{1,0:T(8,128)(2,1)} %copy-done.24, bf16[128,512]{1,0:T(8,128)(2,1)} %copy-done.25, bf16[128,512]{1,0:T(8,128)(2,1)} %copy-done.26, bf16[128,512]{1,0:T(8,128)(2,1)} %copy-done.8, ...), custom_call_target="tpu_custom_call" | custom-call | tf_op jit(solution)/shard_map/pallas_call | solution.py:191
  159.0 3.9 %shard_map.88 = bf16[128,1024]{1,0:T(8,128)(2,1)} custom-call(s32[1]{0:T(128)} %bitcast.place, s32[32]{0:T(128)} %tok_len.7, bf16[128,512]{1,0:T(8,128)(2,1)} %copy-done.7, bf16[128,512]{1,0:T(8,128)(2,1)} %copy-done.24, bf16[128,512]{1,0:T(8,128)(2,1)} %copy-done.25, bf16[128,512]{1,0:T(8,128)(2,1)} %copy-done.26, bf16[128,512]{1,0:T(8,128)(2,1)} %copy-done.8, ...), custom_call_target="tpu_custom_call" | custom-call | tf_op jit(solution)/shard_map/pallas_call | solution.py:191
  163.8 3.9 %shard_map.87.refs_1_ = bf16[128,1024]{1,0:T(8,128)(2,1)} custom-call(s32[1]{0:T(128)} %bitcast.1.place, s32[32]{0:T(128)} %tok_len.7, bf16[128,512]{1,0:T(8,128)(2,1)} %copy-done.7, bf16[128,512]{1,0:T(8,128)(2,1)} %copy-done.24, bf16[128,512]{1,0:T(8,128)(2,1)} %copy-done.25, bf16[128,512]{1,0:T(8,128)(2,1)} %copy-done.26, bf16[128,512]{1,0:T(8,128)(2,1)} %copy-done.8, ...), custom_call_target="tpu_custom_call" | custom-call | tf_op jit(solution)/shard_map/pallas_call | solution.py:191
  167.7 4.0 %shard_map.86.refs_0_ = bf16[128,1024]{1,0:T(8,128)(2,1)} custom-call(s32[1]{0:T(128)} %bitcast.place, s32[32]{0:T(128)} %tok_len.7, bf16[128,512]{1,0:T(8,128)(2,1)} %copy-done.7, bf16[128,512]{1,0:T(8,128)(2,1)} %copy-done.24, bf16[128,512]{1,0:T(8,128)(2,1)} %copy-done.25, bf16[128,512]{1,0:T(8,128)(2,1)} %copy-done.26, bf16[128,512]{1,0:T(8,128)(2,1)} %copy-done.8, ...), custom_call_target="tpu_custom_call" | custom-call | tf_op jit(solution)/shard_map/pallas_call | solution.py:191
  172.6 1.6 shard_map.90
  (118 shorter events, 24.2 us)
Async XLA Ops:
  0.0 30.4 %collective-permute-start.4 = (bf16[256,4096]{1,0:T(8,128)(2,1)}, bf16[256,4096]{1,0:T(8,128)(2,1)}, u32[]{:S(2)}, u32[]{:S(2)}) collective-permute-start(bf16[256,4096]{1,0:T(8,128)(2,1)} %refs_8_.7), channel_id=1, source_target_pairs={{0,1},{1,0},{2,3},{3,2},{4,5},{5,4},{6,7},{7,6},{8,9},{9,8},{10,11... | collective-permute-start | bytes 6291464 | tf_op jit(solution)/shard_map/ppermute | solution.py:28
  0.5 29.1 %collective-permute-start = (bf16[64,4096]{1,0:T(8,128)(2,1)}, bf16[64,4096]{1,0:T(8,128)(2,1)S(1)}, u32[]{:S(2)}, u32[]{:S(2)}) collective-permute-start(bf16[64,4096]{1,0:T(8,128)(2,1)} %refs_0_.3), channel_id=1, source_target_pairs={{0,8},{1,9},{2,10},{3,11},{4,12},{5,13},{6,14},{7,15},{8,0},{9,1},... | collective-permute-start | bytes 1572872 | tf_op jit(solution)/shard_map/ppermute | solution.py:33
  4.1 25.5 %collective-permute-start.1 = (bf16[64,4096]{1,0:T(8,128)(2,1)}, bf16[64,4096]{1,0:T(8,128)(2,1)S(1)}, u32[]{:S(2)}, u32[]{:S(2)}) collective-permute-start(bf16[64,4096]{1,0:T(8,128)(2,1)} %refs_0_.3), channel_id=1, source_target_pairs={{0,2},{1,3},{2,0},{3,1},{4,6},{5,7},{6,4},{7,5},{8,10},{9,11},{10,... | collective-permute-start | bytes 1572872 | tf_op jit(solution)/shard_map/ppermute | solution.py:28
  5.6 24.8 %collective-permute-start.2 = (bf16[64,4096]{1,0:T(8,128)(2,1)}, bf16[64,4096]{1,0:T(8,128)(2,1)}, u32[]{:S(2)}, u32[]{:S(2)}) collective-permute-start(bf16[64,4096]{1,0:T(8,128)(2,1)} %refs_0_.3), channel_id=1, source_target_pairs={{0,4},{1,5},{2,6},{3,7},{4,0},{5,1},{6,2},{7,3},{8,12},{9,13},{10,... | collective-permute-start | bytes 1572872 | tf_op jit(solution)/shard_map/ppermute | solution.py:28
  8.5 21.1 %collective-permute-start.3 = (bf16[256,1024]{1,0:T(8,128)(2,1)S(1)}, bf16[256,1024]{1,0:T(8,128)(2,1)S(1)}, u32[]{:S(2)}, u32[]{:S(2)}) collective-permute-start(bf16[256,1024]{1,0:T(8,128)(2,1)S(1)} %get-tuple-element.88), channel_id=1, source_target_pairs={{0,2},{1,3},{2,0},{3,1},{4,6},{5,7},{6,4},{7,5},{8,10},{9,11},{10,... | collective-permute-start | bytes 1572872 | tf_op jit(solution)/shard_map/ppermute | solution.py:28
  30.4 27.9 %collective-permute-start.9 = (bf16[4096,512]{1,0:T(8,128)(2,1)S(1)}, bf16[4096,512]{1,0:T(8,128)(2,1)S(1)}, u32[]{:S(2)}, u32[]{:S(2)}) collective-permute-start(bf16[4096,512]{1,0:T(8,128)(2,1)S(1)} %pad_maximum_fusion), channel_id=1, source_target_pairs={{0,1},{1,0},{2,3},{3,2},{4,5},{5,4},{6,7},{7,6},{8,9},{9,8},{10,11... | collective-permute-start | bytes 12582920 | tf_op jit(solution)/shard_map/ppermute | solution.py:28
  30.5 26.6 %collective-permute-start.5 = (bf16[64,4096]{1,0:T(8,128)(2,1)S(1)}, bf16[64,4096]{1,0:T(8,128)(2,1)S(1)}, u32[]{:S(2)}, u32[]{:S(2)}) collective-permute-start(bf16[64,4096]{1,0:T(8,128)(2,1)S(1)} %slice.6), channel_id=1, source_target_pairs={{0,8},{1,9},{2,10},{3,11},{4,12},{5,13},{6,14},{7,15},{8,0},{9,1},... | collective-permute-start | bytes 1572872 | tf_op jit(solution)/shard_map/ppermute | solution.py:33
  30.9 26.2 %collective-permute-start.6 = (bf16[64,4096]{1,0:T(8,128)(2,1)S(1)}, bf16[64,4096]{1,0:T(8,128)(2,1)S(1)}, u32[]{:S(2)}, u32[]{:S(2)}) collective-permute-start(bf16[64,4096]{1,0:T(8,128)(2,1)S(1)} %collective-permute-done.refs_0_), channel_id=1, source_target_pairs={{0,4},{1,5},{2,6},{3,7},{4,0},{5,1},{6,2},{7,3},{8,12},{9,13},{10,... | collective-permute-start | bytes 1572872 | tf_op jit(solution)/shard_map/ppermute | solution.py:28
  33.3 23.8 %collective-permute-start.7 = (bf16[64,4096]{1,0:T(8,128)(2,1)S(1)}, bf16[64,4096]{1,0:T(8,128)(2,1)S(1)}, u32[]{:S(2)}, u32[]{:S(2)}) collective-permute-start(bf16[64,4096]{1,0:T(8,128)(2,1)S(1)} %collective-permute-done.refs_0_), channel_id=1, source_target_pairs={{0,2},{1,3},{2,0},{3,1},{4,6},{5,7},{6,4},{7,5},{8,10},{9,11},{10,... | collective-permute-start | bytes 1572872 | tf_op jit(solution)/shard_map/ppermute | solution.py:28
  34.8 23.5 %collective-permute-start.8 = (bf16[64,4096]{1,0:T(8,128)(2,1)}, bf16[64,4096]{1,0:T(8,128)(2,1)S(1)}, u32[]{:S(2)}, u32[]{:S(2)}) collective-permute-start(bf16[64,4096]{1,0:T(8,128)(2,1)} %collective-permute-done.2.refs_2_), channel_id=1, source_target_pairs={{0,2},{1,3},{2,0},{3,1},{4,6},{5,7},{6,4},{7,5},{8,10},{9,11},{10,... | collective-permute-start | bytes 1572872 | tf_op jit(solution)/shard_map/ppermute | solution.py:28
  58.3 26.6 %collective-permute-start.11 = (bf16[64,4096]{1,0:T(8,128)(2,1)S(1)}, bf16[64,4096]{1,0:T(8,128)(2,1)S(1)}, u32[]{:S(2)}, u32[]{:S(2)}) collective-permute-start(bf16[64,4096]{1,0:T(8,128)(2,1)S(1)} %collective-permute-done.5.refs_1_.refs_16_), channel_id=1, source_target_pairs={{0,4},{1,5},{2,6},{3,7},{4,0},{5,1},{6,2},{7,3},{8,12},{9,13},{10,... | collective-permute-start | bytes 1572872 | tf_op jit(solution)/shard_map/ppermute | solution.py:28
  58.6 26.3 %collective-permute-start.12 = (bf16[64,4096]{1,0:T(8,128)(2,1)S(1)}, bf16[64,4096]{1,0:T(8,128)(2,1)S(1)}, u32[]{:S(2)}, u32[]{:S(2)}) collective-permute-start(bf16[64,4096]{1,0:T(8,128)(2,1)S(1)} %collective-permute-done.5.refs_1_.refs_16_), channel_id=1, source_target_pairs={{0,2},{1,3},{2,0},{3,1},{4,6},{5,7},{6,4},{7,5},{8,10},{9,11},{10,... | collective-permute-start | bytes 1572872 | tf_op jit(solution)/shard_map/ppermute | solution.py:28
  60.1 24.9 %collective-permute-start.10 = (bf16[64,4096]{1,0:T(8,128)(2,1)S(1)}, bf16[64,4096]{1,0:T(8,128)(2,1)S(1)}, u32[]{:S(2)}, u32[]{:S(2)}) collective-permute-start(bf16[64,4096]{1,0:T(8,128)(2,1)S(1)} %slice.7), channel_id=1, source_target_pairs={{0,8},{1,9},{2,10},{3,11},{4,12},{5,13},{6,14},{7,15},{8,0},{9,1},... | collective-permute-start | bytes 1572872 | tf_op jit(solution)/shard_map/ppermute | solution.py:33
  62.2 22.8 %collective-permute-start.13 = (bf16[64,4096]{1,0:T(8,128)(2,1)S(1)}, bf16[64,4096]{1,0:T(8,128)(2,1)S(1)}, u32[]{:S(2)}, u32[]{:S(2)}) collective-permute-start(bf16[64,4096]{1,0:T(8,128)(2,1)S(1)} %collective-permute-done.6.refs_2_), channel_id=1, source_target_pairs={{0,2},{1,3},{2,0},{3,1},{4,6},{5,7},{6,4},{7,5},{8,10},{9,11},{10,... | collective-permute-start | bytes 1572872 | tf_op jit(solution)/shard_map/ppermute | solution.py:28
  62.7 22.3 %collective-permute-start.14 = (bf16[256,1024]{1,0:T(8,128)(2,1)S(1)}, bf16[256,1024]{1,0:T(8,128)(2,1)S(1)}, u32[]{:S(2)}, u32[]{:S(2)}) collective-permute-start(bf16[256,1024]{1,0:T(8,128)(2,1)S(1)} %collective-permute-done.3.refs_9_), channel_id=1, source_target_pairs={{0,16},{16,0},{1,17},{17,1},{2,18},{18,2},{3,19},{19,3},{4,20},{20... | collective-permute-start | bytes 1572872 | tf_op jit(solution)/shard_map/ppermute | solution.py:45
  85.0 25.7 %collective-permute-start.19 = (bf16[4096,256]{1,0:T(8,128)(2,1)S(1)}, bf16[4096,256]{1,0:T(8,128)(2,1)S(1)}, u32[]{:S(2)}, u32[]{:S(2)}) collective-permute-start(bf16[4096,256]{1,0:T(8,128)(2,1)S(1)} %copy-done.2), channel_id=1, source_target_pairs={{0,1},{1,0},{2,3},{3,2},{4,5},{5,4},{6,7},{7,6},{8,9},{9,8},{10,11... | collective-permute-start | bytes 6291464 | tf_op jit(solution)/shard_map/ppermute | solution.py:28
  85.1 14.8 %collective-permute-start.15 = (bf16[64,4096]{1,0:T(8,128)(2,1)S(1)}, bf16[64,4096]{1,0:T(8,128)(2,1)S(1)}, u32[]{:S(2)}, u32[]{:S(2)}) collective-permute-start(bf16[64,4096]{1,0:T(8,128)(2,1)S(1)} %collective-permute-done.10.refs_1_.refs_17_), channel_id=1, source_target_pairs={{0,4},{1,5},{2,6},{3,7},{4,0},{5,1},{6,2},{7,3},{8,12},{9,13},{10,... | collective-permute-start | bytes 1572872 | tf_op jit(solution)/shard_map/ppermute | solution.py:28
  85.2 14.8 %collective-permute-start.16 = (bf16[64,4096]{1,0:T(8,128)(2,1)S(1)}, bf16[64,4096]{1,0:T(8,128)(2,1)S(1)}, u32[]{:S(2)}, u32[]{:S(2)}) collective-permute-start(bf16[64,4096]{1,0:T(8,128)(2,1)S(1)} %collective-permute-done.10.refs_1_.refs_17_), channel_id=1, source_target_pairs={{0,2},{1,3},{2,0},{3,1},{4,6},{5,7},{6,4},{7,5},{8,10},{9,11},{10,... | collective-permute-start | bytes 1572872 | tf_op jit(solution)/shard_map/ppermute | solution.py:28
  86.1 24.6 %collective-permute-start.17 = (bf16[64,4096]{1,0:T(8,128)(2,1)S(1)}, bf16[64,4096]{1,0:T(8,128)(2,1)S(1)}, u32[]{:S(2)}, u32[]{:S(2)}) collective-permute-start(bf16[64,4096]{1,0:T(8,128)(2,1)S(1)} %collective-permute-done.11.refs_3_), channel_id=1, source_target_pairs={{0,2},{1,3},{2,0},{3,1},{4,6},{5,7},{6,4},{7,5},{8,10},{9,11},{10,... | collective-permute-start | bytes 1572872 | tf_op jit(solution)/shard_map/ppermute | solution.py:28
  87.3 23.4 %collective-permute-start.18 = (bf16[256,1024]{1,0:T(8,128)(2,1)S(1)}, bf16[256,1024]{1,0:T(8,128)(2,1)S(1)}, u32[]{:S(2)}, u32[]{:S(2)}) collective-permute-start(bf16[256,1024]{1,0:T(8,128)(2,1)S(1)} %get-tuple-element.61), channel_id=1, source_target_pairs={{0,4},{1,5},{2,6},{3,7},{4,0},{5,1},{6,2},{7,3},{8,12},{9,13},{10,... | collective-permute-start | bytes 1572872 | tf_op jit(solution)/shard_map/ppermute | solution.py:28
  110.8 14.8 %collective-permute-start.21 = (bf16[64,4096]{1,0:T(8,128)(2,1)S(1)}, bf16[64,4096]{1,0:T(8,128)(2,1)S(1)}, u32[]{:S(2)}, u32[]{:S(2)}) collective-permute-start(bf16[64,4096]{1,0:T(8,128)(2,1)S(1)} %collective-permute-done.15.refs_3_), channel_id=1, source_target_pairs={{0,2},{1,3},{2,0},{3,1},{4,6},{5,7},{6,4},{7,5},{8,10},{9,11},{10,... | collective-permute-start | bytes 1572872 | tf_op jit(solution)/shard_map/ppermute | solution.py:28
  111.5 15.9 %collective-permute-start.22 = (bf16[256,1024]{1,0:T(8,128)(2,1)S(1)}, bf16[256,1024]{1,0:T(8,128)(2,1)S(1)}, u32[]{:S(2)}, u32[]{:S(2)}) collective-permute-start(bf16[256,1024]{1,0:T(8,128)(2,1)S(1)} %collective-permute-done.3.refs_9_), channel_id=1, source_target_pairs={{0,4},{1,5},{2,6},{3,7},{4,0},{5,1},{6,2},{7,3},{8,12},{9,13},{10,... | collective-permute-start | bytes 1572872 | tf_op jit(solution)/shard_map/ppermute | solution.py:28
  113.2 14.2 %collective-permute-start.23 = (bf16[256,1024]{1,0:T(8,128)(2,1)S(1)}, bf16[256,1024]{1,0:T(8,128)(2,1)S(1)}, u32[]{:S(2)}, u32[]{:S(2)}) collective-permute-start(bf16[256,1024]{1,0:T(8,128)(2,1)S(1)} %collective-permute-done.18.refs_10_), channel_id=1, source_target_pairs={{0,16},{16,0},{1,17},{17,1},{2,18},{18,2},{3,19},{19,3},{4,20},{20... | collective-permute-start | bytes 1572872 | tf_op jit(solution)/shard_map/ppermute | solution.py:45
  117.5 10.4 %collective-permute-start.24 = (bf16[128,512]{1,0:T(8,128)(2,1)S(1)}, bf16[128,512]{1,0:T(8,128)(2,1)S(1)}, u32[]{:S(2)}, u32[]{:S(2)}) collective-permute-start(bf16[128,512]{1,0:T(8,128)(2,1)S(1)} %get-tuple-element.69.refs_0_), channel_id=1, source_target_pairs={{0,2},{1,3},{2,0},{3,1},{4,6},{5,7},{6,4},{7,5},{8,10},{9,11},{10,... | collective-permute-start | bytes 393224 | tf_op jit(solution)/shard_map/ppermute | solution.py:28
  119.0 10.1 %collective-permute-start.25 = (bf16[128,512]{1,0:T(8,128)(2,1)S(1)}, bf16[128,512]{1,0:T(8,128)(2,1)S(1)}, u32[]{:S(2)}, u32[]{:S(2)}) collective-permute-start(bf16[128,512]{1,0:T(8,128)(2,1)S(1)} %get-tuple-element.73), channel_id=1, source_target_pairs={{0,4},{1,5},{2,6},{3,7},{4,0},{5,1},{6,2},{7,3},{8,12},{9,13},{10,... | collective-permute-start | bytes 393224 | tf_op jit(solution)/shard_map/ppermute | solution.py:28
  133.2 24.7 %collective-permute-start.30 = (bf16[768,1024]{1,0:T(8,128)(2,1)}, bf16[768,1024]{1,0:T(8,128)(2,1)S(1)}, u32[]{:S(2)}, u32[]{:S(2)}) collective-permute-start(bf16[768,1024]{1,0:T(8,128)(2,1)} %pad_maximum_fusion.1), channel_id=1, source_target_pairs={{0,1},{1,0},{2,3},{3,2},{4,5},{5,4},{6,7},{7,6},{8,9},{9,8},{10,11... | collective-permute-start | bytes 4718600 | tf_op jit(solution)/shard_map/ppermute | solution.py:28
  133.2 14.6 %collective-permute-start.31 = (bf16[256,1024]{1,0:T(8,128)(2,1)S(1)}, bf16[256,1024]{1,0:T(8,128)(2,1)}, u32[]{:S(2)}, u32[]{:S(2)}) collective-permute-start(bf16[256,1024]{1,0:T(8,128)(2,1)S(1)} %collective-permute-done.22.refs_11_), channel_id=1, source_target_pairs={{0,16},{16,0},{1,17},{17,1},{2,18},{18,2},{3,19},{19,3},{4,20},{20... | collective-permute-start | bytes 1572872 | tf_op jit(solution)/shard_map/ppermute | solution.py:45
  137.5 10.1 %collective-permute-start.28 = (bf16[128,512]{1,0:T(8,128)(2,1)S(1)}, bf16[128,512]{1,0:T(8,128)(2,1)S(1)}, u32[]{:S(2)}, u32[]{:S(2)}) collective-permute-start(bf16[128,512]{1,0:T(8,128)(2,1)S(1)} %get-tuple-element.80), channel_id=1, source_target_pairs={{0,4},{1,5},{2,6},{3,7},{4,0},{5,1},{6,2},{7,3},{8,12},{9,13},{10,... | collective-permute-start | bytes 393224 | tf_op jit(solution)/shard_map/ppermute | solution.py:28
  139.3 8.3 %collective-permute-start.29 = (bf16[128,512]{1,0:T(8,128)(2,1)S(1)}, bf16[128,512]{1,0:T(8,128)(2,1)S(1)}, u32[]{:S(2)}, u32[]{:S(2)}) collective-permute-start(bf16[128,512]{1,0:T(8,128)(2,1)S(1)} %get-tuple-element.80), channel_id=1, source_target_pairs={{0,6},{1,7},{2,4},{3,5},{4,2},{5,3},{6,0},{7,1},{8,14},{9,15},{10,... | collective-permute-start | bytes 393224 | tf_op jit(solution)/shard_map/ppermute | solution.py:28
  139.7 8.0 %collective-permute-start.27 = (bf16[128,512]{1,0:T(8,128)(2,1)S(1)}, bf16[128,512]{1,0:T(8,128)(2,1)S(1)}, u32[]{:S(2)}, u32[]{:S(2)}) collective-permute-start(bf16[128,512]{1,0:T(8,128)(2,1)S(1)} %get-tuple-element.79.refs_4_), channel_id=1, source_target_pairs={{0,2},{1,3},{2,0},{3,1},{4,6},{5,7},{6,4},{7,5},{8,10},{9,11},{10,... | collective-permute-start | bytes 393224 | tf_op jit(solution)/shard_map/ppermute | solution.py:28
  156.4 15.2 %collective-permute-start.35 = (bf16[128,1024]{1,0:T(8,128)(2,1)}, bf16[128,1024]{1,0:T(8,128)(2,1)S(1)}, u32[]{:S(2)}, u32[]{:S(2)}) collective-permute-start(bf16[128,1024]{1,0:T(8,128)(2,1)} %shard_map.89), channel_id=1, source_target_pairs={{0,2},{1,3},{2,0},{3,1},{4,6},{5,7},{6,4},{7,5},{8,10},{9,11},{10,... | collective-permute-start | bytes 786440 | tf_op jit(solution)/shard_map/ppermute | solution.py:28
  163.0 8.7 %collective-permute-start.34 = (bf16[128,1024]{1,0:T(8,128)(2,1)}, bf16[128,1024]{1,0:T(8,128)(2,1)S(1)}, u32[]{:S(2)}, u32[]{:S(2)}) collective-permute-start(bf16[128,1024]{1,0:T(8,128)(2,1)} %shard_map.88), channel_id=1, source_target_pairs={{0,2},{1,3},{2,0},{3,1},{4,6},{5,7},{6,4},{7,5},{8,10},{9,11},{10,... | collective-permute-start | bytes 786440 | tf_op jit(solution)/shard_map/ppermute | solution.py:28
  (35 other events, 753.4 us)

commit v5 on v4

--- a/solution.py
+++ b/solution.py
@@ -17,7 +17,7 @@
 BF16 = jnp.bfloat16
 F32 = jnp.float32
 VMEM_BYTES = 32 * 2**20
-WIDE_VMEM_BYTES = 58 * 2**20
+WIDE_VMEM_BYTES = 52 * 2**20
 
 CORE, NEAR, FAR = 1, 2, 4
 CHIPS = (0, NEAR, FAR, NEAR | FAR)
@@ -145,20 +145,24 @@
 
 
 def project_kernel(near, place, tok_len, *refs):
-    att, weights, x_refs, out = refs[:8], refs[8:16], refs[16:18], refs[18]
+    att, weights, x_refs, out = refs[:8], refs[8:-3], refs[-3:-1], refs[-1]
     me = lax.axis_index("section")
-    width = weights[0].shape[0]
     slot = (me % GROUP) ^ (NEAR if near else 0)
     first_row = (me // GROUP) * MB + 2 * slot
-    total = None
-    for k in range(4):
-        at = FR if near != (k % 2 == 1) else 0
-        for n in range(2):
-            rows = jnp.concatenate(
+    width = att[0].shape[1] // 2
+    columns = []
+    for n in range(2):
+        for k in range(4):
+            at = FR if near != (k % 2 == 1) else 0
+            columns.append(jnp.concatenate(
                 [att[j * 4 + k][at:at + FR, n * width:(n + 1) * width] for j in range(2)], 0
-            )
-            term = dot(rows, weights[4 * n + k][...])
-            total = term if total is None else total + term
+            ))
+    total, done = None, 0
+    for weight in weights:
+        count = weight.shape[0] // width
+        term = dot(jnp.concatenate(columns[done:done + count], 1), weight[...])
+        total = term if total is None else total + term
+        done += count
     row = lax.broadcasted_iota(jnp.int32, (FR, total.shape[1]), 0)
     for j, x_ref in enumerate(x_refs):
         branch = jnp.where(row < tok_len[first_row + j], total[j * FR:(j + 1) * FR], 0.0)
@@ -169,7 +173,8 @@
     width, depth = own.shape
     rows = 2 * FR
     tile = 512
-    steps = pieces[0][0].shape[1] // tile
+    cols = pieces[0][0].shape[1]
+    steps = cols // tile
 
     def everywhere(i, place):
         return 0, place[0] * steps + i
@@ -178,24 +183,22 @@
         return 0, i
 
     att_specs = [pl.BlockSpec((2 * FR, 2 * width), lambda i, place: (0, 0))] * 8
-    full = pl.BlockSpec((width, tile), everywhere)
-    parts = [
-        pl.BlockSpec((width, tile), lambda i, place, block=block: (block, i)) for _, block in pieces
-    ]
+    weights, weight_specs = [], []
+    for mine, others in zip((own, oth), pieces):
+        weights += [mine, *others]
+        weight_specs.append(pl.BlockSpec((width, tile), everywhere))
+        weight_specs += [pl.BlockSpec((other.shape[0], tile), here) for other in others]
     x_specs = [
         pl.BlockSpec((FR, tile), lambda i, place, at=ref.shape[0] // FR - 1: (at, everywhere(i, place)[1]))
         for ref in (x_first, x_last)
     ]
-    arrays = [array for array, _ in pieces]
-    weights = [own, *arrays[:3], oth, *arrays[3:]]
     return pl.pallas_call(
         functools.partial(project_kernel, near),
-        out_shape=jax.ShapeDtypeStruct((rows, steps * tile), BF16),
+        out_shape=jax.ShapeDtypeStruct((rows, cols), BF16),
         grid_spec=pltpu.PrefetchScalarGridSpec(
             num_scalar_prefetch=1,
             grid=(steps,),
-            in_specs=[pl.BlockSpec(memory_space=pltpu.SMEM)]
-            + att_specs + [full, *parts[:3], full, *parts[3:]] + x_specs,
+            in_specs=[pl.BlockSpec(memory_space=pltpu.SMEM)] + att_specs + weight_specs + x_specs,
             out_specs=pl.BlockSpec((rows, tile), here),
         ),
         compiler_params=pltpu.CompilerParams(
@@ -285,19 +288,18 @@
     first = [first_hop, first_near, first_far, first_diag]
     here, there = attend(0, ring, mem_len, first, query_pair, kv)
     att = [here, flip(here, NEAR), flip(there, FAR), flip(there, NEAR | FAR)]
-    last_diag, out_diag, cross_far, *att[1:] = together(
-        last_diag, out_diag, cross_far, *att[1:]
+    last_diag, out_diag, cross_far, *att[1:3] = together(
+        last_diag, out_diag, cross_far, *att[1:3]
     )
     cross_diag = across(out_diag)
-    direct_core = flip(jnp.concatenate([out_near, out_far, out_diag], 0), CORE)
     last = [last_hop, last_near, last_far, last_diag]
     here, there = attend(1, ring, mem_len, last, query_pair, kv)
     att += [here, flip(here, NEAR), flip(there, FAR), flip(there, NEAR | FAR)]
-    crossed_core = flip(after(jnp.concatenate([cross_near, cross_far], 0), *att[5:]), CORE)
-    fetched = [(out_near, 0), (out_far, 0), (out_diag, 0)] + [(direct_core, k) for k in range(3)]
-    handed = [(cross_near, 0), (cross_far, 0), (cross_diag, 0)]
-    handed += [(crossed_core, 0), (crossed_core, 1), (flip(after(cross_diag, *att[5:]), CORE), 0)]
-
+    fetched = jnp.concatenate([out_near, out_far, out_diag], 0)
+    crossed = jnp.concatenate([cross_near, cross_far], 0)
+    fetched, crossed, cross_diag = together(fetched, crossed, cross_diag, att[3], *att[5:])[:3]
+    fetched = [[fetched], [flip(fetched, CORE)]]
+    handed = [[crossed, cross_diag], [flip(crossed, CORE), flip(cross_diag, CORE)]]
     quarters = jnp.stack(
         [2 * side + group, 2 * side + 1 - group, 2 - 2 * side + group, 3 - 2 * side - group]
     ).astype(jnp.int32)

time: 174 us -> 168 us (0.966)
  Pallas kernels: 28.5 us -> 23.5 us
  local copies, waits for them, and re-layouts: 5.36 us -> 2.24 us
  waiting for transfers between devices: 97.5 us -> 99.4 us
    pallas_call x4, Pallas kernels: 15.7 us -> 10.8 us  [project(): pl.pallas_call(functools.partial(project_kernel, near), out_shape=jax.Sha...]
    unnamed x62 -> x36, local copies, waits for them, and re-layouts: 4.02 us -> 0.9 us
  transfers between devices with their start and end apart: 36 -> 36, of which waited for: 13 -> 15; matrix products, arithmetic and copies ran while one was open for 3% -> 3% of each run, Pallas kernels for 15% -> 13%
where the time goes in v5:
time: 168 us
  waiting for transfers between devices  99.4 us (59%)
  starting transfers between devices  38.7 us (23%)
  Pallas kernels  23.5 us (14%)
  other arithmetic  3.45 us (2%)
  local copies, waits for them, and re-layouts  2.24 us (1%)
    ppermute x30, waiting for transfers between devices, flip(): return lax.ppermute(value, 'section', [(i, i ^ bits) for i in range(size)])  59.6 us
    ppermute x3, waiting for transfers between devices, hop(): lax.ppermute(value, 'section', [(i, (i + GROUP) % size) for i in range(si...  39.1 us
    ppermute x30, starting transfers between devices, flip(): return lax.ppermute(value, 'section', [(i, i ^ bits) for i in range(size)])  28.2 us
    pallas_call x4, Pallas kernels, project(): pl.pallas_call(functools.partial(project_kernel, near), out_shape=jax.Sha...  10.8 us
    ppermute x3, starting transfers between devices, hop(): lax.ppermute(value, 'section', [(i, (i + GROUP) % size) for i in range(si...  6.09 us
    pallas_call x2, Pallas kernels, keys_values(): pl.pallas_call(keys_values_kernel, out_shape=jax.ShapeDtypeStruct((total,...  5.69 us
    pallas_call x2, Pallas kernels, attend(): pl.pallas_call(functools.partial(attend_kernel, j, ring), out_shape=[jax....  5.51 us
    ppermute x3, starting transfers between devices, across(): return lax.ppermute(value, 'groups', [(0, 1), (1, 0)])  4.47 us
  transfers between devices with their start and end apart: 36, of which 15 were waited for; matrix products, arithmetic and copies ran while one was open for 3% of the time, Pallas kernels for 13%

profile of v5, /device:TPU:0, one launch (start us, length us, event | category | flops | bytes accessed | tf_op | source)
XLA Modules:
  0.0 167.7 jit_solution(5117486338756250189)
XLA Ops:
  0.5 3.6 %collective-permute-start = (bf16[64,4096]{1,0:T(8,128)(2,1)}, bf16[64,4096]{1,0:T(8,128)(2,1)S(1)}, u32[]{:S(2)}, u32[]{:S(2)}) collective-permute-start(bf16[64,4096]{1,0:T(8,128)(2,1)} %refs_0_.3), channel_id=1, source_target_pairs={{0,8},{1,9},{2,10},{3,11},{4,12},{5,13},{6,14},{7,15},{8,0},{9,1},... | collective-permute-start | bytes 1572872 | tf_op jit(solution)/shard_map/ppermute | solution.py:33
  4.1 1.5 collective-permute-start.1
  5.6 1.6 collective-permute-start.2
  9.1 2.0 %pad_maximum_fusion = bf16[4096,512]{1,0:T(8,128)(2,1)S(1)} fusion(bf16[4096,256]{1,0:T(8,128)(2,1)} %refs_5_.3, bf16[4096,256]{1,0:T(8,128)(2,1)S(1)} %copy-done), kind=kLoop, calls=%fused_computation | loop fusion | flops 8388608 | bytes 8388608 | tf_op jit(solution)/shard_map/concatenate | solution.py:248
  11.1 18.4 %collective-permute-done.3 = bf16[256,1024]{1,0:T(8,128)(2,1)S(1)} collective-permute-done((bf16[256,1024]{1,0:T(8,128)(2,1)S(1)}, bf16[256,1024]{1,0:T(8,128)(2,1)S(1)}, u32[]{:S(2)}, u32[]{:S(2)}) %collective-permute-start.3) | collective-permute-done | bytes 524320 | tf_op jit(solution)/shard_map/ppermute | solution.py:28
  30.9 2.5 %collective-permute-start.6 = (bf16[64,4096]{1,0:T(8,128)(2,1)S(1)}, bf16[64,4096]{1,0:T(8,128)(2,1)S(1)}, u32[]{:S(2)}, u32[]{:S(2)}) collective-permute-start(bf16[64,4096]{1,0:T(8,128)(2,1)S(1)} %collective-permute-done.refs_0_), channel_id=1, source_target_pairs={{0,4},{1,5},{2,6},{3,7},{4,0},{5,1},{6,2},{7,3},{8,12},{9,13},{10,... | collective-permute-start | bytes 1572872 | tf_op jit(solution)/shard_map/ppermute | solution.py:28
  33.3 1.5 collective-permute-start.7
  35.4 21.7 %collective-permute-done.5.refs_1_.refs_12_.refs_14_ = bf16[64,4096]{1,0:T(8,128)(2,1)S(1)} collective-permute-done((bf16[64,4096]{1,0:T(8,128)(2,1)S(1)}, bf16[64,4096]{1,0:T(8,128)(2,1)S(1)}, u32[]{:S(2)}, u32[]{:S(2)}) %collective-permute-start.5) | collective-permute-done | bytes 524320 | tf_op jit(solution)/shard_map/ppermute | solution.py:33
  60.1 2.1 %collective-permute-start.10 = (bf16[64,4096]{1,0:T(8,128)(2,1)S(1)}, bf16[64,4096]{1,0:T(8,128)(2,1)S(1)}, u32[]{:S(2)}, u32[]{:S(2)}) collective-permute-start(bf16[64,4096]{1,0:T(8,128)(2,1)S(1)} %slice.7), channel_id=1, source_target_pairs={{0,8},{1,9},{2,10},{3,11},{4,12},{5,13},{6,14},{7,15},{8,0},{9,1},... | collective-permute-start | bytes 1572872 | tf_op jit(solution)/shard_map/ppermute | solution.py:33
  62.7 1.5 collective-permute-start.14
  64.2 3.4 %shard_map.82.refs_7_ = bf16[256,1024]{1,0:T(8,128)(2,1)S(1)} custom-call(bf16[64,4096]{1,0:T(8,128)(2,1)S(1)} %copy-done.11, bf16[64,4096]{1,0:T(8,128)(2,1)S(1)} %copy-done.13, bf16[64,4096]{1,0:T(8,128)(2,1)} %collective-permute-done.2.refs_2_, bf16[64,4096]{1,0:T(8,128)(2,1)S(1)} %collective-permute-done.8.refs_3_, bf16[4096,256]{1,0:T(8,128)(2,1)S(1)} %copy-done, ...), custom_call_target="tpu_custom_call" | custom-call | tf_op jit(solution)/shard_map/pallas_call | solution.py:74
  67.6 17.4 %collective-permute-done.10.refs_1_.refs_13_.refs_15_ = bf16[64,4096]{1,0:T(8,128)(2,1)S(1)} collective-permute-done((bf16[64,4096]{1,0:T(8,128)(2,1)S(1)}, bf16[64,4096]{1,0:T(8,128)(2,1)S(1)}, u32[]{:S(2)}, u32[]{:S(2)}) %collective-permute-start.10) | collective-permute-done | bytes 524320 | tf_op jit(solution)/shard_map/ppermute | solution.py:33
  87.3 1.9 %collective-permute-start.18 = (bf16[256,1024]{1,0:T(8,128)(2,1)S(1)}, bf16[256,1024]{1,0:T(8,128)(2,1)S(1)}, u32[]{:S(2)}, u32[]{:S(2)}) collective-permute-start(bf16[256,1024]{1,0:T(8,128)(2,1)S(1)} %get-tuple-element.61), channel_id=1, source_target_pairs={{0,4},{1,5},{2,6},{3,7},{4,0},{5,1},{6,2},{7,3},{8,12},{9,13},{10,... | collective-permute-start | bytes 1572872 | tf_op jit(solution)/shard_map/ppermute | solution.py:28
  89.2 2.3 %shard_map.83.refs_7_ = bf16[512,1024]{1,0:T(8,128)(2,1)S(1)} custom-call(bf16[64,4096]{1,0:T(8,128)(2,1)S(1)} %copy-done.10, bf16[64,4096]{1,0:T(8,128)(2,1)S(1)} %collective-permute-done.7.refs_1_, bf16[64,4096]{1,0:T(8,128)(2,1)S(1)} %collective-permute-done.6.refs_2_, bf16[64,4096]{1,0:T(8,128)(2,1)S(1)} %collective-permute-done.13.refs_3_, ...), custom_call_target="tpu_custom_call" | custom-call | tf_op jit(solution)/shard_map/pallas_call | solution.py:74
  91.5 8.3 %collective-permute-done.15.refs_3_ = bf16[64,4096]{1,0:T(8,128)(2,1)S(1)} collective-permute-done((bf16[64,4096]{1,0:T(8,128)(2,1)S(1)}, bf16[64,4096]{1,0:T(8,128)(2,1)S(1)}, u32[]{:S(2)}, u32[]{:S(2)}) %collective-permute-start.15) | collective-permute-done | bytes 524320 | tf_op jit(solution)/shard_map/ppermute | solution.py:28
  100.0 10.7 %collective-permute-done.17.refs_4_ = bf16[64,4096]{1,0:T(8,128)(2,1)S(1)} collective-permute-done((bf16[64,4096]{1,0:T(8,128)(2,1)S(1)}, bf16[64,4096]{1,0:T(8,128)(2,1)S(1)}, u32[]{:S(2)}, u32[]{:S(2)}) %collective-permute-start.17) | collective-permute-done | bytes 524320 | tf_op jit(solution)/shard_map/ppermute | solution.py:28
  111.4 1.8 %collective-permute-start.22 = (bf16[256,1024]{1,0:T(8,128)(2,1)S(1)}, bf16[256,1024]{1,0:T(8,128)(2,1)S(1)}, u32[]{:S(2)}, u32[]{:S(2)}) collective-permute-start(bf16[256,1024]{1,0:T(8,128)(2,1)S(1)} %collective-permute-done.3), channel_id=1, source_target_pairs={{0,4},{1,5},{2,6},{3,7},{4,0},{5,1},{6,2},{7,3},{8,12},{9,13},{10,... | collective-permute-start | bytes 1572872 | tf_op jit(solution)/shard_map/ppermute | solution.py:28
  113.2 1.5 collective-permute-start.23
  114.7 2.8 %shard_map.84 = (bf16[128,512]{1,0:T(8,128)(2,1)S(1)}, bf16[128,512]{1,0:T(8,128)(2,1)S(1)}) custom-call(s32[16]{0:T(128)S(1)} %copy-done.15, bf16[64,4096]{1,0:T(8,128)(2,1)S(1)} %collective-permute-done.5.refs_1_.refs_12_.refs_14_, bf16[64,4096]{1,0:T(8,128)(2,1)S(1)} %collective-permute-done.12.refs_2_.refs_12_.refs_14_, ...), custom_call_target="tpu_custom_call" | custom-call | tf_op jit(solution)/shard_map/pallas_call | solution.py:136
  119.1 6.3 %collective-permute-done.21.refs_4_ = bf16[64,4096]{1,0:T(8,128)(2,1)S(1)} collective-permute-done((bf16[64,4096]{1,0:T(8,128)(2,1)S(1)}, bf16[64,4096]{1,0:T(8,128)(2,1)S(1)}, u32[]{:S(2)}, u32[]{:S(2)}) %collective-permute-start.21) | collective-permute-done | bytes 524320 | tf_op jit(solution)/shard_map/ppermute | solution.py:28
  128.2 1.5 collective-permute-start.30
  129.7 2.6 %collective-permute-start.26 = (bf16[128,512]{1,0:T(8,128)(2,1)S(1)}, bf16[128,512]{1,0:T(8,128)(2,1)S(1)}, u32[]{:S(2)}, u32[]{:S(2)}) collective-permute-start(bf16[128,512]{1,0:T(8,128)(2,1)S(1)} %get-tuple-element.73), channel_id=1, source_target_pairs={{0,6},{1,7},{2,4},{3,5},{4,2},{5,3},{6,0},{7,1},{8,14},{9,15},{10,... | collective-permute-start | bytes 393224 | tf_op jit(solution)/shard_map/ppermute | solution.py:28
  132.3 2.8 %shard_map.85 = (bf16[128,512]{1,0:T(8,128)(2,1)S(1)}, bf16[128,512]{1,0:T(8,128)(2,1)S(1)}) custom-call(s32[16]{0:T(128)S(1)} %copy-done.15, bf16[64,4096]{1,0:T(8,128)(2,1)S(1)} %collective-permute-done.10.refs_1_.refs_13_.refs_15_, bf16[64,4096]{1,0:T(8,128)(2,1)S(1)} %collective-permute-done.16.refs_2_.refs_13_.refs_15_, ...), custom_call_target="tpu_custom_call" | custom-call | tf_op jit(solution)/shard_map/pallas_call | solution.py:136
  135.4 1.8 %collective-permute-start.29 = (bf16[128,512]{1,0:T(8,128)(2,1)S(1)}, bf16[128,512]{1,0:T(8,128)(2,1)S(1)}, u32[]{:S(2)}, u32[]{:S(2)}) collective-permute-start(bf16[128,512]{1,0:T(8,128)(2,1)S(1)} %get-tuple-element.79), channel_id=1, source_target_pairs={{0,6},{1,7},{2,4},{3,5},{4,2},{5,3},{6,0},{7,1},{8,14},{9,15},{10,... | collective-permute-start | bytes 393224 | tf_op jit(solution)/shard_map/ppermute | solution.py:28
  139.9 3.6 %collective-permute-done.27.refs_5_ = bf16[128,512]{1,0:T(8,128)(2,1)S(1)} collective-permute-done((bf16[128,512]{1,0:T(8,128)(2,1)S(1)}, bf16[128,512]{1,0:T(8,128)(2,1)S(1)}, u32[]{:S(2)}, u32[]{:S(2)}) %collective-permute-start.27) | collective-permute-done | bytes 131104 | tf_op jit(solution)/shard_map/ppermute | solution.py:28
  144.2 5.2 %collective-permute-done.33.refs_13_ = bf16[256,1024]{1,0:T(8,128)(2,1)} collective-permute-done((bf16[256,1024]{1,0:T(8,128)(2,1)S(1)}, bf16[256,1024]{1,0:T(8,128)(2,1)}, u32[]{:S(2)}, u32[]{:S(2)}) %collective-permute-start.33) | collective-permute-done | bytes 524320 | tf_op jit(solution)/shard_map/ppermute | solution.py:28
  149.4 2.6 %shard_map.89 = bf16[128,1024]{1,0:T(8,128)(2,1)S(1)} custom-call(s32[1]{0:T(128)} %bitcast.1.place, s32[32]{0:T(128)S(1)} %copy-done.14, bf16[128,512]{1,0:T(8,128)(2,1)S(1)} %get-tuple-element.69.refs_0_, bf16[128,512]{1,0:T(8,128)(2,1)S(1)} %collective-permute-done.24.refs_1_, bf16[128,512]{1,0:T(8,128)(2,1)S(1)} %collective-permute-done.25.refs_2_, ...), custom_call_target="tpu_custom_call" | custom-call | tf_op jit(solution)/shard_map/pallas_call | solution.py:195
  153.5 2.7 %shard_map.88 = bf16[128,1024]{1,0:T(8,128)(2,1)S(1)} custom-call(s32[1]{0:T(128)} %bitcast.place, s32[32]{0:T(128)S(1)} %copy-done.14, bf16[128,512]{1,0:T(8,128)(2,1)S(1)} %get-tuple-element.69.refs_0_, bf16[128,512]{1,0:T(8,128)(2,1)S(1)} %collective-permute-done.24.refs_1_, bf16[128,512]{1,0:T(8,128)(2,1)S(1)} %collective-permute-done.25.refs_2_, ...), custom_call_target="tpu_custom_call" | custom-call | tf_op jit(solution)/shard_map/pallas_call | solution.py:195
  157.1 2.7 %shard_map.87.refs_1_ = bf16[128,1024]{1,0:T(8,128)(2,1)S(1)} custom-call(s32[1]{0:T(128)} %bitcast.1.place, s32[32]{0:T(128)S(1)} %copy-done.14, bf16[128,512]{1,0:T(8,128)(2,1)S(1)} %get-tuple-element.69.refs_0_, bf16[128,512]{1,0:T(8,128)(2,1)S(1)} %collective-permute-done.24.refs_1_, bf16[128,512]{1,0:T(8,128)(2,1)S(1)} %collective-permute-done.25.refs_2_, ...), custom_call_target="tpu_custom_call" | custom-call | tf_op jit(solution)/shard_map/pallas_call | solution.py:195
  159.7 2.8 %shard_map.86.refs_0_ = bf16[128,1024]{1,0:T(8,128)(2,1)S(1)} custom-call(s32[1]{0:T(128)} %bitcast.place, s32[32]{0:T(128)S(1)} %copy-done.14, bf16[128,512]{1,0:T(8,128)(2,1)S(1)} %get-tuple-element.69.refs_0_, bf16[128,512]{1,0:T(8,128)(2,1)S(1)} %collective-permute-done.24.refs_1_, bf16[128,512]{1,0:T(8,128)(2,1)S(1)} %collective-permute-done.25.refs_2_, ...), custom_call_target="tpu_custom_call" | custom-call | tf_op jit(solution)/shard_map/pallas_call | solution.py:195
  162.5 3.6 %collective-permute-done.34.refs_2_ = bf16[128,1024]{1,0:T(8,128)(2,1)S(1)} collective-permute-done((bf16[128,1024]{1,0:T(8,128)(2,1)S(1)}, bf16[128,1024]{1,0:T(8,128)(2,1)S(1)}, u32[]{:S(2)}, u32[]{:S(2)}) %collective-permute-start.34) | collective-permute-done | bytes 262176 | tf_op jit(solution)/shard_map/ppermute | solution.py:28
  166.1 1.6 shard_map.90
  (92 shorter events, 21.2 us)
Async XLA Ops:
  0.0 30.4 %collective-permute-start.4 = (bf16[256,4096]{1,0:T(8,128)(2,1)}, bf16[256,4096]{1,0:T(8,128)(2,1)}, u32[]{:S(2)}, u32[]{:S(2)}) collective-permute-start(bf16[256,4096]{1,0:T(8,128)(2,1)} %refs_8_.7), channel_id=1, source_target_pairs={{0,1},{1,0},{2,3},{3,2},{4,5},{5,4},{6,7},{7,6},{8,9},{9,8},{10,11... | collective-permute-start | bytes 6291464 | tf_op jit(solution)/shard_map/ppermute | solution.py:28
  0.5 29.1 %collective-permute-start = (bf16[64,4096]{1,0:T(8,128)(2,1)}, bf16[64,4096]{1,0:T(8,128)(2,1)S(1)}, u32[]{:S(2)}, u32[]{:S(2)}) collective-permute-start(bf16[64,4096]{1,0:T(8,128)(2,1)} %refs_0_.3), channel_id=1, source_target_pairs={{0,8},{1,9},{2,10},{3,11},{4,12},{5,13},{6,14},{7,15},{8,0},{9,1},... | collective-permute-start | bytes 1572872 | tf_op jit(solution)/shard_map/ppermute | solution.py:33
  4.1 25.4 %collective-permute-start.1 = (bf16[64,4096]{1,0:T(8,128)(2,1)}, bf16[64,4096]{1,0:T(8,128)(2,1)S(1)}, u32[]{:S(2)}, u32[]{:S(2)}) collective-permute-start(bf16[64,4096]{1,0:T(8,128)(2,1)} %refs_0_.3), channel_id=1, source_target_pairs={{0,2},{1,3},{2,0},{3,1},{4,6},{5,7},{6,4},{7,5},{8,10},{9,11},{10,... | collective-permute-start | bytes 1572872 | tf_op jit(solution)/shard_map/ppermute | solution.py:28
  5.6 24.8 %collective-permute-start.2 = (bf16[64,4096]{1,0:T(8,128)(2,1)}, bf16[64,4096]{1,0:T(8,128)(2,1)}, u32[]{:S(2)}, u32[]{:S(2)}) collective-permute-start(bf16[64,4096]{1,0:T(8,128)(2,1)} %refs_0_.3), channel_id=1, source_target_pairs={{0,4},{1,5},{2,6},{3,7},{4,0},{5,1},{6,2},{7,3},{8,12},{9,13},{10,... | collective-permute-start | bytes 1572872 | tf_op jit(solution)/shard_map/ppermute | solution.py:28
  8.5 21.1 %collective-permute-start.3 = (bf16[256,1024]{1,0:T(8,128)(2,1)S(1)}, bf16[256,1024]{1,0:T(8,128)(2,1)S(1)}, u32[]{:S(2)}, u32[]{:S(2)}) collective-permute-start(bf16[256,1024]{1,0:T(8,128)(2,1)S(1)} %get-tuple-element.88), channel_id=1, source_target_pairs={{0,2},{1,3},{2,0},{3,1},{4,6},{5,7},{6,4},{7,5},{8,10},{9,11},{10,... | collective-permute-start | bytes 1572872 | tf_op jit(solution)/shard_map/ppermute | solution.py:28
  30.4 27.9 %collective-permute-start.9 = (bf16[4096,512]{1,0:T(8,128)(2,1)S(1)}, bf16[4096,512]{1,0:T(8,128)(2,1)S(1)}, u32[]{:S(2)}, u32[]{:S(2)}) collective-permute-start(bf16[4096,512]{1,0:T(8,128)(2,1)S(1)} %pad_maximum_fusion), channel_id=1, source_target_pairs={{0,1},{1,0},{2,3},{3,2},{4,5},{5,4},{6,7},{7,6},{8,9},{9,8},{10,11... | collective-permute-start | bytes 12582920 | tf_op jit(solution)/shard_map/ppermute | solution.py:28
  30.5 26.6 %collective-permute-start.5 = (bf16[64,4096]{1,0:T(8,128)(2,1)S(1)}, bf16[64,4096]{1,0:T(8,128)(2,1)S(1)}, u32[]{:S(2)}, u32[]{:S(2)}) collective-permute-start(bf16[64,4096]{1,0:T(8,128)(2,1)S(1)} %slice.6), channel_id=1, source_target_pairs={{0,8},{1,9},{2,10},{3,11},{4,12},{5,13},{6,14},{7,15},{8,0},{9,1},... | collective-permute-start | bytes 1572872 | tf_op jit(solution)/shard_map/ppermute | solution.py:33
  30.9 26.2 %collective-permute-start.6 = (bf16[64,4096]{1,0:T(8,128)(2,1)S(1)}, bf16[64,4096]{1,0:T(8,128)(2,1)S(1)}, u32[]{:S(2)}, u32[]{:S(2)}) collective-permute-start(bf16[64,4096]{1,0:T(8,128)(2,1)S(1)} %collective-permute-done.refs_0_), channel_id=1, source_target_pairs={{0,4},{1,5},{2,6},{3,7},{4,0},{5,1},{6,2},{7,3},{8,12},{9,13},{10,... | collective-permute-start | bytes 1572872 | tf_op jit(solution)/shard_map/ppermute | solution.py:28
  33.3 23.8 %collective-permute-start.7 = (bf16[64,4096]{1,0:T(8,128)(2,1)S(1)}, bf16[64,4096]{1,0:T(8,128)(2,1)S(1)}, u32[]{:S(2)}, u32[]{:S(2)}) collective-permute-start(bf16[64,4096]{1,0:T(8,128)(2,1)S(1)} %collective-permute-done.refs_0_), channel_id=1, source_target_pairs={{0,2},{1,3},{2,0},{3,1},{4,6},{5,7},{6,4},{7,5},{8,10},{9,11},{10,... | collective-permute-start | bytes 1572872 | tf_op jit(solution)/shard_map/ppermute | solution.py:28
  34.8 23.5 %collective-permute-start.8 = (bf16[64,4096]{1,0:T(8,128)(2,1)}, bf16[64,4096]{1,0:T(8,128)(2,1)S(1)}, u32[]{:S(2)}, u32[]{:S(2)}) collective-permute-start(bf16[64,4096]{1,0:T(8,128)(2,1)} %collective-permute-done.2.refs_2_), channel_id=1, source_target_pairs={{0,2},{1,3},{2,0},{3,1},{4,6},{5,7},{6,4},{7,5},{8,10},{9,11},{10,... | collective-permute-start | bytes 1572872 | tf_op jit(solution)/shard_map/ppermute | solution.py:28
  58.3 26.6 %collective-permute-start.11 = (bf16[64,4096]{1,0:T(8,128)(2,1)S(1)}, bf16[64,4096]{1,0:T(8,128)(2,1)S(1)}, u32[]{:S(2)}, u32[]{:S(2)}) collective-permute-start(bf16[64,4096]{1,0:T(8,128)(2,1)S(1)} %collective-permute-done.5.refs_1_.refs_12_.refs_14_), channel_id=1, source_target_pairs={{0,4},{1,5},{2,6},{3,7},{4,0},{5,1},{6,2},{7,3},{8,12},{9,13},{10,... | collective-permute-start | bytes 1572872 | tf_op jit(solution)/shard_map/ppermute | solution.py:28
  58.6 26.3 %collective-permute-start.12 = (bf16[64,4096]{1,0:T(8,128)(2,1)S(1)}, bf16[64,4096]{1,0:T(8,128)(2,1)S(1)}, u32[]{:S(2)}, u32[]{:S(2)}) collective-permute-start(bf16[64,4096]{1,0:T(8,128)(2,1)S(1)} %collective-permute-done.5.refs_1_.refs_12_.refs_14_), channel_id=1, source_target_pairs={{0,2},{1,3},{2,0},{3,1},{4,6},{5,7},{6,4},{7,5},{8,10},{9,11},{10,... | collective-permute-start | bytes 1572872 | tf_op jit(solution)/shard_map/ppermute | solution.py:28
  60.1 24.9 %collective-permute-start.10 = (bf16[64,4096]{1,0:T(8,128)(2,1)S(1)}, bf16[64,4096]{1,0:T(8,128)(2,1)S(1)}, u32[]{:S(2)}, u32[]{:S(2)}) collective-permute-start(bf16[64,4096]{1,0:T(8,128)(2,1)S(1)} %slice.7), channel_id=1, source_target_pairs={{0,8},{1,9},{2,10},{3,11},{4,12},{5,13},{6,14},{7,15},{8,0},{9,1},... | collective-permute-start | bytes 1572872 | tf_op jit(solution)/shard_map/ppermute | solution.py:33
  62.2 22.8 %collective-permute-start.13 = (bf16[64,4096]{1,0:T(8,128)(2,1)S(1)}, bf16[64,4096]{1,0:T(8,128)(2,1)S(1)}, u32[]{:S(2)}, u32[]{:S(2)}) collective-permute-start(bf16[64,4096]{1,0:T(8,128)(2,1)S(1)} %collective-permute-done.6.refs_2_), channel_id=1, source_target_pairs={{0,2},{1,3},{2,0},{3,1},{4,6},{5,7},{6,4},{7,5},{8,10},{9,11},{10,... | collective-permute-start | bytes 1572872 | tf_op jit(solution)/shard_map/ppermute | solution.py:28
  62.7 22.3 %collective-permute-start.14 = (bf16[256,1024]{1,0:T(8,128)(2,1)S(1)}, bf16[256,1024]{1,0:T(8,128)(2,1)S(1)}, u32[]{:S(2)}, u32[]{:S(2)}) collective-permute-start(bf16[256,1024]{1,0:T(8,128)(2,1)S(1)} %collective-permute-done.3), channel_id=1, source_target_pairs={{0,16},{16,0},{1,17},{17,1},{2,18},{18,2},{3,19},{19,3},{4,20},{20... | collective-permute-start | bytes 1572872 | tf_op jit(solution)/shard_map/ppermute | solution.py:45
  85.0 25.7 %collective-permute-start.19 = (bf16[4096,256]{1,0:T(8,128)(2,1)S(1)}, bf16[4096,256]{1,0:T(8,128)(2,1)S(1)}, u32[]{:S(2)}, u32[]{:S(2)}) collective-permute-start(bf16[4096,256]{1,0:T(8,128)(2,1)S(1)} %copy-done.2), channel_id=1, source_target_pairs={{0,1},{1,0},{2,3},{3,2},{4,5},{5,4},{6,7},{7,6},{8,9},{9,8},{10,11... | collective-permute-start | bytes 6291464 | tf_op jit(solution)/shard_map/ppermute | solution.py:28
  85.1 14.8 %collective-permute-start.15 = (bf16[64,4096]{1,0:T(8,128)(2,1)S(1)}, bf16[64,4096]{1,0:T(8,128)(2,1)S(1)}, u32[]{:S(2)}, u32[]{:S(2)}) collective-permute-start(bf16[64,4096]{1,0:T(8,128)(2,1)S(1)} %collective-permute-done.10.refs_1_.refs_13_.refs_15_), channel_id=1, source_target_pairs={{0,4},{1,5},{2,6},{3,7},{4,0},{5,1},{6,2},{7,3},{8,12},{9,13},{10,... | collective-permute-start | bytes 1572872 | tf_op jit(solution)/shard_map/ppermute | solution.py:28
  85.2 14.8 %collective-permute-start.16 = (bf16[64,4096]{1,0:T(8,128)(2,1)S(1)}, bf16[64,4096]{1,0:T(8,128)(2,1)S(1)}, u32[]{:S(2)}, u32[]{:S(2)}) collective-permute-start(bf16[64,4096]{1,0:T(8,128)(2,1)S(1)} %collective-permute-done.10.refs_1_.refs_13_.refs_15_), channel_id=1, source_target_pairs={{0,2},{1,3},{2,0},{3,1},{4,6},{5,7},{6,4},{7,5},{8,10},{9,11},{10,... | collective-permute-start | bytes 1572872 | tf_op jit(solution)/shard_map/ppermute | solution.py:28
  86.1 24.6 %collective-permute-start.17 = (bf16[64,4096]{1,0:T(8,128)(2,1)S(1)}, bf16[64,4096]{1,0:T(8,128)(2,1)S(1)}, u32[]{:S(2)}, u32[]{:S(2)}) collective-permute-start(bf16[64,4096]{1,0:T(8,128)(2,1)S(1)} %collective-permute-done.11.refs_3_), channel_id=1, source_target_pairs={{0,2},{1,3},{2,0},{3,1},{4,6},{5,7},{6,4},{7,5},{8,10},{9,11},{10,... | collective-permute-start | bytes 1572872 | tf_op jit(solution)/shard_map/ppermute | solution.py:28
  87.3 23.4 %collective-permute-start.18 = (bf16[256,1024]{1,0:T(8,128)(2,1)S(1)}, bf16[256,1024]{1,0:T(8,128)(2,1)S(1)}, u32[]{:S(2)}, u32[]{:S(2)}) collective-permute-start(bf16[256,1024]{1,0:T(8,128)(2,1)S(1)} %get-tuple-element.61), channel_id=1, source_target_pairs={{0,4},{1,5},{2,6},{3,7},{4,0},{5,1},{6,2},{7,3},{8,12},{9,13},{10,... | collective-permute-start | bytes 1572872 | tf_op jit(solution)/shard_map/ppermute | solution.py:28
  110.7 14.8 %collective-permute-start.21 = (bf16[64,4096]{1,0:T(8,128)(2,1)S(1)}, bf16[64,4096]{1,0:T(8,128)(2,1)S(1)}, u32[]{:S(2)}, u32[]{:S(2)}) collective-permute-start(bf16[64,4096]{1,0:T(8,128)(2,1)S(1)} %collective-permute-done.15.refs_3_), channel_id=1, source_target_pairs={{0,2},{1,3},{2,0},{3,1},{4,6},{5,7},{6,4},{7,5},{8,10},{9,11},{10,... | collective-permute-start | bytes 1572872 | tf_op jit(solution)/shard_map/ppermute | solution.py:28
  111.4 14.8 %collective-permute-start.22 = (bf16[256,1024]{1,0:T(8,128)(2,1)S(1)}, bf16[256,1024]{1,0:T(8,128)(2,1)S(1)}, u32[]{:S(2)}, u32[]{:S(2)}) collective-permute-start(bf16[256,1024]{1,0:T(8,128)(2,1)S(1)} %collective-permute-done.3), channel_id=1, source_target_pairs={{0,4},{1,5},{2,6},{3,7},{4,0},{5,1},{6,2},{7,3},{8,12},{9,13},{10,... | collective-permute-start | bytes 1572872 | tf_op jit(solution)/shard_map/ppermute | solution.py:28
  113.2 13.7 %collective-permute-start.23 = (bf16[256,1024]{1,0:T(8,128)(2,1)S(1)}, bf16[256,1024]{1,0:T(8,128)(2,1)S(1)}, u32[]{:S(2)}, u32[]{:S(2)}) collective-permute-start(bf16[256,1024]{1,0:T(8,128)(2,1)S(1)} %collective-permute-done.18), channel_id=1, source_target_pairs={{0,16},{16,0},{1,17},{17,1},{2,18},{18,2},{3,19},{19,3},{4,20},{20... | collective-permute-start | bytes 1572872 | tf_op jit(solution)/shard_map/ppermute | solution.py:45
  117.4 10.4 %collective-permute-start.24 = (bf16[128,512]{1,0:T(8,128)(2,1)S(1)}, bf16[128,512]{1,0:T(8,128)(2,1)S(1)}, u32[]{:S(2)}, u32[]{:S(2)}) collective-permute-start(bf16[128,512]{1,0:T(8,128)(2,1)S(1)} %get-tuple-element.69.refs_0_), channel_id=1, source_target_pairs={{0,2},{1,3},{2,0},{3,1},{4,6},{5,7},{6,4},{7,5},{8,10},{9,11},{10,... | collective-permute-start | bytes 393224 | tf_op jit(solution)/shard_map/ppermute | solution.py:28
  118.9 9.3 %collective-permute-start.25 = (bf16[128,512]{1,0:T(8,128)(2,1)S(1)}, bf16[128,512]{1,0:T(8,128)(2,1)S(1)}, u32[]{:S(2)}, u32[]{:S(2)}) collective-permute-start(bf16[128,512]{1,0:T(8,128)(2,1)S(1)} %get-tuple-element.73), channel_id=1, source_target_pairs={{0,4},{1,5},{2,6},{3,7},{4,0},{5,1},{6,2},{7,3},{8,12},{9,13},{10,... | collective-permute-start | bytes 393224 | tf_op jit(solution)/shard_map/ppermute | solution.py:28
  128.2 15.4 %collective-permute-start.30 = (bf16[256,1024]{1,0:T(8,128)(2,1)S(1)}, bf16[256,1024]{1,0:T(8,128)(2,1)S(1)}, u32[]{:S(2)}, u32[]{:S(2)}) collective-permute-start(bf16[256,1024]{1,0:T(8,128)(2,1)S(1)} %collective-permute-done.22), channel_id=1, source_target_pairs={{0,16},{16,0},{1,17},{17,1},{2,18},{18,2},{3,19},{19,3},{4,20},{20... | collective-permute-start | bytes 1572872 | tf_op jit(solution)/shard_map/ppermute | solution.py:45
  129.7 10.2 %collective-permute-start.26 = (bf16[128,512]{1,0:T(8,128)(2,1)S(1)}, bf16[128,512]{1,0:T(8,128)(2,1)S(1)}, u32[]{:S(2)}, u32[]{:S(2)}) collective-permute-start(bf16[128,512]{1,0:T(8,128)(2,1)S(1)} %get-tuple-element.73), channel_id=1, source_target_pairs={{0,6},{1,7},{2,4},{3,5},{4,2},{5,3},{6,0},{7,1},{8,14},{9,15},{10,... | collective-permute-start | bytes 393224 | tf_op jit(solution)/shard_map/ppermute | solution.py:28
  135.0 8.5 %collective-permute-start.28 = (bf16[128,512]{1,0:T(8,128)(2,1)S(1)}, bf16[128,512]{1,0:T(8,128)(2,1)S(1)}, u32[]{:S(2)}, u32[]{:S(2)}) collective-permute-start(bf16[128,512]{1,0:T(8,128)(2,1)S(1)} %get-tuple-element.79), channel_id=1, source_target_pairs={{0,4},{1,5},{2,6},{3,7},{4,0},{5,1},{6,2},{7,3},{8,12},{9,13},{10,... | collective-permute-start | bytes 393224 | tf_op jit(solution)/shard_map/ppermute | solution.py:28
  135.4 8.2 %collective-permute-start.29 = (bf16[128,512]{1,0:T(8,128)(2,1)S(1)}, bf16[128,512]{1,0:T(8,128)(2,1)S(1)}, u32[]{:S(2)}, u32[]{:S(2)}) collective-permute-start(bf16[128,512]{1,0:T(8,128)(2,1)S(1)} %get-tuple-element.79), channel_id=1, source_target_pairs={{0,6},{1,7},{2,4},{3,5},{4,2},{5,3},{6,0},{7,1},{8,14},{9,15},{10,... | collective-permute-start | bytes 393224 | tf_op jit(solution)/shard_map/ppermute | solution.py:28
  143.6 9.9 %collective-permute-start.31 = (bf16[768,1024]{1,0:T(8,128)(2,1)}, bf16[768,1024]{1,0:T(8,128)(2,1)}, u32[]{:S(2)}, u32[]{:S(2)}) collective-permute-start(bf16[768,1024]{1,0:T(8,128)(2,1)} %pad_maximum_fusion.1.refs_9_), channel_id=1, source_target_pairs={{0,1},{1,0},{2,3},{3,2},{4,5},{5,4},{6,7},{7,6},{8,9},{9,8},{10,11... | collective-permute-start | bytes 4718600 | tf_op jit(solution)/shard_map/ppermute | solution.py:28
  152.1 10.4 %collective-permute-start.35 = (bf16[128,1024]{1,0:T(8,128)(2,1)S(1)}, bf16[128,1024]{1,0:T(8,128)(2,1)S(1)}, u32[]{:S(2)}, u32[]{:S(2)}) collective-permute-start(bf16[128,1024]{1,0:T(8,128)(2,1)S(1)} %shard_map.89), channel_id=1, source_target_pairs={{0,2},{1,3},{2,0},{3,1},{4,6},{5,7},{6,4},{7,5},{8,10},{9,11},{10,... | collective-permute-start | bytes 786440 | tf_op jit(solution)/shard_map/ppermute | solution.py:28
  156.3 9.8 %collective-permute-start.34 = (bf16[128,1024]{1,0:T(8,128)(2,1)S(1)}, bf16[128,1024]{1,0:T(8,128)(2,1)S(1)}, u32[]{:S(2)}, u32[]{:S(2)}) collective-permute-start(bf16[128,1024]{1,0:T(8,128)(2,1)S(1)} %shard_map.88), channel_id=1, source_target_pairs={{0,2},{1,3},{2,0},{3,1},{4,6},{5,7},{6,4},{7,5},{8,10},{9,11},{10,... | collective-permute-start | bytes 786440 | tf_op jit(solution)/shard_map/ppermute | solution.py:28
  (22 other events, 510.0 us)

commit v6 on v5

--- a/solution.py
+++ b/solution.py
@@ -62,7 +62,7 @@
     for k, ref in enumerate(mem_refs):
         rows[k * MEMF:(k + 1) * MEMF, :] = ref[:MEMF]
     width = key_own.shape[1]
-    weights = (key_own[...], pair_oth[:, :width], val_own[...], pair_oth[:, width:])
+    weights = (key_own[...], pair_oth[:, :width], val_own[...], pair_oth[:, width:2 * width])
     for k, weight in enumerate(weights):
         out[done:, k * width:(k + 1) * width] = dot(rows[...], weight).astype(BF16)
 
@@ -95,7 +95,7 @@
         scale = lax.rsqrt(jnp.mean(wide * wide, -1, keepdims=True) + NORM_EPS)
         normed[k * FR:(k + 1) * FR, :] = (wide * scale).astype(BF16)
     queries = jnp.concatenate(
-        [dot(normed[...], query_own[...]), dot(normed[...], query_oth[...])], 1
+        [dot(normed[...], query_own[...]), dot(normed[...], query_oth[:, 2 * width:])], 1
     ).astype(BF16)
     is_own = (section + j) % 2 == core
     column = lax.broadcasted_iota(jnp.int32, (FR, MEMF), 1)
@@ -144,7 +144,8 @@
     )(mem_len, *pieces, *weights, *kv)
 
 
-def project_kernel(near, place, tok_len, *refs):
+def project_kernel(near, skip, place, tok_len, *refs):
+    refs = refs[skip:]
     att, weights, x_refs, out = refs[:8], refs[8:-3], refs[-3:-1], refs[-1]
     me = lax.axis_index("section")
     slot = (me % GROUP) ^ (NEAR if near else 0)
@@ -169,11 +170,11 @@
         out[j * FR:(j + 1) * FR, :] = (x_ref[...].astype(F32) + branch).astype(BF16)
 
 
-def project(near, place, tok_len, att, own, oth, pieces, x_first, x_last):
+def project(near, place, tok_len, att, own, oth, pieces, x_first, x_last, into=None):
     width, depth = own.shape
     rows = 2 * FR
     tile = 512
-    cols = pieces[0][0].shape[1]
+    cols = pieces[0][0][0].shape[1]
     steps = cols // tile
 
     def everywhere(i, place):
@@ -184,46 +185,59 @@
 
     att_specs = [pl.BlockSpec((2 * FR, 2 * width), lambda i, place: (0, 0))] * 8
     weights, weight_specs = [], []
+    into = [] if near or into is None else [into]
     for mine, others in zip((own, oth), pieces):
-        weights += [mine, *others]
+        weights.append(mine)
         weight_specs.append(pl.BlockSpec((width, tile), everywhere))
-        weight_specs += [pl.BlockSpec((other.shape[0], tile), here) for other in others]
+        for n, (array, block) in enumerate(others):
+            height = array.shape[0] if n else width
+            weights.append(array)
+            weight_specs.append(
+                pl.BlockSpec((height, tile), lambda i, place, block=block: (block, i))
+            )
     x_specs = [
         pl.BlockSpec((FR, tile), lambda i, place, at=ref.shape[0] // FR - 1: (at, everywhere(i, place)[1]))
         for ref in (x_first, x_last)
     ]
     return pl.pallas_call(
-        functools.partial(project_kernel, near),
-        out_shape=jax.ShapeDtypeStruct((rows, cols), BF16),
+        functools.partial(project_kernel, near, len(into)),
+        out_shape=jax.ShapeDtypeStruct((rows, cols if near else depth), BF16),
         grid_spec=pltpu.PrefetchScalarGridSpec(
             num_scalar_prefetch=1,
             grid=(steps,),
-            in_specs=[pl.BlockSpec(memory_space=pltpu.SMEM)] + att_specs + weight_specs + x_specs,
-            out_specs=pl.BlockSpec((rows, tile), here),
+            in_specs=[pl.BlockSpec(memory_space=pltpu.SMEM)] + [pl.BlockSpec(memory_space=pl.ANY)] * len(into) + att_specs + weight_specs + x_specs,
+            out_specs=pl.BlockSpec((rows, tile), here if near else everywhere),
         ),
         compiler_params=pltpu.CompilerParams(
             vmem_limit_bytes=WIDE_VMEM_BYTES, dimension_semantics=("arbitrary",)
         ),
         cost_estimate=pl.CostEstimate(flops=0, bytes_accessed=0, transcendentals=0),
-    )(place, tok_len, *att, *weights, x_first, x_last)
-
-
-def assemble_kernel(order, *refs):
-    out = refs[-1]
-    cols = refs[0].shape[1]
-    for k, ref in enumerate(refs[:-1]):
-        out[:, pl.ds(pl.multiple_of(order[k] * cols, 128), cols)] = ref[...]
-
-
-def assemble(order, parts):
-    rows, cols = parts[0].shape
+        input_output_aliases={2: 0} if into else {},
+    )(place, tok_len, *into, *att, *weights, x_first, x_last)
+
+
+def assemble_kernel(place, mine, theirs_a, theirs_b, out):
+    for k, ref in enumerate((theirs_a, theirs_b)):
+        @pl.when(pl.program_id(0) == k)
+        def _(ref=ref):
+            out[...] = ref[...]
+
+
+def assemble(place, mine, theirs):
+    rows, cols = theirs[0].shape
     return pl.pallas_call(
         assemble_kernel,
-        out_shape=jax.ShapeDtypeStruct((rows, len(parts) * cols), BF16),
-        in_specs=[pl.BlockSpec(memory_space=pltpu.SMEM)] + whole(len(parts)),
-        out_specs=pl.BlockSpec(memory_space=pltpu.VMEM),
+        out_shape=jax.ShapeDtypeStruct(mine.shape, BF16),
+        grid_spec=pltpu.PrefetchScalarGridSpec(
+            num_scalar_prefetch=1,
+            grid=(2,),
+            in_specs=[pl.BlockSpec(memory_space=pl.ANY)]
+            + [pl.BlockSpec((rows, cols), lambda i, place: (0, 0))] * 2,
+            out_specs=pl.BlockSpec((rows, cols), lambda i, place: (0, place[i])),
+        ),
+        input_output_aliases={1: 0},
         compiler_params=pltpu.CompilerParams(vmem_limit_bytes=VMEM_BYTES),
-    )(order, *parts)
+    )(place, mine, *theirs)
 
 
 def shards(arriving, memory, w_query, w_key, w_value, w_out, tok_len, mem_len):
@@ -245,7 +259,7 @@
 
     out_near = flip(to_near, NEAR)
     out_core = flip(w_out, CORE)
-    kv_pair = jnp.concatenate([w_key, w_value], 1)
+    kv_pair = jnp.concatenate([w_key, w_value, w_query], 1)
     if ring:
         mem_hop, mem_near, mem_far = hop(memory), flip(memory, NEAR), flip(memory, FAR)
     else:
@@ -269,18 +283,18 @@
     cross_near = across(out_near)
     mem_first = [memory, mem_near, mem_far, mem_diag] if ring else gathered[:4]
     kv_first = keys_values(mem_first, kv_weights)
-    last_hop, first_far, first_near, hop_diag, cross_near, kv_first, to_far, w_query = together(
-        last_hop, first_far, first_near, hop_diag, cross_near, kv_first, to_far, w_query
+    last_hop, first_far, first_near, hop_diag, cross_near, kv_first, to_far = together(
+        last_hop, first_far, first_near, hop_diag, cross_near, kv_first, to_far
     )
     last_far, last_near, first_diag = flip(last_hop, FAR), flip(last_hop, NEAR), flip(first_far, NEAR)
     out_far = flip(to_far, FAR)
-    query_oth = flip(w_query, CORE)
+    near_core = flip(jnp.concatenate([out_near, cross_near], 0), CORE)
     mem_second = [mem_hop, hop_near, hop_far, hop_diag] if ring else gathered[4:]
     kv_second = keys_values(mem_second, kv_weights, kv_first)
-    last_far, last_near, first_diag, out_far, query_oth, kv_second, out_near = together(
-        last_far, last_near, first_diag, out_far, query_oth, kv_second, out_near
-    )
-    query_pair = [w_query, query_oth]
+    last_far, last_near, first_diag, out_far, near_core, kv_second, out_near = together(
+        last_far, last_near, first_diag, out_far, near_core, kv_second, out_near
+    )
+    query_pair = [w_query, kv_pair]
     last_diag = flip(last_far, NEAR)
     out_diag = flip(out_near, FAR)
     cross_far = across(out_far)
@@ -295,24 +309,29 @@
     last = [last_hop, last_near, last_far, last_diag]
     here, there = attend(1, ring, mem_len, last, query_pair, kv)
     att += [here, flip(here, NEAR), flip(there, FAR), flip(there, NEAR | FAR)]
-    fetched = jnp.concatenate([out_near, out_far, out_diag], 0)
-    crossed = jnp.concatenate([cross_near, cross_far], 0)
-    fetched, crossed, cross_diag = together(fetched, crossed, cross_diag, att[3], *att[5:])[:3]
-    fetched = [[fetched], [flip(fetched, CORE)]]
-    handed = [[crossed, cross_diag], [flip(crossed, CORE), flip(cross_diag, CORE)]]
+    fetched = jnp.concatenate([out_far, out_diag], 0)
+    fetched, cross_far, cross_diag = together(fetched, cross_far, cross_diag, att[3], *att[5:])[:3]
+    handed = [cross_far, cross_diag]
+    handed_core = [flip(part, CORE) for part in handed]
+    fetched_core = flip(after(fetched, *handed_core), CORE)
+    fetched = [[(out_near, 0), (fetched, 0)], [(near_core, 0), (fetched_core, 0)]]
+    handed = [
+        [(cross_near, 0)] + [(part, 0) for part in handed],
+        [(near_core, 1)] + [(part, 0) for part in handed_core],
+    ]
     quarters = jnp.stack(
         [2 * side + group, 2 * side + 1 - group, 2 - 2 * side + group, 3 - 2 * side - group]
     ).astype(jnp.int32)
-    def part(near, n, pieces, *others):
+    def part(near, n, pieces, into=None):
         at = 1 if near else 0
         return project(
-            near, after(quarters[n:n + 1], *others), tok_len, att, w_out, out_core, pieces, first[at], last[at]
+            near, quarters[n:n + 1], tok_len, att, w_out, out_core, pieces, first[at], last[at], into
         )
 
     theirs_b = flip(part(True, 1, handed), NEAR)
     theirs_a = flip(part(True, 0, fetched), NEAR)
-    mine = [part(False, 0, fetched), part(False, 1, handed)]
-    return assemble(quarters, mine + [theirs_a, theirs_b])
+    mine = part(False, 1, handed, part(False, 0, fetched))
+    return assemble(quarters[2:], mine, [theirs_a, theirs_b])
 
 
 def solution(mesh):

time: 168 us -> 166 us (0.988)
  waiting for transfers between devices: 99.4 us -> 94.8 us
    ppermute x30, waiting for transfers between devices: 59.6 us -> 55 us  [flip(): return lax.ppermute(value, 'section', [(i, i ^ bits) for i in range(size)])]
  transfers between devices with their start and end apart: 36 -> 36, of which waited for: 15 -> 16; matrix products, arithmetic and copies ran while one was open for 3% -> 3% of each run, Pallas kernels for 13% -> 14%
where the time goes in v6:
time: 166 us
  waiting for transfers between devices  94.8 us (57%)
  starting transfers between devices  38.9 us (23%)
  Pallas kernels  24.4 us (15%)
  other arithmetic  4.35 us (3%)
  local copies, waits for them, and re-layouts  3.26 us (2%)
    ppermute x30, waiting for transfers between devices, flip(): return lax.ppermute(value, 'section', [(i, i ^ bits) for i in range(size)])  55 us
    ppermute x3, waiting for transfers between devices, hop(): lax.ppermute(value, 'section', [(i, (i + GROUP) % size) for i in range(si...  39.1 us
    ppermute x30, starting transfers between devices, flip(): return lax.ppermute(value, 'section', [(i, i ^ bits) for i in range(size)])  28.3 us
    pallas_call x4, Pallas kernels, project(): pl.pallas_call(functools.partial(project_kernel, near, len(into)), out_sh...  11.7 us
    ppermute x3, starting transfers between devices, hop(): lax.ppermute(value, 'section', [(i, (i + GROUP) % size) for i in range(si...  6.09 us
    pallas_call x2, Pallas kernels, keys_values(): pl.pallas_call(keys_values_kernel, out_shape=jax.ShapeDtypeStruct((total,...  5.75 us
    pallas_call x2, Pallas kernels, attend(): pl.pallas_call(functools.partial(attend_kernel, j, ring), out_shape=[jax....  5.53 us
    ppermute x3, starting transfers between devices, across(): return lax.ppermute(value, 'groups', [(0, 1), (1, 0)])  4.47 us
  transfers between devices with their start and end apart: 36, of which 16 were waited for; matrix products, arithmetic and copies ran while one was open for 3% of the time, Pallas kernels for 14%

profile of v6, /device:TPU:0, one launch (start us, length us, event | category | flops | bytes accessed | tf_op | source)
XLA Modules:
  0.0 166.0 jit_solution(4214690066088537156)
XLA Ops:
  0.5 3.6 %collective-permute-start = (bf16[64,4096]{1,0:T(8,128)(2,1)}, bf16[64,4096]{1,0:T(8,128)(2,1)S(1)}, u32[]{:S(2)}, u32[]{:S(2)}) collective-permute-start(bf16[64,4096]{1,0:T(8,128)(2,1)} %refs_0_.3), channel_id=1, source_target_pairs={{0,8},{1,9},{2,10},{3,11},{4,12},{5,13},{6,14},{7,15},{8,0},{9,1},... | collective-permute-start | bytes 1572872 | tf_op jit(solution)/shard_map/ppermute | solution.py:33
  4.1 1.5 collective-permute-start.1
  5.6 1.6 collective-permute-start.2
  9.1 3.1 %pad_maximum_fusion = bf16[4096,768]{1,0:T(8,128)(2,1)S(1)} fusion(bf16[4096,256]{1,0:T(8,128)(2,1)} %refs_5_.7, bf16[4096,256]{1,0:T(8,128)(2,1)S(1)} %copy-done, bf16[4096,256]{1,0:T(8,128)(2,1)} %refs_4_.3), kind=kLoop, calls=%fused_computation | loop fusion | flops 18874368 | bytes 12582912 | tf_op jit(solution)/shard_map/concatenate | solution.py:262
  12.2 17.3 %collective-permute-done.3.refs_9_ = bf16[256,1024]{1,0:T(8,128)(2,1)S(1)} collective-permute-done((bf16[256,1024]{1,0:T(8,128)(2,1)S(1)}, bf16[256,1024]{1,0:T(8,128)(2,1)S(1)}, u32[]{:S(2)}, u32[]{:S(2)}) %collective-permute-start.3) | collective-permute-done | bytes 524320 | tf_op jit(solution)/shard_map/ppermute | solution.py:28
  30.9 2.5 %collective-permute-start.6 = (bf16[64,4096]{1,0:T(8,128)(2,1)S(1)}, bf16[64,4096]{1,0:T(8,128)(2,1)S(1)}, u32[]{:S(2)}, u32[]{:S(2)}) collective-permute-start(bf16[64,4096]{1,0:T(8,128)(2,1)S(1)} %collective-permute-done.refs_0_), channel_id=1, source_target_pairs={{0,4},{1,5},{2,6},{3,7},{4,0},{5,1},{6,2},{7,3},{8,12},{9,13},{10,... | collective-permute-start | bytes 1572872 | tf_op jit(solution)/shard_map/ppermute | solution.py:28
  33.4 1.5 collective-permute-start.7
  35.4 21.7 %collective-permute-done.5.refs_1_.refs_14_.refs_17_ = bf16[64,4096]{1,0:T(8,128)(2,1)S(1)} collective-permute-done((bf16[64,4096]{1,0:T(8,128)(2,1)S(1)}, bf16[64,4096]{1,0:T(8,128)(2,1)S(1)}, u32[]{:S(2)}, u32[]{:S(2)}) %collective-permute-start.5) | collective-permute-done | bytes 524320 | tf_op jit(solution)/shard_map/ppermute | solution.py:33
  60.1 2.1 %collective-permute-start.10 = (bf16[64,4096]{1,0:T(8,128)(2,1)S(1)}, bf16[64,4096]{1,0:T(8,128)(2,1)S(1)}, u32[]{:S(2)}, u32[]{:S(2)}) collective-permute-start(bf16[64,4096]{1,0:T(8,128)(2,1)S(1)} %slice.7), channel_id=1, source_target_pairs={{0,8},{1,9},{2,10},{3,11},{4,12},{5,13},{6,14},{7,15},{8,0},{9,1},... | collective-permute-start | bytes 1572872 | tf_op jit(solution)/shard_map/ppermute | solution.py:33
  62.7 1.5 collective-permute-start.14
  64.2 3.4 %shard_map.82.refs_7_ = bf16[256,1024]{1,0:T(8,128)(2,1)S(1)} custom-call(bf16[64,4096]{1,0:T(8,128)(2,1)S(1)} %copy-done.13, bf16[64,4096]{1,0:T(8,128)(2,1)S(1)} %copy-done.15, bf16[64,4096]{1,0:T(8,128)(2,1)} %collective-permute-done.2.refs_2_, bf16[64,4096]{1,0:T(8,128)(2,1)S(1)} %collective-permute-done.8.refs_3_, bf16[4096,256]{1,0:T(8,128)(2,1)S(1)} %copy-done.1, ...), custom_call_target="tpu_custom_call" | custom-call | tf_op jit(solution)/shard_map/pallas_call | solution.py:74
  67.6 17.4 %collective-permute-done.10.refs_1_.refs_15_.refs_18_ = bf16[64,4096]{1,0:T(8,128)(2,1)S(1)} collective-permute-done((bf16[64,4096]{1,0:T(8,128)(2,1)S(1)}, bf16[64,4096]{1,0:T(8,128)(2,1)S(1)}, u32[]{:S(2)}, u32[]{:S(2)}) %collective-permute-start.10) | collective-permute-done | bytes 524320 | tf_op jit(solution)/shard_map/ppermute | solution.py:33
  87.3 1.9 %collective-permute-start.18 = (bf16[256,1024]{1,0:T(8,128)(2,1)S(1)}, bf16[256,1024]{1,0:T(8,128)(2,1)S(1)}, u32[]{:S(2)}, u32[]{:S(2)}) collective-permute-start(bf16[256,1024]{1,0:T(8,128)(2,1)S(1)} %get-tuple-element.61), channel_id=1, source_target_pairs={{0,4},{1,5},{2,6},{3,7},{4,0},{5,1},{6,2},{7,3},{8,12},{9,13},{10,... | collective-permute-start | bytes 1572872 | tf_op jit(solution)/shard_map/ppermute | solution.py:28
  89.3 2.4 %shard_map.83.refs_7_ = bf16[512,1024]{1,0:T(8,128)(2,1)S(1)} custom-call(bf16[64,4096]{1,0:T(8,128)(2,1)S(1)} %copy-done.12, bf16[64,4096]{1,0:T(8,128)(2,1)S(1)} %collective-permute-done.7.refs_1_, bf16[64,4096]{1,0:T(8,128)(2,1)S(1)} %collective-permute-done.6.refs_2_, bf16[64,4096]{1,0:T(8,128)(2,1)S(1)} %collective-permute-done.13.refs_3_, ...), custom_call_target="tpu_custom_call" | custom-call | tf_op jit(solution)/shard_map/pallas_call | solution.py:74
  91.7 8.3 %collective-permute-done.15.refs_3_ = bf16[64,4096]{1,0:T(8,128)(2,1)S(1)} collective-permute-done((bf16[64,4096]{1,0:T(8,128)(2,1)S(1)}, bf16[64,4096]{1,0:T(8,128)(2,1)S(1)}, u32[]{:S(2)}, u32[]{:S(2)}) %collective-permute-start.15) | collective-permute-done | bytes 524320 | tf_op jit(solution)/shard_map/ppermute | solution.py:28
  100.1 10.7 %collective-permute-done.17.refs_4_ = bf16[64,4096]{1,0:T(8,128)(2,1)S(1)} collective-permute-done((bf16[64,4096]{1,0:T(8,128)(2,1)S(1)}, bf16[64,4096]{1,0:T(8,128)(2,1)S(1)}, u32[]{:S(2)}, u32[]{:S(2)}) %collective-permute-start.17) | collective-permute-done | bytes 524320 | tf_op jit(solution)/shard_map/ppermute | solution.py:28
  111.5 1.8 %collective-permute-start.22 = (bf16[256,1024]{1,0:T(8,128)(2,1)S(1)}, bf16[256,1024]{1,0:T(8,128)(2,1)S(1)}, u32[]{:S(2)}, u32[]{:S(2)}) collective-permute-start(bf16[256,1024]{1,0:T(8,128)(2,1)S(1)} %collective-permute-done.3.refs_9_), channel_id=1, source_target_pairs={{0,4},{1,5},{2,6},{3,7},{4,0},{5,1},{6,2},{7,3},{8,12},{9,13},{10,... | collective-permute-start | bytes 1572872 | tf_op jit(solution)/shard_map/ppermute | solution.py:28
  113.3 1.5 collective-permute-start.23
  114.8 2.8 %shard_map.84 = (bf16[128,512]{1,0:T(8,128)(2,1)S(1)}, bf16[128,512]{1,0:T(8,128)(2,1)S(1)}) custom-call(s32[16]{0:T(128)S(1)} %copy-done.17, bf16[64,4096]{1,0:T(8,128)(2,1)S(1)} %collective-permute-done.5.refs_1_.refs_14_.refs_17_, bf16[64,4096]{1,0:T(8,128)(2,1)S(1)} %collective-permute-done.12.refs_2_.refs_14_.refs_16_, ...), custom_call_target="tpu_custom_call" | custom-call | tf_op jit(solution)/shard_map/pallas_call | solution.py:136
  117.6 1.4 collective-permute-start.24
  119.3 6.3 %collective-permute-done.21.refs_4_ = bf16[64,4096]{1,0:T(8,128)(2,1)S(1)} collective-permute-done((bf16[64,4096]{1,0:T(8,128)(2,1)S(1)}, bf16[64,4096]{1,0:T(8,128)(2,1)S(1)}, u32[]{:S(2)}, u32[]{:S(2)}) %collective-permute-start.21) | collective-permute-done | bytes 524320 | tf_op jit(solution)/shard_map/ppermute | solution.py:28
  128.4 1.5 collective-permute-start.30
  129.9 2.6 %collective-permute-start.26 = (bf16[128,512]{1,0:T(8,128)(2,1)S(1)}, bf16[128,512]{1,0:T(8,128)(2,1)S(1)}, u32[]{:S(2)}, u32[]{:S(2)}) collective-permute-start(bf16[128,512]{1,0:T(8,128)(2,1)S(1)} %get-tuple-element.72), channel_id=1, source_target_pairs={{0,6},{1,7},{2,4},{3,5},{4,2},{5,3},{6,0},{7,1},{8,14},{9,15},{10,... | collective-permute-start | bytes 393224 | tf_op jit(solution)/shard_map/ppermute | solution.py:28
  132.4 2.8 %shard_map.85 = (bf16[128,512]{1,0:T(8,128)(2,1)S(1)}, bf16[128,512]{1,0:T(8,128)(2,1)S(1)}) custom-call(s32[16]{0:T(128)S(1)} %copy-done.17, bf16[64,4096]{1,0:T(8,128)(2,1)S(1)} %collective-permute-done.10.refs_1_.refs_15_.refs_18_, bf16[64,4096]{1,0:T(8,128)(2,1)S(1)} %collective-permute-done.16.refs_2_.refs_15_.refs_17_, ...), custom_call_target="tpu_custom_call" | custom-call | tf_op jit(solution)/shard_map/pallas_call | solution.py:136
  135.6 1.8 %collective-permute-start.29 = (bf16[128,512]{1,0:T(8,128)(2,1)S(1)}, bf16[128,512]{1,0:T(8,128)(2,1)S(1)}, u32[]{:S(2)}, u32[]{:S(2)}) collective-permute-start(bf16[128,512]{1,0:T(8,128)(2,1)S(1)} %get-tuple-element.78), channel_id=1, source_target_pairs={{0,6},{1,7},{2,4},{3,5},{4,2},{5,3},{6,0},{7,1},{8,14},{9,15},{10,... | collective-permute-start | bytes 393224 | tf_op jit(solution)/shard_map/ppermute | solution.py:28
  139.8 3.9 %collective-permute-done.27.refs_5_.refs_6_ = bf16[128,512]{1,0:T(8,128)(2,1)S(1)} collective-permute-done((bf16[128,512]{1,0:T(8,128)(2,1)S(1)}, bf16[128,512]{1,0:T(8,128)(2,1)S(1)}, u32[]{:S(2)}, u32[]{:S(2)}) %collective-permute-start.27) | collective-permute-done | bytes 131104 | tf_op jit(solution)/shard_map/ppermute | solution.py:28
  147.7 2.6 %shard_map.89 = bf16[128,1024]{1,0:T(8,128)(2,1)S(1)} custom-call(s32[1]{0:T(128)} %bitcast.2.place, s32[32]{0:T(128)S(1)} %copy-done.16, bf16[128,512]{1,0:T(8,128)(2,1)S(1)} %get-tuple-element.68.refs_0_.refs_1_, bf16[128,512]{1,0:T(8,128)(2,1)S(1)} %collective-permute-done.24.refs_1_.refs_2_, ...), custom_call_target="tpu_custom_call" | custom-call | tf_op jit(solution)/shard_map/pallas_call | solution.py:202
  150.3 1.5 collective-permute-start.35
  151.8 2.6 %shard_map.88 = bf16[128,1024]{1,0:T(8,128)(2,1)S(1)} custom-call(s32[1]{0:T(128)} %bitcast.3.place, s32[32]{0:T(128)S(1)} %copy-done.16, bf16[128,512]{1,0:T(8,128)(2,1)S(1)} %get-tuple-element.68.refs_0_.refs_1_, bf16[128,512]{1,0:T(8,128)(2,1)S(1)} %collective-permute-done.24.refs_1_.refs_2_, ...), custom_call_target="tpu_custom_call" | custom-call | tf_op jit(solution)/shard_map/pallas_call | solution.py:202
  155.2 3.2 %shard_map.86.refs_0_ = bf16[128,4096]{1,0:T(8,128)(2,1)} custom-call(s32[1]{0:T(128)} %bitcast.3.place, s32[32]{0:T(128)S(1)} %copy-done.16, bf16[128,512]{1,0:T(8,128)(2,1)S(1)} %get-tuple-element.68.refs_0_.refs_1_, bf16[128,512]{1,0:T(8,128)(2,1)S(1)} %collective-permute-done.24.refs_1_.refs_2_, ...), custom_call_target="tpu_custom_call" | custom-call | tf_op jit(solution)/shard_map/pallas_call | solution.py:202
  158.4 3.2 %shard_map.87.mine = bf16[128,4096]{1,0:T(8,128)(2,1)} custom-call(s32[1]{0:T(128)} %bitcast.2.place, s32[32]{0:T(128)S(1)} %copy-done.16, bf16[128,4096]{1,0:T(8,128)(2,1)} %shard_map.86.refs_0_, bf16[128,512]{1,0:T(8,128)(2,1)S(1)} %get-tuple-element.68.refs_0_.refs_1_, ...), custom_call_target="tpu_custom_call", output_to_operand_aliasing={{}: (2, {})} | custom-call | tf_op jit(solution)/shard_map/pallas_call | solution.py:202
  161.6 2.9 %collective-permute-done.34.theirs_a = bf16[128,1024]{1,0:T(8,128)(2,1)S(1)} collective-permute-done((bf16[128,1024]{1,0:T(8,128)(2,1)S(1)}, bf16[128,1024]{1,0:T(8,128)(2,1)S(1)}, u32[]{:S(2)}, u32[]{:S(2)}) %collective-permute-start.34) | collective-permute-done | bytes 262176 | tf_op jit(solution)/shard_map/ppermute | solution.py:28
  (104 shorter events, 22.7 us)
Async XLA Ops:
  0.0 30.4 %collective-permute-start.4 = (bf16[256,4096]{1,0:T(8,128)(2,1)}, bf16[256,4096]{1,0:T(8,128)(2,1)}, u32[]{:S(2)}, u32[]{:S(2)}) collective-permute-start(bf16[256,4096]{1,0:T(8,128)(2,1)} %refs_8_.5), channel_id=1, source_target_pairs={{0,1},{1,0},{2,3},{3,2},{4,5},{5,4},{6,7},{7,6},{8,9},{9,8},{10,11... | collective-permute-start | bytes 6291464 | tf_op jit(solution)/shard_map/ppermute | solution.py:28
  0.5 29.1 %collective-permute-start = (bf16[64,4096]{1,0:T(8,128)(2,1)}, bf16[64,4096]{1,0:T(8,128)(2,1)S(1)}, u32[]{:S(2)}, u32[]{:S(2)}) collective-permute-start(bf16[64,4096]{1,0:T(8,128)(2,1)} %refs_0_.3), channel_id=1, source_target_pairs={{0,8},{1,9},{2,10},{3,11},{4,12},{5,13},{6,14},{7,15},{8,0},{9,1},... | collective-permute-start | bytes 1572872 | tf_op jit(solution)/shard_map/ppermute | solution.py:33
  4.1 25.5 %collective-permute-start.1 = (bf16[64,4096]{1,0:T(8,128)(2,1)}, bf16[64,4096]{1,0:T(8,128)(2,1)S(1)}, u32[]{:S(2)}, u32[]{:S(2)}) collective-permute-start(bf16[64,4096]{1,0:T(8,128)(2,1)} %refs_0_.3), channel_id=1, source_target_pairs={{0,2},{1,3},{2,0},{3,1},{4,6},{5,7},{6,4},{7,5},{8,10},{9,11},{10,... | collective-permute-start | bytes 1572872 | tf_op jit(solution)/shard_map/ppermute | solution.py:28
  5.6 24.8 %collective-permute-start.2 = (bf16[64,4096]{1,0:T(8,128)(2,1)}, bf16[64,4096]{1,0:T(8,128)(2,1)}, u32[]{:S(2)}, u32[]{:S(2)}) collective-permute-start(bf16[64,4096]{1,0:T(8,128)(2,1)} %refs_0_.3), channel_id=1, source_target_pairs={{0,4},{1,5},{2,6},{3,7},{4,0},{5,1},{6,2},{7,3},{8,12},{9,13},{10,... | collective-permute-start | bytes 1572872 | tf_op jit(solution)/shard_map/ppermute | solution.py:28
  8.5 21.1 %collective-permute-start.3 = (bf16[256,1024]{1,0:T(8,128)(2,1)S(1)}, bf16[256,1024]{1,0:T(8,128)(2,1)S(1)}, u32[]{:S(2)}, u32[]{:S(2)}) collective-permute-start(bf16[256,1024]{1,0:T(8,128)(2,1)S(1)} %get-tuple-element.88), channel_id=1, source_target_pairs={{0,2},{1,3},{2,0},{3,1},{4,6},{5,7},{6,4},{7,5},{8,10},{9,11},{10,... | collective-permute-start | bytes 1572872 | tf_op jit(solution)/shard_map/ppermute | solution.py:28
  30.4 27.9 %collective-permute-start.9 = (bf16[4096,768]{1,0:T(8,128)(2,1)S(1)}, bf16[4096,768]{1,0:T(8,128)(2,1)S(1)}, u32[]{:S(2)}, u32[]{:S(2)}) collective-permute-start(bf16[4096,768]{1,0:T(8,128)(2,1)S(1)} %pad_maximum_fusion), channel_id=1, source_target_pairs={{0,1},{1,0},{2,3},{3,2},{4,5},{5,4},{6,7},{7,6},{8,9},{9,8},{10,11... | collective-permute-start | bytes 18874376 | tf_op jit(solution)/shard_map/ppermute | solution.py:28
  30.5 26.6 %collective-permute-start.5 = (bf16[64,4096]{1,0:T(8,128)(2,1)S(1)}, bf16[64,4096]{1,0:T(8,128)(2,1)S(1)}, u32[]{:S(2)}, u32[]{:S(2)}) collective-permute-start(bf16[64,4096]{1,0:T(8,128)(2,1)S(1)} %slice.6), channel_id=1, source_target_pairs={{0,8},{1,9},{2,10},{3,11},{4,12},{5,13},{6,14},{7,15},{8,0},{9,1},... | collective-permute-start | bytes 1572872 | tf_op jit(solution)/shard_map/ppermute | solution.py:33
  30.9 26.2 %collective-permute-start.6 = (bf16[64,4096]{1,0:T(8,128)(2,1)S(1)}, bf16[64,4096]{1,0:T(8,128)(2,1)S(1)}, u32[]{:S(2)}, u32[]{:S(2)}) collective-permute-start(bf16[64,4096]{1,0:T(8,128)(2,1)S(1)} %collective-permute-done.refs_0_), channel_id=1, source_target_pairs={{0,4},{1,5},{2,6},{3,7},{4,0},{5,1},{6,2},{7,3},{8,12},{9,13},{10,... | collective-permute-start | bytes 1572872 | tf_op jit(solution)/shard_map/ppermute | solution.py:28
  33.4 23.8 %collective-permute-start.7 = (bf16[64,4096]{1,0:T(8,128)(2,1)S(1)}, bf16[64,4096]{1,0:T(8,128)(2,1)S(1)}, u32[]{:S(2)}, u32[]{:S(2)}) collective-permute-start(bf16[64,4096]{1,0:T(8,128)(2,1)S(1)} %collective-permute-done.refs_0_), channel_id=1, source_target_pairs={{0,2},{1,3},{2,0},{3,1},{4,6},{5,7},{6,4},{7,5},{8,10},{9,11},{10,... | collective-permute-start | bytes 1572872 | tf_op jit(solution)/shard_map/ppermute | solution.py:28
  34.8 23.5 %collective-permute-start.8 = (bf16[64,4096]{1,0:T(8,128)(2,1)}, bf16[64,4096]{1,0:T(8,128)(2,1)S(1)}, u32[]{:S(2)}, u32[]{:S(2)}) collective-permute-start(bf16[64,4096]{1,0:T(8,128)(2,1)} %collective-permute-done.2.refs_2_), channel_id=1, source_target_pairs={{0,2},{1,3},{2,0},{3,1},{4,6},{5,7},{6,4},{7,5},{8,10},{9,11},{10,... | collective-permute-start | bytes 1572872 | tf_op jit(solution)/shard_map/ppermute | solution.py:28
  58.3 26.6 %collective-permute-start.11 = (bf16[64,4096]{1,0:T(8,128)(2,1)S(1)}, bf16[64,4096]{1,0:T(8,128)(2,1)S(1)}, u32[]{:S(2)}, u32[]{:S(2)}) collective-permute-start(bf16[64,4096]{1,0:T(8,128)(2,1)S(1)} %collective-permute-done.5.refs_1_.refs_14_.refs_17_), channel_id=1, source_target_pairs={{0,4},{1,5},{2,6},{3,7},{4,0},{5,1},{6,2},{7,3},{8,12},{9,13},{10,... | collective-permute-start | bytes 1572872 | tf_op jit(solution)/shard_map/ppermute | solution.py:28
  58.6 26.3 %collective-permute-start.12 = (bf16[64,4096]{1,0:T(8,128)(2,1)S(1)}, bf16[64,4096]{1,0:T(8,128)(2,1)S(1)}, u32[]{:S(2)}, u32[]{:S(2)}) collective-permute-start(bf16[64,4096]{1,0:T(8,128)(2,1)S(1)} %collective-permute-done.5.refs_1_.refs_14_.refs_17_), channel_id=1, source_target_pairs={{0,2},{1,3},{2,0},{3,1},{4,6},{5,7},{6,4},{7,5},{8,10},{9,11},{10,... | collective-permute-start | bytes 1572872 | tf_op jit(solution)/shard_map/ppermute | solution.py:28
  60.1 24.9 %collective-permute-start.10 = (bf16[64,4096]{1,0:T(8,128)(2,1)S(1)}, bf16[64,4096]{1,0:T(8,128)(2,1)S(1)}, u32[]{:S(2)}, u32[]{:S(2)}) collective-permute-start(bf16[64,4096]{1,0:T(8,128)(2,1)S(1)} %slice.7), channel_id=1, source_target_pairs={{0,8},{1,9},{2,10},{3,11},{4,12},{5,13},{6,14},{7,15},{8,0},{9,1},... | collective-permute-start | bytes 1572872 | tf_op jit(solution)/shard_map/ppermute | solution.py:33
  62.2 22.8 %collective-permute-start.13 = (bf16[64,4096]{1,0:T(8,128)(2,1)S(1)}, bf16[64,4096]{1,0:T(8,128)(2,1)S(1)}, u32[]{:S(2)}, u32[]{:S(2)}) collective-permute-start(bf16[64,4096]{1,0:T(8,128)(2,1)S(1)} %collective-permute-done.6.refs_2_), channel_id=1, source_target_pairs={{0,2},{1,3},{2,0},{3,1},{4,6},{5,7},{6,4},{7,5},{8,10},{9,11},{10,... | collective-permute-start | bytes 1572872 | tf_op jit(solution)/shard_map/ppermute | solution.py:28
  62.7 22.3 %collective-permute-start.14 = (bf16[256,1024]{1,0:T(8,128)(2,1)S(1)}, bf16[256,1024]{1,0:T(8,128)(2,1)S(1)}, u32[]{:S(2)}, u32[]{:S(2)}) collective-permute-start(bf16[256,1024]{1,0:T(8,128)(2,1)S(1)} %collective-permute-done.3.refs_9_), channel_id=1, source_target_pairs={{0,16},{16,0},{1,17},{17,1},{2,18},{18,2},{3,19},{19,3},{4,20},{20... | collective-permute-start | bytes 1572872 | tf_op jit(solution)/shard_map/ppermute | solution.py:45
  85.1 25.7 %collective-permute-start.19 = (bf16[512,1024]{1,0:T(8,128)(2,1)S(1)}, bf16[512,1024]{1,0:T(8,128)(2,1)S(1)}, u32[]{:S(2)}, u32[]{:S(2)}) collective-permute-start(bf16[512,1024]{1,0:T(8,128)(2,1)S(1)} %pad_maximum_fusion.1), channel_id=1, source_target_pairs={{0,1},{1,0},{2,3},{3,2},{4,5},{5,4},{6,7},{7,6},{8,9},{9,8},{10,11... | collective-permute-start | bytes 3145736 | tf_op jit(solution)/shard_map/ppermute | solution.py:28
  85.2 14.8 %collective-permute-start.15 = (bf16[64,4096]{1,0:T(8,128)(2,1)S(1)}, bf16[64,4096]{1,0:T(8,128)(2,1)S(1)}, u32[]{:S(2)}, u32[]{:S(2)}) collective-permute-start(bf16[64,4096]{1,0:T(8,128)(2,1)S(1)} %collective-permute-done.10.refs_1_.refs_15_.refs_18_), channel_id=1, source_target_pairs={{0,4},{1,5},{2,6},{3,7},{4,0},{5,1},{6,2},{7,3},{8,12},{9,13},{10,... | collective-permute-start | bytes 1572872 | tf_op jit(solution)/shard_map/ppermute | solution.py:28
  85.3 14.8 %collective-permute-start.16 = (bf16[64,4096]{1,0:T(8,128)(2,1)S(1)}, bf16[64,4096]{1,0:T(8,128)(2,1)S(1)}, u32[]{:S(2)}, u32[]{:S(2)}) collective-permute-start(bf16[64,4096]{1,0:T(8,128)(2,1)S(1)} %collective-permute-done.10.refs_1_.refs_15_.refs_18_), channel_id=1, source_target_pairs={{0,2},{1,3},{2,0},{3,1},{4,6},{5,7},{6,4},{7,5},{8,10},{9,11},{10,... | collective-permute-start | bytes 1572872 | tf_op jit(solution)/shard_map/ppermute | solution.py:28
  86.1 24.6 %collective-permute-start.17 = (bf16[64,4096]{1,0:T(8,128)(2,1)S(1)}, bf16[64,4096]{1,0:T(8,128)(2,1)S(1)}, u32[]{:S(2)}, u32[]{:S(2)}) collective-permute-start(bf16[64,4096]{1,0:T(8,128)(2,1)S(1)} %collective-permute-done.11.refs_3_), channel_id=1, source_target_pairs={{0,2},{1,3},{2,0},{3,1},{4,6},{5,7},{6,4},{7,5},{8,10},{9,11},{10,... | collective-permute-start | bytes 1572872 | tf_op jit(solution)/shard_map/ppermute | solution.py:28
  87.3 23.4 %collective-permute-start.18 = (bf16[256,1024]{1,0:T(8,128)(2,1)S(1)}, bf16[256,1024]{1,0:T(8,128)(2,1)S(1)}, u32[]{:S(2)}, u32[]{:S(2)}) collective-permute-start(bf16[256,1024]{1,0:T(8,128)(2,1)S(1)} %get-tuple-element.61), channel_id=1, source_target_pairs={{0,4},{1,5},{2,6},{3,7},{4,0},{5,1},{6,2},{7,3},{8,12},{9,13},{10,... | collective-permute-start | bytes 1572872 | tf_op jit(solution)/shard_map/ppermute | solution.py:28
  110.8 14.8 %collective-permute-start.21 = (bf16[64,4096]{1,0:T(8,128)(2,1)S(1)}, bf16[64,4096]{1,0:T(8,128)(2,1)S(1)}, u32[]{:S(2)}, u32[]{:S(2)}) collective-permute-start(bf16[64,4096]{1,0:T(8,128)(2,1)S(1)} %collective-permute-done.15.refs_3_), channel_id=1, source_target_pairs={{0,2},{1,3},{2,0},{3,1},{4,6},{5,7},{6,4},{7,5},{8,10},{9,11},{10,... | collective-permute-start | bytes 1572872 | tf_op jit(solution)/shard_map/ppermute | solution.py:28
  111.5 14.8 %collective-permute-start.22 = (bf16[256,1024]{1,0:T(8,128)(2,1)S(1)}, bf16[256,1024]{1,0:T(8,128)(2,1)S(1)}, u32[]{:S(2)}, u32[]{:S(2)}) collective-permute-start(bf16[256,1024]{1,0:T(8,128)(2,1)S(1)} %collective-permute-done.3.refs_9_), channel_id=1, source_target_pairs={{0,4},{1,5},{2,6},{3,7},{4,0},{5,1},{6,2},{7,3},{8,12},{9,13},{10,... | collective-permute-start | bytes 1572872 | tf_op jit(solution)/shard_map/ppermute | solution.py:28
  113.3 13.7 %collective-permute-start.23 = (bf16[256,1024]{1,0:T(8,128)(2,1)S(1)}, bf16[256,1024]{1,0:T(8,128)(2,1)S(1)}, u32[]{:S(2)}, u32[]{:S(2)}) collective-permute-start(bf16[256,1024]{1,0:T(8,128)(2,1)S(1)} %collective-permute-done.18), channel_id=1, source_target_pairs={{0,16},{16,0},{1,17},{17,1},{2,18},{18,2},{3,19},{19,3},{4,20},{20... | collective-permute-start | bytes 1572872 | tf_op jit(solution)/shard_map/ppermute | solution.py:45
  117.6 10.4 %collective-permute-start.24 = (bf16[128,512]{1,0:T(8,128)(2,1)S(1)}, bf16[128,512]{1,0:T(8,128)(2,1)S(1)}, u32[]{:S(2)}, u32[]{:S(2)}) collective-permute-start(bf16[128,512]{1,0:T(8,128)(2,1)S(1)} %get-tuple-element.68.refs_0_.refs_1_), channel_id=1, source_target_pairs={{0,2},{1,3},{2,0},{3,1},{4,6},{5,7},{6,4},{7,5},{8,10},{9,11},{10,... | collective-permute-start | bytes 393224 | tf_op jit(solution)/shard_map/ppermute | solution.py:28
  119.1 9.3 %collective-permute-start.25 = (bf16[128,512]{1,0:T(8,128)(2,1)S(1)}, bf16[128,512]{1,0:T(8,128)(2,1)S(1)}, u32[]{:S(2)}, u32[]{:S(2)}) collective-permute-start(bf16[128,512]{1,0:T(8,128)(2,1)S(1)} %get-tuple-element.72), channel_id=1, source_target_pairs={{0,4},{1,5},{2,6},{3,7},{4,0},{5,1},{6,2},{7,3},{8,12},{9,13},{10,... | collective-permute-start | bytes 393224 | tf_op jit(solution)/shard_map/ppermute | solution.py:28
  128.4 15.4 %collective-permute-start.30 = (bf16[256,1024]{1,0:T(8,128)(2,1)S(1)}, bf16[256,1024]{1,0:T(8,128)(2,1)S(1)}, u32[]{:S(2)}, u32[]{:S(2)}) collective-permute-start(bf16[256,1024]{1,0:T(8,128)(2,1)S(1)} %collective-permute-done.22), channel_id=1, source_target_pairs={{0,16},{16,0},{1,17},{17,1},{2,18},{18,2},{3,19},{19,3},{4,20},{20... | collective-permute-start | bytes 1572872 | tf_op jit(solution)/shard_map/ppermute | solution.py:45
  129.9 10.0 %collective-permute-start.26 = (bf16[128,512]{1,0:T(8,128)(2,1)S(1)}, bf16[128,512]{1,0:T(8,128)(2,1)S(1)}, u32[]{:S(2)}, u32[]{:S(2)}) collective-permute-start(bf16[128,512]{1,0:T(8,128)(2,1)S(1)} %get-tuple-element.72), channel_id=1, source_target_pairs={{0,6},{1,7},{2,4},{3,5},{4,2},{5,3},{6,0},{7,1},{8,14},{9,15},{10,... | collective-permute-start | bytes 393224 | tf_op jit(solution)/shard_map/ppermute | solution.py:28
  135.2 8.5 %collective-permute-start.28 = (bf16[128,512]{1,0:T(8,128)(2,1)S(1)}, bf16[128,512]{1,0:T(8,128)(2,1)S(1)}, u32[]{:S(2)}, u32[]{:S(2)}) collective-permute-start(bf16[128,512]{1,0:T(8,128)(2,1)S(1)} %get-tuple-element.78), channel_id=1, source_target_pairs={{0,4},{1,5},{2,6},{3,7},{4,0},{5,1},{6,2},{7,3},{8,12},{9,13},{10,... | collective-permute-start | bytes 393224 | tf_op jit(solution)/shard_map/ppermute | solution.py:28
  135.6 8.2 %collective-permute-start.29 = (bf16[128,512]{1,0:T(8,128)(2,1)S(1)}, bf16[128,512]{1,0:T(8,128)(2,1)S(1)}, u32[]{:S(2)}, u32[]{:S(2)}) collective-permute-start(bf16[128,512]{1,0:T(8,128)(2,1)S(1)} %get-tuple-element.78), channel_id=1, source_target_pairs={{0,6},{1,7},{2,4},{3,5},{4,2},{5,3},{6,0},{7,1},{8,14},{9,15},{10,... | collective-permute-start | bytes 393224 | tf_op jit(solution)/shard_map/ppermute | solution.py:28
  137.4 6.4 %collective-permute-start.27 = (bf16[128,512]{1,0:T(8,128)(2,1)S(1)}, bf16[128,512]{1,0:T(8,128)(2,1)S(1)}, u32[]{:S(2)}, u32[]{:S(2)}) collective-permute-start(bf16[128,512]{1,0:T(8,128)(2,1)S(1)} %get-tuple-element.77.refs_4_.refs_5_), channel_id=1, source_target_pairs={{0,2},{1,3},{2,0},{3,1},{4,6},{5,7},{6,4},{7,5},{8,10},{9,11},{10,... | collective-permute-start | bytes 393224 | tf_op jit(solution)/shard_map/ppermute | solution.py:28
  150.3 11.3 %collective-permute-start.35 = (bf16[128,1024]{1,0:T(8,128)(2,1)S(1)}, bf16[128,1024]{1,0:T(8,128)(2,1)S(1)}, u32[]{:S(2)}, u32[]{:S(2)}) collective-permute-start(bf16[128,1024]{1,0:T(8,128)(2,1)S(1)} %shard_map.89), channel_id=1, source_target_pairs={{0,2},{1,3},{2,0},{3,1},{4,6},{5,7},{6,4},{7,5},{8,10},{9,11},{10,... | collective-permute-start | bytes 786440 | tf_op jit(solution)/shard_map/ppermute | solution.py:28
  154.4 10.2 %collective-permute-start.34 = (bf16[128,1024]{1,0:T(8,128)(2,1)S(1)}, bf16[128,1024]{1,0:T(8,128)(2,1)S(1)}, u32[]{:S(2)}, u32[]{:S(2)}) collective-permute-start(bf16[128,1024]{1,0:T(8,128)(2,1)S(1)} %shard_map.88), channel_id=1, source_target_pairs={{0,2},{1,3},{2,0},{3,1},{4,6},{5,7},{6,4},{7,5},{8,10},{9,11},{10,... | collective-permute-start | bytes 786440 | tf_op jit(solution)/shard_map/ppermute | solution.py:28
  (28 other events, 605.5 us)

commit v7 on v6

--- a/solution.py
+++ b/solution.py
@@ -85,7 +85,7 @@
 def attend_kernel(j, ring, *refs):
     mem_len, x0, x1, x2, x3, query_own, query_oth = refs[:7]
     kv_own, kv_oth = refs[7:9]
-    outs, normed = refs[9:11], refs[11]
+    earlier, outs, normed = refs[9:-3 - j], refs[-3 - j:-1], refs[-1]
     width = query_own.shape[1]
     heads = 2 * width // HD
     me = lax.axis_index("section")
@@ -129,19 +129,23 @@
             outs[k // 2][k % 2 * FR:(k % 2 + 1) * FR, h * HD:(h + 1) * HD] = dot(
                 probs[at:at + FR], values[k][:, h * HD:(h + 1) * HD]
             ).astype(BF16)
-
-
-def attend(j, ring, mem_len, pieces, weights, kv):
+    if earlier:
+        outs[2][:2 * FR, :] = earlier[0][...]
+        outs[2][2 * FR:, :] = outs[1][...]
+
+
+def attend(j, ring, mem_len, pieces, weights, kv, *earlier):
     depth, width = weights[0].shape
+    heights = [2 * FR] * 2 + [4 * FR] * len(earlier)
     return pl.pallas_call(
         functools.partial(attend_kernel, j, ring),
-        out_shape=[jax.ShapeDtypeStruct((2 * FR, 2 * width), BF16)] * 2,
-        in_specs=[pl.BlockSpec(memory_space=pltpu.SMEM)] + whole(8),
-        out_specs=whole(2),
+        out_shape=[jax.ShapeDtypeStruct((height, 2 * width), BF16) for height in heights],
+        in_specs=[pl.BlockSpec(memory_space=pltpu.SMEM)] + whole(8 + len(earlier)),
+        out_specs=whole(len(heights)),
         scratch_shapes=[pltpu.VMEM((4 * FR, depth), BF16)],
         compiler_params=pltpu.CompilerParams(vmem_limit_bytes=VMEM_BYTES),
         cost_estimate=pl.CostEstimate(flops=0, bytes_accessed=0, transcendentals=0),
-    )(mem_len, *pieces, *weights, *kv)
+    )(mem_len, *pieces, *weights, *kv, *earlier)
 
 
 def project_kernel(near, skip, place, tok_len, *refs):
@@ -183,7 +187,10 @@
     def here(i, place):
         return 0, i
 
-    att_specs = [pl.BlockSpec((2 * FR, 2 * width), lambda i, place: (0, 0))] * 8
+    att_specs = [
+        pl.BlockSpec((2 * FR, 2 * width), lambda i, place, block=block: (block, 0)) for _, block in att
+    ]
+    att = [array for array, _ in att]
     weights, weight_specs = [], []
     into = [] if near or into is None else [into]
     for mine, others in zip((own, oth), pieces):
@@ -301,16 +308,16 @@
     kv = [kv_second, flip(kv_second, CORE)]
     first = [first_hop, first_near, first_far, first_diag]
     here, there = attend(0, ring, mem_len, first, query_pair, kv)
-    att = [here, flip(here, NEAR), flip(there, FAR), flip(there, NEAR | FAR)]
+    att = [here, flip(here, NEAR), flip(there, FAR)]
     last_diag, out_diag, cross_far, *att[1:3] = together(
         last_diag, out_diag, cross_far, *att[1:3]
     )
     cross_diag = across(out_diag)
     last = [last_hop, last_near, last_far, last_diag]
-    here, there = attend(1, ring, mem_len, last, query_pair, kv)
-    att += [here, flip(here, NEAR), flip(there, FAR), flip(there, NEAR | FAR)]
+    here, there, both = attend(1, ring, mem_len, last, query_pair, kv, there)
+    att += [here, flip(here, NEAR), flip(there, FAR), flip(both, NEAR | FAR)]
     fetched = jnp.concatenate([out_far, out_diag], 0)
-    fetched, cross_far, cross_diag = together(fetched, cross_far, cross_diag, att[3], *att[5:])[:3]
+    fetched, cross_diag = together(fetched, cross_diag, *att[4:])[:2]
     handed = [cross_far, cross_diag]
     handed_core = [flip(part, CORE) for part in handed]
     fetched_core = flip(after(fetched, *handed_core), CORE)
@@ -322,6 +329,8 @@
     quarters = jnp.stack(
         [2 * side + group, 2 * side + 1 - group, 2 - 2 * side + group, 3 - 2 * side - group]
     ).astype(jnp.int32)
+    att = [(att[k], 0) for k in (0, 1, 2, 6, 3, 4, 5)] + [(att[6], 1)]
+
     def part(near, n, pieces, into=None):
         at = 1 if near else 0
         return project(

time: 166 us -> 165 us (level)
  starting transfers between devices: 38.9 us -> 35.8 us
    ppermute x30 -> x29, starting transfers between devices: 28.3 us -> 25.3 us  [flip(): return lax.ppermute(value, 'section', [(i, i ^ bits) for i in range(size)])]
    ppermute x30 -> x29, waiting for transfers between devices: 55 us -> 56.6 us  [flip(): return lax.ppermute(value, 'section', [(i, i ^ bits) for i in range(size)])]
  transfers between devices with their start and end apart: 36 -> 35, of which waited for: 16 -> 15; matrix products, arithmetic and copies ran while one was open for 3% -> 3% of each run, Pallas kernels for 14% -> 14%
where the time goes in v7:
time: 165 us
  waiting for transfers between devices  96.4 us (58%)
  starting transfers between devices  35.8 us (22%)
  Pallas kernels  24.4 us (15%)
  other arithmetic  4.33 us (3%)
  local copies, waits for them, and re-layouts  3.83 us (2%)
    ppermute x29, waiting for transfers between devices, flip(): return lax.ppermute(value, 'section', [(i, i ^ bits) for i in range(size)])  56.6 us
    ppermute x3, waiting for transfers between devices, hop(): lax.ppermute(value, 'section', [(i, (i + GROUP) % size) for i in range(si...  39.1 us
    ppermute x29, starting transfers between devices, flip(): return lax.ppermute(value, 'section', [(i, i ^ bits) for i in range(size)])  25.3 us
    pallas_call x4, Pallas kernels, project(): pl.pallas_call(functools.partial(project_kernel, near, len(into)), out_sh...  11.7 us
    ppermute x3, starting transfers between devices, hop(): lax.ppermute(value, 'section', [(i, (i + GROUP) % size) for i in range(si...  6.08 us
    pallas_call x2, Pallas kernels, keys_values(): pl.pallas_call(keys_values_kernel, out_shape=jax.ShapeDtypeStruct((total,...  5.73 us
    pallas_call x2, Pallas kernels, attend(): pl.pallas_call(functools.partial(attend_kernel, j, ring), out_shape=[jax....  5.55 us
    ppermute x3, starting transfers between devices, across(): return lax.ppermute(value, 'groups', [(0, 1), (1, 0)])  4.47 us
  transfers between devices with their start and end apart: 35, of which 15 were waited for; matrix products, arithmetic and copies ran while one was open for 3% of the time, Pallas kernels for 14%

profile of v7, /device:TPU:0, one launch (start us, length us, event | category | flops | bytes accessed | tf_op | source)
XLA Modules:
  0.0 165.1 jit_solution(5918432909722518020)
XLA Ops:
  0.5 3.6 %collective-permute-start = (bf16[64,4096]{1,0:T(8,128)(2,1)}, bf16[64,4096]{1,0:T(8,128)(2,1)S(1)}, u32[]{:S(2)}, u32[]{:S(2)}) collective-permute-start(bf16[64,4096]{1,0:T(8,128)(2,1)} %refs_0_.3), channel_id=1, source_target_pairs={{0,8},{1,9},{2,10},{3,11},{4,12},{5,13},{6,14},{7,15},{8,0},{9,1},... | collective-permute-start | bytes 1572872 | tf_op jit(solution)/shard_map/ppermute | solution.py:33
  4.1 1.5 collective-permute-start.1
  5.6 1.6 collective-permute-start.2
  9.1 3.1 %pad_maximum_fusion = bf16[4096,768]{1,0:T(8,128)(2,1)S(1)} fusion(bf16[4096,256]{1,0:T(8,128)(2,1)} %refs_5_.7, bf16[4096,256]{1,0:T(8,128)(2,1)S(1)} %copy-done, bf16[4096,256]{1,0:T(8,128)(2,1)} %refs_4_.3), kind=kLoop, calls=%fused_computation | loop fusion | flops 18874368 | bytes 12582912 | tf_op jit(solution)/shard_map/concatenate | solution.py:269
  12.2 17.3 %collective-permute-done.3.refs_9_ = bf16[256,1024]{1,0:T(8,128)(2,1)S(1)} collective-permute-done((bf16[256,1024]{1,0:T(8,128)(2,1)S(1)}, bf16[256,1024]{1,0:T(8,128)(2,1)S(1)}, u32[]{:S(2)}, u32[]{:S(2)}) %collective-permute-start.3) | collective-permute-done | bytes 524320 | tf_op jit(solution)/shard_map/ppermute | solution.py:28
  30.9 2.5 %collective-permute-start.6 = (bf16[64,4096]{1,0:T(8,128)(2,1)S(1)}, bf16[64,4096]{1,0:T(8,128)(2,1)S(1)}, u32[]{:S(2)}, u32[]{:S(2)}) collective-permute-start(bf16[64,4096]{1,0:T(8,128)(2,1)S(1)} %collective-permute-done.refs_0_), channel_id=1, source_target_pairs={{0,4},{1,5},{2,6},{3,7},{4,0},{5,1},{6,2},{7,3},{8,12},{9,13},{10,... | collective-permute-start | bytes 1572872 | tf_op jit(solution)/shard_map/ppermute | solution.py:28
  33.4 1.5 collective-permute-start.7
  35.4 21.7 %collective-permute-done.5.refs_1_.refs_14_.refs_17_ = bf16[64,4096]{1,0:T(8,128)(2,1)S(1)} collective-permute-done((bf16[64,4096]{1,0:T(8,128)(2,1)S(1)}, bf16[64,4096]{1,0:T(8,128)(2,1)S(1)}, u32[]{:S(2)}, u32[]{:S(2)}) %collective-permute-start.5) | collective-permute-done | bytes 524320 | tf_op jit(solution)/shard_map/ppermute | solution.py:33
  58.6 1.4 collective-permute-start.12
  60.1 2.1 %collective-permute-start.10 = (bf16[64,4096]{1,0:T(8,128)(2,1)S(1)}, bf16[64,4096]{1,0:T(8,128)(2,1)S(1)}, u32[]{:S(2)}, u32[]{:S(2)}) collective-permute-start(bf16[64,4096]{1,0:T(8,128)(2,1)S(1)} %slice.7), channel_id=1, source_target_pairs={{0,8},{1,9},{2,10},{3,11},{4,12},{5,13},{6,14},{7,15},{8,0},{9,1},... | collective-permute-start | bytes 1572872 | tf_op jit(solution)/shard_map/ppermute | solution.py:33
  62.7 1.5 collective-permute-start.14
  64.2 3.4 %shard_map.82.refs_7_ = bf16[256,1024]{1,0:T(8,128)(2,1)S(1)} custom-call(bf16[64,4096]{1,0:T(8,128)(2,1)S(1)} %copy-done.13, bf16[64,4096]{1,0:T(8,128)(2,1)S(1)} %copy-done.15, bf16[64,4096]{1,0:T(8,128)(2,1)} %collective-permute-done.2.refs_2_, bf16[64,4096]{1,0:T(8,128)(2,1)S(1)} %collective-permute-done.8.refs_3_, bf16[4096,256]{1,0:T(8,128)(2,1)S(1)} %copy-done.1, ...), custom_call_target="tpu_custom_call" | custom-call | tf_op jit(solution)/shard_map/pallas_call | solution.py:74
  67.6 17.4 %collective-permute-done.10.refs_1_.refs_15_.refs_18_ = bf16[64,4096]{1,0:T(8,128)(2,1)S(1)} collective-permute-done((bf16[64,4096]{1,0:T(8,128)(2,1)S(1)}, bf16[64,4096]{1,0:T(8,128)(2,1)S(1)}, u32[]{:S(2)}, u32[]{:S(2)}) %collective-permute-start.10) | collective-permute-done | bytes 524320 | tf_op jit(solution)/shard_map/ppermute | solution.py:33
  87.3 1.9 %collective-permute-start.18 = (bf16[256,1024]{1,0:T(8,128)(2,1)S(1)}, bf16[256,1024]{1,0:T(8,128)(2,1)S(1)}, u32[]{:S(2)}, u32[]{:S(2)}) collective-permute-start(bf16[256,1024]{1,0:T(8,128)(2,1)S(1)} %get-tuple-element.61), channel_id=1, source_target_pairs={{0,4},{1,5},{2,6},{3,7},{4,0},{5,1},{6,2},{7,3},{8,12},{9,13},{10,... | collective-permute-start | bytes 1572872 | tf_op jit(solution)/shard_map/ppermute | solution.py:28
  89.3 2.4 %shard_map.83.refs_7_ = bf16[512,1024]{1,0:T(8,128)(2,1)S(1)} custom-call(bf16[64,4096]{1,0:T(8,128)(2,1)S(1)} %copy-done.12, bf16[64,4096]{1,0:T(8,128)(2,1)S(1)} %collective-permute-done.7.refs_1_, bf16[64,4096]{1,0:T(8,128)(2,1)S(1)} %collective-permute-done.6.refs_2_, bf16[64,4096]{1,0:T(8,128)(2,1)S(1)} %collective-permute-done.13.refs_3_, ...), custom_call_target="tpu_custom_call" | custom-call | tf_op jit(solution)/shard_map/pallas_call | solution.py:74
  91.7 8.3 %collective-permute-done.15.refs_3_ = bf16[64,4096]{1,0:T(8,128)(2,1)S(1)} collective-permute-done((bf16[64,4096]{1,0:T(8,128)(2,1)S(1)}, bf16[64,4096]{1,0:T(8,128)(2,1)S(1)}, u32[]{:S(2)}, u32[]{:S(2)}) %collective-permute-start.15) | collective-permute-done | bytes 524320 | tf_op jit(solution)/shard_map/ppermute | solution.py:28
  100.1 10.7 %collective-permute-done.17.refs_4_ = bf16[64,4096]{1,0:T(8,128)(2,1)S(1)} collective-permute-done((bf16[64,4096]{1,0:T(8,128)(2,1)S(1)}, bf16[64,4096]{1,0:T(8,128)(2,1)S(1)}, u32[]{:S(2)}, u32[]{:S(2)}) %collective-permute-start.17) | collective-permute-done | bytes 524320 | tf_op jit(solution)/shard_map/ppermute | solution.py:28
  111.5 1.8 %collective-permute-start.22 = (bf16[256,1024]{1,0:T(8,128)(2,1)S(1)}, bf16[256,1024]{1,0:T(8,128)(2,1)S(1)}, u32[]{:S(2)}, u32[]{:S(2)}) collective-permute-start(bf16[256,1024]{1,0:T(8,128)(2,1)S(1)} %collective-permute-done.3.refs_9_), channel_id=1, source_target_pairs={{0,4},{1,5},{2,6},{3,7},{4,0},{5,1},{6,2},{7,3},{8,12},{9,13},{10,... | collective-permute-start | bytes 1572872 | tf_op jit(solution)/shard_map/ppermute | solution.py:28
  113.3 1.5 collective-permute-start.23
  114.8 2.8 %shard_map.84 = (bf16[128,512]{1,0:T(8,128)(2,1)S(1)}, bf16[128,512]{1,0:T(8,128)(2,1)S(1)}) custom-call(s32[16]{0:T(128)S(1)} %copy-done.17, bf16[64,4096]{1,0:T(8,128)(2,1)S(1)} %collective-permute-done.5.refs_1_.refs_14_.refs_17_, bf16[64,4096]{1,0:T(8,128)(2,1)S(1)} %collective-permute-done.12.refs_2_.refs_14_.refs_16_, ...), custom_call_target="tpu_custom_call" | custom-call | tf_op jit(solution)/shard_map/pallas_call | solution.py:140
  117.6 1.4 collective-permute-start.24
  119.3 6.3 %collective-permute-done.21.refs_4_ = bf16[64,4096]{1,0:T(8,128)(2,1)S(1)} collective-permute-done((bf16[64,4096]{1,0:T(8,128)(2,1)S(1)}, bf16[64,4096]{1,0:T(8,128)(2,1)S(1)}, u32[]{:S(2)}, u32[]{:S(2)}) %collective-permute-start.21) | collective-permute-done | bytes 524320 | tf_op jit(solution)/shard_map/ppermute | solution.py:28
  128.4 1.5 collective-permute-start.29
  129.9 2.8 %shard_map.85 = (bf16[128,512]{1,0:T(8,128)(2,1)S(1)}, bf16[128,512]{1,0:T(8,128)(2,1)S(1)}, bf16[256,512]{1,0:T(8,128)(2,1)S(1)}) custom-call(s32[16]{0:T(128)S(1)} %copy-done.17, bf16[64,4096]{1,0:T(8,128)(2,1)S(1)} %collective-permute-done.10.refs_1_.refs_15_.refs_18_, bf16[64,4096]{1,0:T(8,128)(2,1)S(1)} %collective-permute-done.16.refs_2_.refs_15_.refs_17_, ...), custom_call_target="tpu_custom_call" | custom-call | tf_op jit(solution)/shard_map/pallas_call | solution.py:140
  132.7 2.6 %collective-permute-start.26 = (bf16[256,512]{1,0:T(8,128)(2,1)S(1)}, bf16[256,512]{1,0:T(8,128)(2,1)S(1)}, u32[]{:S(2)}, u32[]{:S(2)}) collective-permute-start(bf16[256,512]{1,0:T(8,128)(2,1)S(1)} %get-tuple-element.77), channel_id=1, source_target_pairs={{0,6},{1,7},{2,4},{3,5},{4,2},{5,3},{6,0},{7,1},{8,14},{9,15},{10,... | collective-permute-start | bytes 786440 | tf_op jit(solution)/shard_map/ppermute | solution.py:28
  137.3 6.5 %collective-permute-done.27.refs_5_.refs_6_ = bf16[128,512]{1,0:T(8,128)(2,1)S(1)} collective-permute-done((bf16[128,512]{1,0:T(8,128)(2,1)S(1)}, bf16[128,512]{1,0:T(8,128)(2,1)S(1)}, u32[]{:S(2)}, u32[]{:S(2)}) %collective-permute-start.27) | collective-permute-done | bytes 131104 | tf_op jit(solution)/shard_map/ppermute | solution.py:28
  146.7 2.6 %shard_map.89 = bf16[128,1024]{1,0:T(8,128)(2,1)S(1)} custom-call(s32[1]{0:T(128)} %bitcast.2.place, s32[32]{0:T(128)S(1)} %copy-done.16, bf16[128,512]{1,0:T(8,128)(2,1)S(1)} %get-tuple-element.68.refs_0_.refs_1_, bf16[128,512]{1,0:T(8,128)(2,1)S(1)} %collective-permute-done.24.refs_1_.refs_2_, ...), custom_call_target="tpu_custom_call" | custom-call | tf_op jit(solution)/shard_map/pallas_call | solution.py:209
  149.4 1.4 collective-permute-start.34
  150.8 2.6 %shard_map.88 = bf16[128,1024]{1,0:T(8,128)(2,1)S(1)} custom-call(s32[1]{0:T(128)} %bitcast.3.place, s32[32]{0:T(128)S(1)} %copy-done.16, bf16[128,512]{1,0:T(8,128)(2,1)S(1)} %get-tuple-element.68.refs_0_.refs_1_, bf16[128,512]{1,0:T(8,128)(2,1)S(1)} %collective-permute-done.24.refs_1_.refs_2_, ...), custom_call_target="tpu_custom_call" | custom-call | tf_op jit(solution)/shard_map/pallas_call | solution.py:209
  154.3 3.2 %shard_map.86.refs_0_ = bf16[128,4096]{1,0:T(8,128)(2,1)} custom-call(s32[1]{0:T(128)} %bitcast.3.place, s32[32]{0:T(128)S(1)} %copy-done.16, bf16[128,512]{1,0:T(8,128)(2,1)S(1)} %get-tuple-element.68.refs_0_.refs_1_, bf16[128,512]{1,0:T(8,128)(2,1)S(1)} %collective-permute-done.24.refs_1_.refs_2_, ...), custom_call_target="tpu_custom_call" | custom-call | tf_op jit(solution)/shard_map/pallas_call | solution.py:209
  157.5 3.2 %shard_map.87.mine = bf16[128,4096]{1,0:T(8,128)(2,1)} custom-call(s32[1]{0:T(128)} %bitcast.2.place, s32[32]{0:T(128)S(1)} %copy-done.16, bf16[128,4096]{1,0:T(8,128)(2,1)} %shard_map.86.refs_0_, bf16[128,512]{1,0:T(8,128)(2,1)S(1)} %get-tuple-element.68.refs_0_.refs_1_, ...), custom_call_target="tpu_custom_call", output_to_operand_aliasing={{}: (2, {})} | custom-call | tf_op jit(solution)/shard_map/pallas_call | solution.py:209
  160.7 2.9 %collective-permute-done.33.theirs_a = bf16[128,1024]{1,0:T(8,128)(2,1)S(1)} collective-permute-done((bf16[128,1024]{1,0:T(8,128)(2,1)S(1)}, bf16[128,1024]{1,0:T(8,128)(2,1)S(1)}, u32[]{:S(2)}, u32[]{:S(2)}) %collective-permute-start.33) | collective-permute-done | bytes 262176 | tf_op jit(solution)/shard_map/ppermute | solution.py:28
  (102 shorter events, 19.7 us)
Async XLA Ops:
  0.0 30.4 %collective-permute-start.4 = (bf16[256,4096]{1,0:T(8,128)(2,1)}, bf16[256,4096]{1,0:T(8,128)(2,1)}, u32[]{:S(2)}, u32[]{:S(2)}) collective-permute-start(bf16[256,4096]{1,0:T(8,128)(2,1)} %refs_8_.5), channel_id=1, source_target_pairs={{0,1},{1,0},{2,3},{3,2},{4,5},{5,4},{6,7},{7,6},{8,9},{9,8},{10,11... | collective-permute-start | bytes 6291464 | tf_op jit(solution)/shard_map/ppermute | solution.py:28
  0.5 29.1 %collective-permute-start = (bf16[64,4096]{1,0:T(8,128)(2,1)}, bf16[64,4096]{1,0:T(8,128)(2,1)S(1)}, u32[]{:S(2)}, u32[]{:S(2)}) collective-permute-start(bf16[64,4096]{1,0:T(8,128)(2,1)} %refs_0_.3), channel_id=1, source_target_pairs={{0,8},{1,9},{2,10},{3,11},{4,12},{5,13},{6,14},{7,15},{8,0},{9,1},... | collective-permute-start | bytes 1572872 | tf_op jit(solution)/shard_map/ppermute | solution.py:33
  4.1 25.5 %collective-permute-start.1 = (bf16[64,4096]{1,0:T(8,128)(2,1)}, bf16[64,4096]{1,0:T(8,128)(2,1)S(1)}, u32[]{:S(2)}, u32[]{:S(2)}) collective-permute-start(bf16[64,4096]{1,0:T(8,128)(2,1)} %refs_0_.3), channel_id=1, source_target_pairs={{0,2},{1,3},{2,0},{3,1},{4,6},{5,7},{6,4},{7,5},{8,10},{9,11},{10,... | collective-permute-start | bytes 1572872 | tf_op jit(solution)/shard_map/ppermute | solution.py:28
  5.6 24.8 %collective-permute-start.2 = (bf16[64,4096]{1,0:T(8,128)(2,1)}, bf16[64,4096]{1,0:T(8,128)(2,1)}, u32[]{:S(2)}, u32[]{:S(2)}) collective-permute-start(bf16[64,4096]{1,0:T(8,128)(2,1)} %refs_0_.3), channel_id=1, source_target_pairs={{0,4},{1,5},{2,6},{3,7},{4,0},{5,1},{6,2},{7,3},{8,12},{9,13},{10,... | collective-permute-start | bytes 1572872 | tf_op jit(solution)/shard_map/ppermute | solution.py:28
  8.5 21.1 %collective-permute-start.3 = (bf16[256,1024]{1,0:T(8,128)(2,1)S(1)}, bf16[256,1024]{1,0:T(8,128)(2,1)S(1)}, u32[]{:S(2)}, u32[]{:S(2)}) collective-permute-start(bf16[256,1024]{1,0:T(8,128)(2,1)S(1)} %get-tuple-element.88), channel_id=1, source_target_pairs={{0,2},{1,3},{2,0},{3,1},{4,6},{5,7},{6,4},{7,5},{8,10},{9,11},{10,... | collective-permute-start | bytes 1572872 | tf_op jit(solution)/shard_map/ppermute | solution.py:28
  30.4 27.9 %collective-permute-start.9 = (bf16[4096,768]{1,0:T(8,128)(2,1)S(1)}, bf16[4096,768]{1,0:T(8,128)(2,1)S(1)}, u32[]{:S(2)}, u32[]{:S(2)}) collective-permute-start(bf16[4096,768]{1,0:T(8,128)(2,1)S(1)} %pad_maximum_fusion), channel_id=1, source_target_pairs={{0,1},{1,0},{2,3},{3,2},{4,5},{5,4},{6,7},{7,6},{8,9},{9,8},{10,11... | collective-permute-start | bytes 18874376 | tf_op jit(solution)/shard_map/ppermute | solution.py:28
  30.5 26.6 %collective-permute-start.5 = (bf16[64,4096]{1,0:T(8,128)(2,1)S(1)}, bf16[64,4096]{1,0:T(8,128)(2,1)S(1)}, u32[]{:S(2)}, u32[]{:S(2)}) collective-permute-start(bf16[64,4096]{1,0:T(8,128)(2,1)S(1)} %slice.6), channel_id=1, source_target_pairs={{0,8},{1,9},{2,10},{3,11},{4,12},{5,13},{6,14},{7,15},{8,0},{9,1},... | collective-permute-start | bytes 1572872 | tf_op jit(solution)/shard_map/ppermute | solution.py:33
  30.9 26.2 %collective-permute-start.6 = (bf16[64,4096]{1,0:T(8,128)(2,1)S(1)}, bf16[64,4096]{1,0:T(8,128)(2,1)S(1)}, u32[]{:S(2)}, u32[]{:S(2)}) collective-permute-start(bf16[64,4096]{1,0:T(8,128)(2,1)S(1)} %collective-permute-done.refs_0_), channel_id=1, source_target_pairs={{0,4},{1,5},{2,6},{3,7},{4,0},{5,1},{6,2},{7,3},{8,12},{9,13},{10,... | collective-permute-start | bytes 1572872 | tf_op jit(solution)/shard_map/ppermute | solution.py:28
  33.4 23.7 %collective-permute-start.7 = (bf16[64,4096]{1,0:T(8,128)(2,1)S(1)}, bf16[64,4096]{1,0:T(8,128)(2,1)S(1)}, u32[]{:S(2)}, u32[]{:S(2)}) collective-permute-start(bf16[64,4096]{1,0:T(8,128)(2,1)S(1)} %collective-permute-done.refs_0_), channel_id=1, source_target_pairs={{0,2},{1,3},{2,0},{3,1},{4,6},{5,7},{6,4},{7,5},{8,10},{9,11},{10,... | collective-permute-start | bytes 1572872 | tf_op jit(solution)/shard_map/ppermute | solution.py:28
  34.8 23.5 %collective-permute-start.8 = (bf16[64,4096]{1,0:T(8,128)(2,1)}, bf16[64,4096]{1,0:T(8,128)(2,1)S(1)}, u32[]{:S(2)}, u32[]{:S(2)}) collective-permute-start(bf16[64,4096]{1,0:T(8,128)(2,1)} %collective-permute-done.2.refs_2_), channel_id=1, source_target_pairs={{0,2},{1,3},{2,0},{3,1},{4,6},{5,7},{6,4},{7,5},{8,10},{9,11},{10,... | collective-permute-start | bytes 1572872 | tf_op jit(solution)/shard_map/ppermute | solution.py:28
  58.3 26.6 %collective-permute-start.11 = (bf16[64,4096]{1,0:T(8,128)(2,1)S(1)}, bf16[64,4096]{1,0:T(8,128)(2,1)S(1)}, u32[]{:S(2)}, u32[]{:S(2)}) collective-permute-start(bf16[64,4096]{1,0:T(8,128)(2,1)S(1)} %collective-permute-done.5.refs_1_.refs_14_.refs_17_), channel_id=1, source_target_pairs={{0,4},{1,5},{2,6},{3,7},{4,0},{5,1},{6,2},{7,3},{8,12},{9,13},{10,... | collective-permute-start | bytes 1572872 | tf_op jit(solution)/shard_map/ppermute | solution.py:28
  58.6 26.3 %collective-permute-start.12 = (bf16[64,4096]{1,0:T(8,128)(2,1)S(1)}, bf16[64,4096]{1,0:T(8,128)(2,1)S(1)}, u32[]{:S(2)}, u32[]{:S(2)}) collective-permute-start(bf16[64,4096]{1,0:T(8,128)(2,1)S(1)} %collective-permute-done.5.refs_1_.refs_14_.refs_17_), channel_id=1, source_target_pairs={{0,2},{1,3},{2,0},{3,1},{4,6},{5,7},{6,4},{7,5},{8,10},{9,11},{10,... | collective-permute-start | bytes 1572872 | tf_op jit(solution)/shard_map/ppermute | solution.py:28
  60.1 24.9 %collective-permute-start.10 = (bf16[64,4096]{1,0:T(8,128)(2,1)S(1)}, bf16[64,4096]{1,0:T(8,128)(2,1)S(1)}, u32[]{:S(2)}, u32[]{:S(2)}) collective-permute-start(bf16[64,4096]{1,0:T(8,128)(2,1)S(1)} %slice.7), channel_id=1, source_target_pairs={{0,8},{1,9},{2,10},{3,11},{4,12},{5,13},{6,14},{7,15},{8,0},{9,1},... | collective-permute-start | bytes 1572872 | tf_op jit(solution)/shard_map/ppermute | solution.py:33
  62.2 22.8 %collective-permute-start.13 = (bf16[64,4096]{1,0:T(8,128)(2,1)S(1)}, bf16[64,4096]{1,0:T(8,128)(2,1)S(1)}, u32[]{:S(2)}, u32[]{:S(2)}) collective-permute-start(bf16[64,4096]{1,0:T(8,128)(2,1)S(1)} %collective-permute-done.6.refs_2_), channel_id=1, source_target_pairs={{0,2},{1,3},{2,0},{3,1},{4,6},{5,7},{6,4},{7,5},{8,10},{9,11},{10,... | collective-permute-start | bytes 1572872 | tf_op jit(solution)/shard_map/ppermute | solution.py:28
  62.7 22.3 %collective-permute-start.14 = (bf16[256,1024]{1,0:T(8,128)(2,1)S(1)}, bf16[256,1024]{1,0:T(8,128)(2,1)S(1)}, u32[]{:S(2)}, u32[]{:S(2)}) collective-permute-start(bf16[256,1024]{1,0:T(8,128)(2,1)S(1)} %collective-permute-done.3.refs_9_), channel_id=1, source_target_pairs={{0,16},{16,0},{1,17},{17,1},{2,18},{18,2},{3,19},{19,3},{4,20},{20... | collective-permute-start | bytes 1572872 | tf_op jit(solution)/shard_map/ppermute | solution.py:45
  85.1 25.7 %collective-permute-start.19 = (bf16[512,1024]{1,0:T(8,128)(2,1)S(1)}, bf16[512,1024]{1,0:T(8,128)(2,1)S(1)}, u32[]{:S(2)}, u32[]{:S(2)}) collective-permute-start(bf16[512,1024]{1,0:T(8,128)(2,1)S(1)} %pad_maximum_fusion.1), channel_id=1, source_target_pairs={{0,1},{1,0},{2,3},{3,2},{4,5},{5,4},{6,7},{7,6},{8,9},{9,8},{10,11... | collective-permute-start | bytes 3145736 | tf_op jit(solution)/shard_map/ppermute | solution.py:28
  85.2 14.8 %collective-permute-start.15 = (bf16[64,4096]{1,0:T(8,128)(2,1)S(1)}, bf16[64,4096]{1,0:T(8,128)(2,1)S(1)}, u32[]{:S(2)}, u32[]{:S(2)}) collective-permute-start(bf16[64,4096]{1,0:T(8,128)(2,1)S(1)} %collective-permute-done.10.refs_1_.refs_15_.refs_18_), channel_id=1, source_target_pairs={{0,4},{1,5},{2,6},{3,7},{4,0},{5,1},{6,2},{7,3},{8,12},{9,13},{10,... | collective-permute-start | bytes 1572872 | tf_op jit(solution)/shard_map/ppermute | solution.py:28
  85.2 14.8 %collective-permute-start.16 = (bf16[64,4096]{1,0:T(8,128)(2,1)S(1)}, bf16[64,4096]{1,0:T(8,128)(2,1)S(1)}, u32[]{:S(2)}, u32[]{:S(2)}) collective-permute-start(bf16[64,4096]{1,0:T(8,128)(2,1)S(1)} %collective-permute-done.10.refs_1_.refs_15_.refs_18_), channel_id=1, source_target_pairs={{0,2},{1,3},{2,0},{3,1},{4,6},{5,7},{6,4},{7,5},{8,10},{9,11},{10,... | collective-permute-start | bytes 1572872 | tf_op jit(solution)/shard_map/ppermute | solution.py:28
  86.1 24.6 %collective-permute-start.17 = (bf16[64,4096]{1,0:T(8,128)(2,1)S(1)}, bf16[64,4096]{1,0:T(8,128)(2,1)S(1)}, u32[]{:S(2)}, u32[]{:S(2)}) collective-permute-start(bf16[64,4096]{1,0:T(8,128)(2,1)S(1)} %collective-permute-done.11.refs_3_), channel_id=1, source_target_pairs={{0,2},{1,3},{2,0},{3,1},{4,6},{5,7},{6,4},{7,5},{8,10},{9,11},{10,... | collective-permute-start | bytes 1572872 | tf_op jit(solution)/shard_map/ppermute | solution.py:28
  87.3 23.4 %collective-permute-start.18 = (bf16[256,1024]{1,0:T(8,128)(2,1)S(1)}, bf16[256,1024]{1,0:T(8,128)(2,1)S(1)}, u32[]{:S(2)}, u32[]{:S(2)}) collective-permute-start(bf16[256,1024]{1,0:T(8,128)(2,1)S(1)} %get-tuple-element.61), channel_id=1, source_target_pairs={{0,4},{1,5},{2,6},{3,7},{4,0},{5,1},{6,2},{7,3},{8,12},{9,13},{10,... | collective-permute-start | bytes 1572872 | tf_op jit(solution)/shard_map/ppermute | solution.py:28
  110.8 14.8 %collective-permute-start.21 = (bf16[64,4096]{1,0:T(8,128)(2,1)S(1)}, bf16[64,4096]{1,0:T(8,128)(2,1)S(1)}, u32[]{:S(2)}, u32[]{:S(2)}) collective-permute-start(bf16[64,4096]{1,0:T(8,128)(2,1)S(1)} %collective-permute-done.15.refs_3_), channel_id=1, source_target_pairs={{0,2},{1,3},{2,0},{3,1},{4,6},{5,7},{6,4},{7,5},{8,10},{9,11},{10,... | collective-permute-start | bytes 1572872 | tf_op jit(solution)/shard_map/ppermute | solution.py:28
  111.5 14.8 %collective-permute-start.22 = (bf16[256,1024]{1,0:T(8,128)(2,1)S(1)}, bf16[256,1024]{1,0:T(8,128)(2,1)S(1)}, u32[]{:S(2)}, u32[]{:S(2)}) collective-permute-start(bf16[256,1024]{1,0:T(8,128)(2,1)S(1)} %collective-permute-done.3.refs_9_), channel_id=1, source_target_pairs={{0,4},{1,5},{2,6},{3,7},{4,0},{5,1},{6,2},{7,3},{8,12},{9,13},{10,... | collective-permute-start | bytes 1572872 | tf_op jit(solution)/shard_map/ppermute | solution.py:28
  113.3 13.7 %collective-permute-start.23 = (bf16[256,1024]{1,0:T(8,128)(2,1)S(1)}, bf16[256,1024]{1,0:T(8,128)(2,1)S(1)}, u32[]{:S(2)}, u32[]{:S(2)}) collective-permute-start(bf16[256,1024]{1,0:T(8,128)(2,1)S(1)} %collective-permute-done.18), channel_id=1, source_target_pairs={{0,16},{16,0},{1,17},{17,1},{2,18},{18,2},{3,19},{19,3},{4,20},{20... | collective-permute-start | bytes 1572872 | tf_op jit(solution)/shard_map/ppermute | solution.py:45
  117.6 10.4 %collective-permute-start.24 = (bf16[128,512]{1,0:T(8,128)(2,1)S(1)}, bf16[128,512]{1,0:T(8,128)(2,1)S(1)}, u32[]{:S(2)}, u32[]{:S(2)}) collective-permute-start(bf16[128,512]{1,0:T(8,128)(2,1)S(1)} %get-tuple-element.68.refs_0_.refs_1_), channel_id=1, source_target_pairs={{0,2},{1,3},{2,0},{3,1},{4,6},{5,7},{6,4},{7,5},{8,10},{9,11},{10,... | collective-permute-start | bytes 393224 | tf_op jit(solution)/shard_map/ppermute | solution.py:28
  119.0 9.3 %collective-permute-start.25 = (bf16[128,512]{1,0:T(8,128)(2,1)S(1)}, bf16[128,512]{1,0:T(8,128)(2,1)S(1)}, u32[]{:S(2)}, u32[]{:S(2)}) collective-permute-start(bf16[128,512]{1,0:T(8,128)(2,1)S(1)} %get-tuple-element.72.refs_9_), channel_id=1, source_target_pairs={{0,4},{1,5},{2,6},{3,7},{4,0},{5,1},{6,2},{7,3},{8,12},{9,13},{10,... | collective-permute-start | bytes 393224 | tf_op jit(solution)/shard_map/ppermute | solution.py:28
  128.4 15.4 %collective-permute-start.29 = (bf16[256,1024]{1,0:T(8,128)(2,1)S(1)}, bf16[256,1024]{1,0:T(8,128)(2,1)S(1)}, u32[]{:S(2)}, u32[]{:S(2)}) collective-permute-start(bf16[256,1024]{1,0:T(8,128)(2,1)S(1)} %collective-permute-done.22), channel_id=1, source_target_pairs={{0,16},{16,0},{1,17},{17,1},{2,18},{18,2},{3,19},{19,3},{4,20},{20... | collective-permute-start | bytes 1572872 | tf_op jit(solution)/shard_map/ppermute | solution.py:45
  132.7 11.1 %collective-permute-start.26 = (bf16[256,512]{1,0:T(8,128)(2,1)S(1)}, bf16[256,512]{1,0:T(8,128)(2,1)S(1)}, u32[]{:S(2)}, u32[]{:S(2)}) collective-permute-start(bf16[256,512]{1,0:T(8,128)(2,1)S(1)} %get-tuple-element.77), channel_id=1, source_target_pairs={{0,6},{1,7},{2,4},{3,5},{4,2},{5,3},{6,0},{7,1},{8,14},{9,15},{10,... | collective-permute-start | bytes 786440 | tf_op jit(solution)/shard_map/ppermute | solution.py:28
  135.3 8.5 %collective-permute-start.27 = (bf16[128,512]{1,0:T(8,128)(2,1)S(1)}, bf16[128,512]{1,0:T(8,128)(2,1)S(1)}, u32[]{:S(2)}, u32[]{:S(2)}) collective-permute-start(bf16[128,512]{1,0:T(8,128)(2,1)S(1)} %get-tuple-element.78.refs_4_.refs_5_), channel_id=1, source_target_pairs={{0,2},{1,3},{2,0},{3,1},{4,6},{5,7},{6,4},{7,5},{8,10},{9,11},{10,... | collective-permute-start | bytes 393224 | tf_op jit(solution)/shard_map/ppermute | solution.py:28
  135.9 7.8 %collective-permute-start.28 = (bf16[128,512]{1,0:T(8,128)(2,1)S(1)}, bf16[128,512]{1,0:T(8,128)(2,1)S(1)}, u32[]{:S(2)}, u32[]{:S(2)}) collective-permute-start(bf16[128,512]{1,0:T(8,128)(2,1)S(1)} %get-tuple-element.79), channel_id=1, source_target_pairs={{0,4},{1,5},{2,6},{3,7},{4,0},{5,1},{6,2},{7,3},{8,12},{9,13},{10,... | collective-permute-start | bytes 393224 | tf_op jit(solution)/shard_map/ppermute | solution.py:28
  136.2 7.6 %collective-permute-start.30 = (bf16[256,1024]{1,0:T(8,128)(2,1)S(1)}, bf16[256,1024]{1,0:T(8,128)(2,1)S(1)}, u32[]{:S(2)}, u32[]{:S(2)}) collective-permute-start(bf16[256,1024]{1,0:T(8,128)(2,1)S(1)} %collective-permute-done.23.refs_11_.refs_10_), channel_id=1, source_target_pairs={{0,1},{1,0},{2,3},{3,2},{4,5},{5,4},{6,7},{7,6},{8,9},{9,8},{10,11... | collective-permute-start | bytes 1572872 | tf_op jit(solution)/shard_map/ppermute | solution.py:28
  149.4 11.3 %collective-permute-start.34 = (bf16[128,1024]{1,0:T(8,128)(2,1)S(1)}, bf16[128,1024]{1,0:T(8,128)(2,1)S(1)}, u32[]{:S(2)}, u32[]{:S(2)}) collective-permute-start(bf16[128,1024]{1,0:T(8,128)(2,1)S(1)} %shard_map.89), channel_id=1, source_target_pairs={{0,2},{1,3},{2,0},{3,1},{4,6},{5,7},{6,4},{7,5},{8,10},{9,11},{10,... | collective-permute-start | bytes 786440 | tf_op jit(solution)/shard_map/ppermute | solution.py:28
  153.5 10.2 %collective-permute-start.33 = (bf16[128,1024]{1,0:T(8,128)(2,1)S(1)}, bf16[128,1024]{1,0:T(8,128)(2,1)S(1)}, u32[]{:S(2)}, u32[]{:S(2)}) collective-permute-start(bf16[128,1024]{1,0:T(8,128)(2,1)S(1)} %shard_map.88), channel_id=1, source_target_pairs={{0,2},{1,3},{2,0},{3,1},{4,6},{5,7},{6,4},{7,5},{8,10},{9,11},{10,... | collective-permute-start | bytes 786440 | tf_op jit(solution)/shard_map/ppermute | solution.py:28
  (27 other events, 596.9 us)
